TPU v7x, 32 devices: a whole 2x2x4 slice. The times are simulated.
32 devices in a mesh: wide: 8 (over y, x, core), narrow: 4 (over z).
Axes of the slice: x: 2, y: 2, z: 4, core: 2. Of those that a mesh axis runs over, the one named last changes fastest.
Arguments:
- tokens: bfloat16 [4, 2048, 2048], P('narrow', 'wide'), may hold values from -6 to 6
- lengths: int32 [4, 4], P('narrow'), may hold values from 1 to 2045, as said below
- gain_attn: bfloat16 [2048], P(('wide', 'narrow')), may hold values from 0.25 to 1.75
- w_qkv: bfloat16 [2048, 3072], P(('wide', 'narrow')), may hold values from -0.125 to 0.125
- w_out: bfloat16 [2048, 2048], P(('wide', 'narrow')), may hold values from -1 to 1
- gain_mlp: bfloat16 [2048], P(('wide', 'narrow')), may hold values from 0.25 to 1.75
- w_gateup: bfloat16 [2048, 16384], P(('wide', 'narrow')), may hold values from -0.125 to 0.125
- w_down: bfloat16 [8192, 2048], P(('wide', 'narrow')), may hold values from -0.0625 to 0.0625
- cotangent: bfloat16 [4, 2048, 2048], P('narrow', 'wide'), may hold values from -6 to 6
Outputs:
- layer_out: bfloat16 [4, 2048, 2048], P('narrow', 'wide')
- grad_tokens: bfloat16 [4, 2048, 2048], P('narrow', 'wide')
- grad_gain_attn: float32 [2048], P(('wide', 'narrow'))
- grad_qkv: float32 [2048, 3072], P(('wide', 'narrow'))
- grad_wout: float32 [2048, 2048], P(('wide', 'narrow'))
- grad_gain_mlp: float32 [2048], P(('wide', 'narrow'))
- grad_gateup: float32 [2048, 16384], P(('wide', 'narrow'))
- grad_down: float32 [8192, 2048], P(('wide', 'narrow'))
Inputs may be any that keep to these rules, and one draw needn't show every extreme that they name: `lengths`: each row sums to 2048. In each row one entry, at a place drawn per row, is larger than 1792; the others are at most 64.
All inputs are finite; a program needn't handle non-finite values.
Results may differ from a plain program's by a relative error of at most 0.015.
Values may be sent and summed in bfloat16 or wider, within the bound.
A program may use at most 512 MiB of HBM per device.

v0:
```python
import math

import jax
import jax.numpy as jnp
from jax import lax
from jax.sharding import PartitionSpec as P

FF = 8192
HEADS = 32
KV_HEADS = 8
HEAD_DIM = 64


EPS = 1e-05
NEGATIVE = -1e30


def places(lengths_row, total_rows):
    seq_ends = jnp.cumsum(lengths_row)
    starts = seq_ends - lengths_row
    row_index = jnp.arange(total_rows, dtype=jnp.int32)
    segments = jnp.sum((row_index[:, None] >= seq_ends[None, :]).astype(jnp.int32), -1)
    slot_index = jnp.arange(lengths_row.shape[0], dtype=jnp.int32)
    owned = segments[:, None] == slot_index[None, :]
    positions = row_index - jnp.sum(jnp.where(owned, starts[None, :], 0), -1)
    return (segments, positions)


def rotary(positions, half_width):
    channel = jnp.arange(half_width, dtype=jnp.float32)
    inverse_rate = jnp.power(500000.0, -channel / half_width)
    wavelength = 2.0 * math.pi / inverse_rate
    smooth = (8192.0 / wavelength - 1.0) / 3.0
    blended = (1.0 - smooth) * inverse_rate / 32.0 + smooth * inverse_rate
    frequency = jnp.where(
        wavelength < 2048.0,
        inverse_rate,
        jnp.where(wavelength > 8192.0, inverse_rate / 32.0, blended),
    )
    angles = positions[:, None] * frequency[None, :]
    return (jnp.cos(angles), jnp.sin(angles))


def rotate(vector, cosine_table, sine_table):
    half_width = vector.shape[-1] // 2
    front_half = vector[..., :half_width]
    back_half = vector[..., half_width:]
    cosine_part = cosine_table[:, None, :]
    sine_part = sine_table[:, None, :]
    return jnp.concatenate(
        [
            front_half * cosine_part - back_half * sine_part,
            back_half * cosine_part + front_half * sine_part,
        ],
        -1,
    )


def unrotate(vector, cosine_table, sine_table):
    half_width = vector.shape[-1] // 2
    front_half = vector[..., :half_width]
    back_half = vector[..., half_width:]
    cosine_part = cosine_table[:, None, :]
    sine_part = sine_table[:, None, :]
    return jnp.concatenate(
        [
            front_half * cosine_part + back_half * sine_part,
            back_half * cosine_part - front_half * sine_part,
        ],
        -1,
    )


def norm_back(grad_unit, unit_rows, row_scale):
    return row_scale * (grad_unit - unit_rows * jnp.mean(grad_unit * unit_rows, -1, keepdims=True))


def per_device(tokens, lengths, gain_attn, w_qkv, w_out, gain_mlp, w_gateup, w_down, cotangent):
    local_rows = tokens.shape[1]
    pack_rows = local_rows * lax.axis_size("wide")
    first_row = lax.axis_index("wide") * local_rows
    query_width = HEADS * HEAD_DIM
    key_width = KV_HEADS * HEAD_DIM
    groups = HEADS // KV_HEADS
    score_scale = 1.0 / math.sqrt(HEAD_DIM)
    block_len = min(512, pack_rows)
    blocks = pack_rows // block_len
    segments, positions = places(lengths[0], pack_rows)
    own_rows = first_row + jnp.arange(local_rows, dtype=jnp.int32)
    own_segments = lax.dynamic_slice_in_dim(segments, first_row, local_rows)
    own_positions = lax.dynamic_slice_in_dim(positions, first_row, local_rows)
    lowest = first_row - own_positions[0]
    highest = first_row + local_rows - 1
    cosine_table, sine_table = rotary(own_positions.astype(jnp.float32), HEAD_DIM // 2)
    inputs = tokens[0].astype(jnp.float32)
    gain_one, gain_two, qkv_whole, out_whole = (
        lax.all_gather(gain_attn, ("wide", "narrow"), axis=0, tiled=True),
        lax.all_gather(gain_mlp, ("wide", "narrow"), axis=0, tiled=True),
        lax.all_gather(w_qkv, ("wide", "narrow"), axis=0, tiled=True),
        lax.all_gather(w_out, ("wide", "narrow"), axis=0, tiled=True),
    )
    gain_one = gain_one.astype(jnp.float32)
    gain_two = gain_two.astype(jnp.float32)
    scale_one = lax.rsqrt(jnp.mean(inputs * inputs, -1, keepdims=True) + EPS)
    unit_one = inputs * scale_one
    normed_one = (unit_one * gain_one).astype(jnp.bfloat16)
    projected = jnp.dot(normed_one, qkv_whole, preferred_element_type=jnp.float32)
    queries = rotate(
        projected[:, :query_width].reshape(local_rows, HEADS, HEAD_DIM), cosine_table, sine_table
    ).astype(jnp.bfloat16)
    grouped = queries.reshape(local_rows, KV_HEADS, groups, HEAD_DIM)
    keys_own = rotate(
        projected[:, query_width : query_width + key_width].reshape(local_rows, KV_HEADS, HEAD_DIM),
        cosine_table,
        sine_table,
    )
    keys_own = keys_own.astype(jnp.bfloat16).reshape(local_rows, key_width)
    values_own = projected[:, query_width + key_width :].astype(jnp.bfloat16)
    keys_all, values_all = (
        lax.all_gather(keys_own, "wide", axis=0, tiled=True),
        lax.all_gather(values_own, "wide", axis=0, tiled=True),
    )

    def active(block_id):
        block_start = block_id * block_len
        return (block_start + block_len > lowest) & (block_start <= highest)

    def block_scores(block_id):
        block_start = block_id * block_len
        keys_block = lax.dynamic_slice_in_dim(keys_all, block_start, block_len).reshape(
            block_len, KV_HEADS, HEAD_DIM
        )
        values_block = lax.dynamic_slice_in_dim(values_all, block_start, block_len).reshape(
            block_len, KV_HEADS, HEAD_DIM
        )
        scores = (
            jnp.einsum("qkgd,pkd->kgqp", grouped, keys_block, preferred_element_type=jnp.float32)
            * score_scale
        )
        key_index = block_start + jnp.arange(block_len, dtype=jnp.int32)
        key_segments = lax.dynamic_slice_in_dim(segments, block_start, block_len)
        allowed = (own_segments[:, None] == key_segments[None, :]) & (
            key_index[None, :] <= own_rows[:, None]
        )
        return (
            jnp.where(allowed, scores, NEGATIVE),
            allowed,
            block_start,
            keys_block,
            values_block,
        )

    def measure(block_id, carried):

        def measure_take(state):
            running_top, running_sum = state
            scores, allowed, block_start, keys_block, values_block = block_scores(block_id)
            new_top = jnp.maximum(running_top, jnp.max(scores, -1))
            terms = jnp.where(allowed, jnp.exp(scores - new_top[..., None]), 0.0)
            return (new_top, running_sum * jnp.exp(running_top - new_top) + jnp.sum(terms, -1))

        return lax.cond(active(block_id), measure_take, lambda unchanged: unchanged, carried)

    stat_shape = (KV_HEADS, groups, local_rows)
    running_top, running_sum = lax.fori_loop(
        0,
        blocks,
        measure,
        (jnp.full(stat_shape, NEGATIVE, jnp.float32), jnp.zeros(stat_shape, jnp.float32)),
    )
    log_total = running_top + jnp.log(running_sum)

    def weigh(block_id, carried):

        def weigh_take(accumulated):
            scores, allowed, block_start, keys_block, values_block = block_scores(block_id)
            rounded_prob = jnp.where(allowed, jnp.exp(scores - log_total[..., None]), 0.0).astype(
                jnp.bfloat16
            )
            return accumulated + jnp.einsum(
                "kgqp,pkd->qkgd", rounded_prob, values_block, preferred_element_type=jnp.float32
            )

        return lax.cond(active(block_id), weigh_take, lambda unchanged: unchanged, carried)

    attended = lax.fori_loop(
        0, blocks, weigh, jnp.zeros((local_rows, KV_HEADS, groups, HEAD_DIM), jnp.float32)
    )
    attended_low = attended.reshape(local_rows, query_width).astype(jnp.bfloat16)
    middle = inputs + jnp.dot(attended_low, out_whole, preferred_element_type=jnp.float32)
    scale_two = lax.rsqrt(jnp.mean(middle * middle, -1, keepdims=True) + EPS)
    unit_two = middle * scale_two
    normed_two = (unit_two * gain_two).astype(jnp.bfloat16)
    gateup_first = lax.all_gather(w_gateup, ("wide", "narrow"), axis=0, tiled=True)
    gate_up = jnp.dot(normed_two, gateup_first, preferred_element_type=jnp.float32)
    gate_part = gate_up[:, :FF]
    up_part = gate_up[:, FF:]
    sigmoid_gate = jax.nn.sigmoid(gate_part)
    hidden = (gate_part * sigmoid_gate * up_part).astype(jnp.bfloat16)
    down_first = lax.all_gather(w_down, ("wide", "narrow"), axis=0, tiled=True)
    down_result = jnp.dot(hidden, down_first, preferred_element_type=jnp.float32)
    layer_out = (middle + down_result).astype(jnp.bfloat16)[None]
    incoming = cotangent[0]
    columns = hidden
    grad_down = lax.psum_scatter(
        jnp.einsum("tf,td->fd", columns, incoming, preferred_element_type=jnp.float32),
        ("wide", "narrow"),
        scatter_dimension=0,
        tiled=True,
    )
    grad_hidden = jnp.einsum(
        "td,fd->tf",
        incoming,
        lax.all_gather(w_down, ("wide", "narrow"), axis=0, tiled=True),
        preferred_element_type=jnp.float32,
    )
    grad_gate = grad_hidden * up_part * sigmoid_gate * (1.0 + gate_part * (1.0 - sigmoid_gate))
    grad_up = grad_hidden * gate_part * sigmoid_gate
    grad_gate_up = jnp.concatenate([grad_gate, grad_up], -1).astype(jnp.bfloat16)
    columns = normed_two
    grad_gateup = lax.psum_scatter(
        jnp.einsum("td,tf->df", columns, grad_gate_up, preferred_element_type=jnp.float32),
        ("wide", "narrow"),
        scatter_dimension=0,
        tiled=True,
    )
    grad_normed_two = jnp.einsum(
        "tf,df->td",
        grad_gate_up,
        lax.all_gather(w_gateup, ("wide", "narrow"), axis=0, tiled=True),
        preferred_element_type=jnp.float32,
    )
    part_gain_two = jnp.sum(grad_normed_two * unit_two, 0)
    grad_middle = incoming.astype(jnp.float32) + norm_back(
        grad_normed_two * gain_two, unit_two, scale_two
    )
    grad_branch = grad_middle.astype(jnp.bfloat16)
    part_wout = jnp.einsum(
        "tq,td->qd", attended_low, grad_branch, preferred_element_type=jnp.float32
    )
    qkv_back, out_back = (
        lax.all_gather(w_qkv, ("wide", "narrow"), axis=0, tiled=True),
        lax.all_gather(w_out, ("wide", "narrow"), axis=0, tiled=True),
    )
    grad_attended = jnp.einsum(
        "td,qd->tq", grad_branch, out_back, preferred_element_type=jnp.float32
    ).astype(jnp.bfloat16)
    grad_grouped = grad_attended.reshape(local_rows, KV_HEADS, groups, HEAD_DIM)
    row_delta = jnp.sum(grad_grouped.astype(jnp.float32) * attended, -1).transpose(1, 2, 0)

    def back_step(block_id, carried):

        def back_take(state):
            grad_queries, grad_keyvalue = state
            scores, allowed, block_start, keys_block, values_block = block_scores(block_id)
            exact_prob = jnp.where(allowed, jnp.exp(scores - log_total[..., None]), 0.0)
            grad_prob = jnp.einsum(
                "qkgd,pkd->kgqp", grad_grouped, values_block, preferred_element_type=jnp.float32
            )
            grad_scores = (exact_prob * (grad_prob - row_delta[..., None])).astype(jnp.bfloat16)
            grad_queries = (
                grad_queries
                + jnp.einsum(
                    "kgqp,pkd->qkgd", grad_scores, keys_block, preferred_element_type=jnp.float32
                )
                * score_scale
            )
            grad_keys = (
                jnp.einsum(
                    "kgqp,qkgd->pkd", grad_scores, grouped, preferred_element_type=jnp.float32
                )
                * score_scale
            )
            grad_values = jnp.einsum(
                "kgqp,qkgd->pkd",
                exact_prob.astype(jnp.bfloat16),
                grad_grouped,
                preferred_element_type=jnp.float32,
            )
            update = jnp.concatenate(
                [
                    grad_keys.reshape(block_len, key_width),
                    grad_values.reshape(block_len, key_width),
                ],
                -1,
            )
            current = lax.dynamic_slice_in_dim(grad_keyvalue, block_start, block_len)
            return (
                grad_queries,
                lax.dynamic_update_slice_in_dim(grad_keyvalue, current + update, block_start, 0),
            )

        return lax.cond(active(block_id), back_take, lambda unchanged: unchanged, carried)

    start_state = (
        jnp.zeros((local_rows, KV_HEADS, groups, HEAD_DIM), jnp.float32),
        jnp.zeros((pack_rows, 2 * key_width), jnp.float32),
    )
    grad_queries, grad_keyvalue = lax.fori_loop(0, blocks, back_step, start_state)
    keyvalue_own = lax.psum_scatter(
        grad_keyvalue.astype(jnp.bfloat16), "wide", scatter_dimension=0, tiled=True
    ).astype(jnp.float32)
    grad_query_rows = unrotate(
        grad_queries.reshape(local_rows, HEADS, HEAD_DIM), cosine_table, sine_table
    ).reshape(local_rows, query_width)
    grad_key_rows = unrotate(
        keyvalue_own[:, :key_width].reshape(local_rows, KV_HEADS, HEAD_DIM),
        cosine_table,
        sine_table,
    ).reshape(local_rows, key_width)
    grad_projected = jnp.concatenate(
        [grad_query_rows, grad_key_rows, keyvalue_own[:, key_width:]], -1
    ).astype(jnp.bfloat16)
    part_qkv = jnp.einsum(
        "td,tc->dc", normed_one, grad_projected, preferred_element_type=jnp.float32
    )
    grad_normed_one = jnp.einsum(
        "tc,dc->td", grad_projected, qkv_back, preferred_element_type=jnp.float32
    )
    part_gain_one = jnp.sum(grad_normed_one * unit_one, 0)
    grad_inputs = grad_middle + norm_back(grad_normed_one * gain_one, unit_one, scale_one)
    grad_tokens = grad_inputs.astype(jnp.bfloat16)[None]
    grad_gain_attn, grad_gain_mlp, grad_qkv, grad_wout = (
        lax.psum_scatter(part_gain_one, ("wide", "narrow"), scatter_dimension=0, tiled=True),
        lax.psum_scatter(part_gain_two, ("wide", "narrow"), scatter_dimension=0, tiled=True),
        lax.psum_scatter(part_qkv, ("wide", "narrow"), scatter_dimension=0, tiled=True),
        lax.psum_scatter(part_wout, ("wide", "narrow"), scatter_dimension=0, tiled=True),
    )
    return (
        layer_out,
        grad_tokens,
        grad_gain_attn,
        grad_qkv,
        grad_wout,
        grad_gain_mlp,
        grad_gateup,
        grad_down,
    )


def solution(mesh):
    placed = (
        P("narrow", "wide", None),
        P("narrow", None),
        P(("wide", "narrow")),
        P(("wide", "narrow"), None),
        P(("wide", "narrow"), None),
        P(("wide", "narrow")),
        P(("wide", "narrow"), None),
        P(("wide", "narrow"), None),
        P("narrow", "wide", None),
    )
    return jax.shard_map(
        per_device,
        mesh=mesh,
        in_specs=placed,
        out_specs=(
            P("narrow", "wide", None),
            P("narrow", "wide", None),
            P(("wide", "narrow")),
            P(("wide", "narrow"), None),
            P(("wide", "narrow"), None),
            P(("wide", "narrow")),
            P(("wide", "narrow"), None),
            P(("wide", "narrow"), None),
        ),
        check_vma=False,
    )
```

profile of v0, /device:TPU:0, one launch (start us, length us, event | category | flops | bytes accessed | tf_op | source)
XLA Modules:
  0.0 5956.1 jit_solution(14917739612043537340)
XLA Ops:
  9.7 42.8 all-reduce.6
  54.0 56.6 all-gather.7.cloned.1.call-done
  110.6 6.8 fusion.56
  126.0 3.1 slice.71
  131.5 14.6 all-gather.9.cloned.1.call-done
  146.1 2.9 copy.58
  149.0 27.8 all-gather.11.cloned.1.call-done
  176.8 8.5 while.49
  176.8 8.3 conditional.9
  178.3 2.5 fusion.6
  180.8 4.3 select_reduce_fusion
  187.0 11.4 while.50
  187.0 11.0 conditional.10
  187.0 2.1 constant_dynamic-slice_fusion.1
  189.4 8.6 bitcast_add_fusion
  198.4 3.5 convert_element_type.102
  201.9 55.1 all-gather.13.cloned.1.call-done
  257.0 7.7 multiply_reduce_fusion.3
  264.7 350.1 %all-gather.15.cloned.1.call-done = bf16[2048,16384]{1,0:T(8,128)(2,1)} async-done(((bf16[64,16384]{1,0:T(8,128)(2,1)}), bf16[2048,16384]{1,0:T(8,128)(2,1)}) %all-gather.15.cloned.1.call-update) | async-done | bytes 67108880 | tf_op jit(solution)/shard_map/all_gather | solution.py:194
  614.8 31.5 fusion.63
  646.3 164.3 %all-gather.17.cloned.1.call-done = bf16[8192,2048]{1,0:T(8,128)(2,1)} async-done(((bf16[256,2048]{1,0:T(8,128)(2,1)}), bf16[8192,2048]{1,0:T(8,128)(2,1)}) %all-gather.17.cloned.1.call-update) | async-done | bytes 33554448 | tf_op jit(solution)/shard_map/all_gather | solution.py:200
  810.6 23.9 multiply_convert_fusion.1
  834.5 29.7 multiply_reduce_fusion
  864.1 2.4 multiply_add_fusion.1
  867.9 6.9 convolution_convert_fusion
  874.8 2.3 copy.59
  878.9 4.3 broadcast_in_dim.106
  883.2 43.1 while.51
  883.4 42.7 conditional.11
  884.7 8.1 fusion.66
  893.1 8.8 fusion.16
  905.3 11.1 fusion.21
  916.5 6.1 fusion.25
  922.6 3.5 fusion.24
  926.3 6.0 convert_element_type.112
  933.5 9.7 fusion.52
  944.4 165.3 %reduce-scatter.9.cloned.1.call-done = bf16[256,1024]{0,1:T(8,128)(2,1)} async-done(((bf16[2048,1024]{0,1:T(8,128)(2,1)}), bf16[256,1024]{0,1:T(8,128)(2,1)}) %reduce-scatter.9.cloned.1.call-update) | async-done | bytes 524304 | tf_op jit(solution)/shard_map/reduce_scatter | solution.py:300
  1111.0 11.3 fusion.50
  1123.6 25.7 fusion.46
  1150.9 47.9 fusion.29
  1198.9 17.3 fusion.36
  1216.2 10.0 fusion.43
  1226.2 43.1 all-reduce.5
  1270.6 3.2 fusion.45
  1273.7 204.2 %reduce-scatter.13.cloned.1.call-done = f32[64,2048]{1,0:T(8,128)} async-done(((f32[2048,2048]{1,0:T(8,128)}), f32[64,2048]{1,0:T(8,128)}) %reduce-scatter.13.cloned.1.call-update) | async-done | bytes 524304 | tf_op jit(solution)/shard_map/reduce_scatter | solution.py:327
  1477.9 251.6 %reduce-scatter.11.cloned.1.call-done = f32[64,3072]{1,0:T(8,128)} async-done(((f32[2048,3072]{1,0:T(8,128)}), f32[64,3072]{1,0:T(8,128)}) %reduce-scatter.11.cloned.1.call-update) | async-done | bytes 786448 | tf_op jit(solution)/shard_map/reduce_scatter | solution.py:326
  1729.5 1413.0 %reduce-scatter.15.cloned.1.call-done = f32[256,2048]{1,0:T(8,128)} async-done(((f32[8192,2048]{1,0:T(8,128)}), f32[256,2048]{1,0:T(8,128)}) %reduce-scatter.15.cloned.1.call-update) | async-done | bytes 2097168 | tf_op jit(solution)/shard_map/reduce_scatter | solution.py:205
  3142.5 2806.8 %reduce-scatter.17.cloned.1.call-done = f32[64,16384]{1,0:T(8,128)} async-done(((f32[2048,16384]{1,0:T(8,128)}), f32[64,16384]{1,0:T(8,128)}) %reduce-scatter.17.cloned.1.call-update) | async-done | bytes 4194320
  (169 shorter events, 33.2 us)
Async XLA Ops:
  7.2 103.4 %all-gather.7.cloned.1.call-start = ((), (), s32[]{:S(2)}) async-start(), calls=%async_computation.5 | async-start | bytes 12976128 | tf_op jit(solution)/shard_map/all_gather | solution.py:99
  7.9 138.2 %all-gather.9.cloned.1.call-start = ((), (), s32[]{:S(2)}) async-start(), calls=%async_computation.6 | async-start | bytes 2359296 | tf_op jit(solution)/shard_map/all_gather | solution.py:121
  52.4 64.9 %copy-start.25 = (f32[2048]{0:T(1024)}, f32[2048]{0:T(1024)S(1)}, u32[]{:S(2)}) copy-start(f32[2048]{0:T(1024)S(1)} %convert_element_type.98) | copy-start | bytes 24580
  54.0 63.4 %copy-start.29 = (f32[256]{0:T(256)}, f32[256]{0:T(256)S(1)}, u32[]{:S(2)}) copy-start(f32[256]{0:T(256)S(1)} %add_rsqrt_fusion.1) | copy-start | bytes 3076
  54.0 65.9 %copy-start.32 = (s32[1,4]{1,0:T(1,128)S(1)}, s32[1,4]{1,0:T(1,128)}, u32[]{:S(2)}) copy-start(s32[1,4]{1,0:T(1,128)} %param.22) | copy-start | bytes 52
  117.4 1.7 copy-start.14
  119.8 57.0 all-gather.11.cloned.1.call-start
  120.6 10.5 copy-start.19
  120.6 10.5 copy-start.21
  122.7 134.3 %all-gather.13.cloned.1.call-start = ((), (), s32[]{:S(2)}) async-start(), calls=%async_computation.8 | async-start | bytes 8650752 | tf_op jit(solution)/shard_map/all_gather | solution.py:100
  123.3 491.5 %all-gather.15.cloned.1.call-start = ((), (), s32[]{:S(2)}) async-start(), calls=%async_computation.9 | async-start | bytes 69206016 | tf_op jit(solution)/shard_map/all_gather | solution.py:194
  123.9 686.7 %all-gather.17.cloned.1.call-start = ((), (), s32[]{:S(2)}) async-start(), calls=%async_computation.10 | async-start | bytes 34603008 | tf_op jit(solution)/shard_map/all_gather | solution.py:200
  124.5 985.3 %reduce-scatter.9.cloned.1.call-start = ((), (), s32[]{:S(2)}) async-start(), calls=%async_computation.11 | async-start | bytes 4718592 | tf_op jit(solution)/shard_map/reduce_scatter | solution.py:300
  126.0 738.2 %copy-start.17 = (f32[2048]{0:T(1024)}, f32[2048]{0:T(1024)S(1)}, u32[]{:S(2)}) copy-start(f32[2048]{0:T(1024)S(1)} %convert_element_type.104) | copy-start | bytes 24580
  198.4 66.3 %copy-start.2 = (bf16[2048,512]{0,1:T(8,128)(2,1)}, bf16[2048,512]{0,1:T(8,128)(2,1)S(1)}, u32[]{:S(2)}) copy-start(bf16[2048,512]{0,1:T(8,128)(2,1)S(1)} %get-tuple-element.1386) | copy-start | bytes 6291460
  198.4 66.3 %copy-start.27 = (f32[8,4,256]{2,1,0:T(4,128)}, f32[8,4,256]{2,1,0:T(4,128)S(1)}, u32[]{:S(2)}) copy-start(f32[8,4,256]{2,1,0:T(4,128)S(1)} %get-tuple-element.1410) | copy-start | bytes 98308
  264.7 599.5 %copy-start.23 = (f32[256]{0:T(256)}, f32[256]{0:T(256)S(1)}, u32[]{:S(2)}) copy-start(f32[256]{0:T(256)S(1)} %add_rsqrt_fusion) | copy-start | bytes 3076
  646.3 188.2 %copy-start.3 = (f32[256,2048]{1,0:T(8,128)S(1)}, f32[256,2048]{1,0:T(8,128)}, u32[]{:S(2)}) copy-start(f32[256,2048]{1,0:T(8,128)} %get-tuple-element.1006) | copy-start | bytes 6291460
  866.6 1.3 copy-start.5
  867.9 9.1 copy-start.7
  878.9 4.3 copy-start.28
  884.7 8.5 copy-start.11
  902.0 3.3 copy-start
  916.5 6.1 copy-start.1
  932.3 1.2 copy-start.9
  932.3 545.6 %reduce-scatter.13.cloned.1.call-start = ((), (), s32[]{:S(2)}) async-start(), calls=%async_computation.13 | async-start | bytes 17301504 | tf_op jit(solution)/shard_map/reduce_scatter | solution.py:327
  943.2 0.8 copy-start.20
  943.2 0.8 copy-start.22
  943.2 786.3 %reduce-scatter.11.cloned.1.call-start = ((), (), s32[]{:S(2)}) async-start(), calls=%async_computation.12 | async-start | bytes 25952256 | tf_op jit(solution)/shard_map/reduce_scatter | solution.py:326
  944.0 167.0 %copy-start.8 = (bf16[1,256,2048]{2,1,0:T(8,128)(2,1)S(1)}, bf16[1,256,2048]{2,1,0:T(8,128)(2,1)}, u32[]{:S(2)}) copy-start(bf16[1,256,2048]{2,1,0:T(8,128)(2,1)} %param.21) | copy-start | bytes 3145732
  944.0 167.0 %copy-start.26 = (f32[2048]{0:T(1024)S(1)}, f32[2048]{0:T(1024)}, u32[]{:S(2)}) copy-start(f32[2048]{0:T(1024)} %copy-done.25) | copy-start | bytes 24580
  944.0 167.0 %copy-start.30 = (f32[256]{0:T(256)S(1)}, f32[256]{0:T(256)}, u32[]{:S(2)}) copy-start(f32[256]{0:T(256)} %copy-done.29) | copy-start | bytes 3076
  944.4 177.9 %copy-start.12 = (bf16[256,32,64]{0,2,1:T(8,128)(2,1)}, bf16[256,32,64]{0,2,1:T(8,128)(2,1)S(1)}, u32[]{:S(2)}) copy-start(bf16[256,32,64]{0,2,1:T(8,128)(2,1)S(1)} %pad_maximum_fusion.5) | copy-start | bytes 3145732
  1110.8 11.5 copy-start.15
  1122.4 1.2 copy-start.10
  1122.4 2020.1 %reduce-scatter.15.cloned.1.call-start = ((), (), s32[]{:S(2)}) async-start(), calls=%async_computation.14 | async-start | bytes 69206016 | tf_op jit(solution)/shard_map/reduce_scatter | solution.py:205
  1149.3 1.6 copy-start.4
  1149.3 1.6 copy-start.18
  1149.3 1.6 copy-start.24
  1149.3 4800.0 %reduce-scatter.17.cloned.1.call-start = ((), (), s32[]{:S(2)}) async-start(), calls=%async_computation.15 | async-start | bytes 138412032
  1198.9 17.4 copy-start.13
  1198.9 17.4 copy-start.16
  1216.2 10.0 copy-start.31
  1216.2 54.3 copy-start.6
Sparse Core Ops, SparseCore 0:
  10.9 99.6 all-gather.6
  119.9 26.1 all-gather.8
  148.6 28.1 all-gather.10
  179.6 77.3 all-gather.12
  259.8 354.9 all-gather.14
  617.6 192.9 all-gather.16
  932.4 177.3 reduce-scatter.8
  1112.7 365.1 reduce-scatter.12
  1486.1 243.3 reduce-scatter.10
  1732.3 1410.2 reduce-scatter.14
  3145.5 2803.7 reduce-scatter.16
where the time goes:
time: 5960 us
  waiting for transfers between devices  5510 us (92%)
  matrix products  275 us (5%)
  blocking collectives  85.9 us (1%)
    unnamed x12, waiting for transfers between devices  2810 us
    reduce_scatter x1, waiting for transfers between devices, per_device(): lax.psum_scatter(jnp.einsum('tf,td->fd', columns, incoming, preferred_ele...  1410 us
    all_gather x1, waiting for transfers between devices, per_device(): lax.all_gather(w_gateup, ('wide', 'narrow'), axis=0, tiled=True)  350 us
    reduce_scatter x1, waiting for transfers between devices, per_device(): lax.psum_scatter(part_qkv, ('wide', 'narrow'), scatter_dimension=0, tiled...  252 us
    reduce_scatter x1, waiting for transfers between devices, per_device(): lax.psum_scatter(part_wout, ('wide', 'narrow'), scatter_dimension=0, tile...  204 us
    reduce_scatter x1, waiting for transfers between devices, per_device(): lax.psum_scatter(grad_keyvalue.astype(jnp.bfloat16), 'wide', scatter_dime...  165 us
    all_gather x1, waiting for transfers between devices, per_device(): down_first = lax.all_gather(w_down, ('wide', 'narrow'), axis=0, tiled=True)  164 us
  transfers between devices with their start and end apart: 11, of which 11 were waited for; matrix products, arithmetic and copies ran while one was open for 3% of the time, Pallas kernels for 0%

commit v1 on v0

v1 whole, which is shorter than its diff:
```python
import functools
import math

import jax
import jax.numpy as jnp
from jax import lax
from jax.experimental import pallas as pl
from jax.experimental.pallas import tpu as pltpu
from jax.sharding import PartitionSpec as P

FF = 8192
HEADS = 32
KV_HEADS = 8
HEAD_DIM = 64
HALF = HEAD_DIM // 2
EPS = 1e-05
NEGATIVE = -1e30
SCORE_SCALE = 1.0 / math.sqrt(HEAD_DIM)
BOTH = ("wide", "narrow")
F32 = jnp.float32
BF16 = jnp.bfloat16
NN = (((1,), (0,)), ((), ()))
NT = (((1,), (1,)), ((), ()))
TN = (((0,), (0,)), ((), ()))


def dot(left, right, dims, kind=F32):
    return lax.dot_general(left, right, dims, preferred_element_type=F32).astype(kind)


def places(lengths_row, total_rows):
    seq_ends = jnp.cumsum(lengths_row)
    starts = seq_ends - lengths_row
    row_index = jnp.arange(total_rows, dtype=jnp.int32)
    segments = jnp.sum((row_index[:, None] >= seq_ends[None, :]).astype(jnp.int32), -1)
    slot_index = jnp.arange(lengths_row.shape[0], dtype=jnp.int32)
    owned = segments[:, None] == slot_index[None, :]
    first = jnp.sum(jnp.where(owned, starts[None, :], 0), -1)
    return first, row_index - first


def rotary(positions, half_width):
    channel = jnp.arange(half_width, dtype=jnp.float32)
    inverse_rate = jnp.power(500000.0, -channel / half_width)
    wavelength = 2.0 * math.pi / inverse_rate
    smooth = (8192.0 / wavelength - 1.0) / 3.0
    blended = (1.0 - smooth) * inverse_rate / 32.0 + smooth * inverse_rate
    frequency = jnp.where(
        wavelength < 2048.0,
        inverse_rate,
        jnp.where(wavelength > 8192.0, inverse_rate / 32.0, blended),
    )
    angles = frequency[:, None] * positions[None, :]
    return jnp.cos(angles), jnp.sin(angles)


def norm_back(grad_unit, unit_rows, row_scale):
    return row_scale * (grad_unit - unit_rows * jnp.mean(grad_unit * unit_rows, -1, keepdims=True))


def attend_kernel(groups, start_ref, x_ref, low_ref, full_ref, log_ref, keys, top, total, acc):
    i = pl.program_id(0)
    blocks, _, rows = x_ref.shape
    width = groups * HEAD_DIM

    @pl.when(i == 0)
    def _():
        for j in range(blocks):
            keys[j] = x_ref[j, width : width + HEAD_DIM, :].T

    top[...] = jnp.full_like(top, NEGATIVE)
    total[...] = jnp.zeros_like(total)
    acc[...] = jnp.zeros_like(acc)
    start = start_ref[0]
    query_row = i * rows + lax.broadcasted_iota(jnp.int32, (rows, rows), 1)
    key_row = lax.broadcasted_iota(jnp.int32, (rows, rows), 0)

    def step(j, carry):
        key_index = key_row + j * rows
        allowed = (key_index <= query_row) & (key_index >= start)
        key_block = keys[j]
        value_block = x_ref[j, width + HEAD_DIM :, :]
        for h in range(groups):
            own = pl.ds(h * HEAD_DIM, HEAD_DIM)
            scores = dot(key_block, x_ref[i, own, :], NN)
            scores = jnp.where(allowed, scores, NEGATIVE)
            old = top[h : h + 1, :]
            new = jnp.maximum(old, jnp.max(scores, 0, keepdims=True))
            shrink = jnp.exp(old - new)
            prob = jnp.exp(scores - new)
            top[h : h + 1, :] = new
            total[h : h + 1, :] = total[h : h + 1, :] * shrink + jnp.sum(prob, 0, keepdims=True)
            acc[own, :] = acc[own, :] * shrink + dot(value_block, prob.astype(BF16), NN)
        return carry

    lax.fori_loop(0, i + 1, step, 0)
    log_ref[0] = top[...] + jnp.log(total[...])
    for h in range(groups):
        own = pl.ds(h * HEAD_DIM, HEAD_DIM)
        result = acc[own, :] / total[h : h + 1, :]
        full_ref[0, own, :] = result
        low_ref[0, own, :] = result.astype(BF16)


def attend(x, start, groups):
    blocks, _, rows = x.shape
    width = groups * HEAD_DIM
    whole = lambda i: (0, 0, 0)
    mine = lambda i: (i, 0, 0)
    return pl.pallas_call(
        functools.partial(attend_kernel, groups),
        grid=(blocks,),
        out_shape=(
            jax.ShapeDtypeStruct((blocks, width, rows), BF16),
            jax.ShapeDtypeStruct((blocks, width, rows), F32),
            jax.ShapeDtypeStruct((blocks, groups, rows), F32),
        ),
        in_specs=[pl.BlockSpec((1, 1, rows), mine), pl.BlockSpec(x.shape, whole)],
        out_specs=(
            pl.BlockSpec((1, width, rows), mine),
            pl.BlockSpec((1, width, rows), mine),
            pl.BlockSpec((1, groups, rows), mine),
        ),
        scratch_shapes=[
            pltpu.VMEM((blocks, rows, HEAD_DIM), BF16),
            pltpu.VMEM((groups, rows), F32),
            pltpu.VMEM((groups, rows), F32),
            pltpu.VMEM((width, rows), F32),
        ],
        compiler_params=pltpu.CompilerParams(vmem_limit_bytes=32 << 20),
        cost_estimate=pl.CostEstimate(
            flops=16 * width * (blocks * rows) ** 2,
            bytes_accessed=2 * x.size * 2,
            transcendentals=groups * (blocks * rows) ** 2 // 2,
        ),
    )(start, x)


def attend_back_kernel(
    groups, start_ref, x_ref, grad_ref, full_ref, log_ref, cos_ref, sin_ref, out_ref,
    keys, values, acc, acc_keys, acc_values,
):
    i = pl.program_id(0)
    blocks, _, rows = x_ref.shape
    width = groups * HEAD_DIM

    @pl.when(i == 0)
    def _():
        for j in range(blocks):
            keys[j] = x_ref[j, width : width + HEAD_DIM, :].T
            values[j] = x_ref[j, width + HEAD_DIM :, :].T
        acc_keys[...] = jnp.zeros_like(acc_keys)
        acc_values[...] = jnp.zeros_like(acc_values)

    acc[...] = jnp.zeros_like(acc)
    start = start_ref[0]
    query_row = i * rows + lax.broadcasted_iota(jnp.int32, (rows, rows), 1)
    key_row = lax.broadcasted_iota(jnp.int32, (rows, rows), 0)
    deltas = [
        jnp.sum(
            grad_ref[0, pl.ds(h * HEAD_DIM, HEAD_DIM), :].astype(F32)
            * full_ref[0, pl.ds(h * HEAD_DIM, HEAD_DIM), :],
            0,
            keepdims=True,
        )
        for h in range(groups)
    ]

    def step(j, carry):
        key_index = key_row + j * rows
        allowed = (key_index <= query_row) & (key_index >= start)
        key_block = keys[j]
        value_block = values[j]
        key_columns = x_ref[j, width : width + HEAD_DIM, :]
        grad_keys = acc_keys[j]
        grad_values = acc_values[j]
        for h in range(groups):
            own = pl.ds(h * HEAD_DIM, HEAD_DIM)
            query = x_ref[i, own, :]
            grad = grad_ref[0, own, :]
            scores = dot(key_block, query, NN)
            scores = jnp.where(allowed, scores, NEGATIVE)
            prob = jnp.exp(scores - log_ref[0, h : h + 1, :])
            grad_prob = dot(value_block, grad, NN)
            grad_scores = (prob * (grad_prob - deltas[h])).astype(BF16)
            acc[own, :] += dot(key_columns, grad_scores, NN)
            grad_keys = grad_keys + dot(query, grad_scores, NT)
            grad_values = grad_values + dot(grad, prob.astype(BF16), NT)
        acc_keys[j] = grad_keys
        acc_values[j] = grad_values
        return carry

    lax.fori_loop(0, i + 1, step, 0)

    def turn_back(block, cos, sin):
        front, back = block[:HALF, :], block[HALF:, :]
        return (front * cos + back * sin).astype(BF16), (back * cos - front * sin).astype(BF16)

    for h in range(groups):
        at = h * HEAD_DIM
        front, back = turn_back(acc[pl.ds(at, HEAD_DIM), :] * SCORE_SCALE, cos_ref[i], sin_ref[i])
        out_ref[i, pl.ds(at, HALF), :] = front
        out_ref[i, pl.ds(at + HALF, HALF), :] = back

    @pl.when(i == blocks - 1)
    def _():
        for j in range(blocks):
            front, back = turn_back(acc_keys[j], cos_ref[j], sin_ref[j])
            out_ref[j, pl.ds(width, HALF), :] = front
            out_ref[j, pl.ds(width + HALF, HALF), :] = back
            out_ref[j, pl.ds(width + HEAD_DIM, HEAD_DIM), :] = acc_values[j].astype(BF16)


def attend_back(x, grad, full, log_total, start, cos, sin, groups):
    blocks, _, rows = x.shape
    width = groups * HEAD_DIM
    whole = lambda i: (0, 0, 0)
    mine = lambda i: (i, 0, 0)
    return pl.pallas_call(
        functools.partial(attend_back_kernel, groups),
        grid=(blocks,),
        out_shape=jax.ShapeDtypeStruct(x.shape, BF16),
        in_specs=[
            pl.BlockSpec((1, 1, rows), mine),
            pl.BlockSpec(x.shape, whole),
            pl.BlockSpec((1, width, rows), mine),
            pl.BlockSpec((1, width, rows), mine),
            pl.BlockSpec((1, groups, rows), mine),
            pl.BlockSpec(cos.shape, whole),
            pl.BlockSpec(sin.shape, whole),
        ],
        out_specs=pl.BlockSpec(x.shape, whole),
        scratch_shapes=[
            pltpu.VMEM((blocks, rows, HEAD_DIM), BF16),
            pltpu.VMEM((blocks, rows, HEAD_DIM), BF16),
            pltpu.VMEM((width, rows), F32),
            pltpu.VMEM((blocks, HEAD_DIM, rows), F32),
            pltpu.VMEM((blocks, HEAD_DIM, rows), F32),
        ],
        compiler_params=pltpu.CompilerParams(vmem_limit_bytes=40 << 20),
        cost_estimate=pl.CostEstimate(
            flops=40 * width * (blocks * rows) ** 2,
            bytes_accessed=4 * x.size * 2,
            transcendentals=groups * (blocks * rows) ** 2 // 2,
        ),
    )(start, x, grad, full, log_total, cos, sin)


def middle_kernel(step_rows, x_ref, c_ref, gate_ref, up_ref, down_ref, hidden_ref, dgate_ref, dup_ref):
    def step(t, carry):
        rows = pl.ds(pl.multiple_of(t * step_rows, step_rows), step_rows)
        x = x_ref[rows, :]
        gate = dot(x, gate_ref[...], NN)
        up = dot(x, up_ref[...], NN)
        grad = dot(c_ref[rows, :], down_ref[...], NT)
        sig = 1.0 / (1.0 + jnp.exp(-gate))
        silu = gate * sig
        hidden_ref[rows, :] = (silu * up).astype(BF16)
        dgate_ref[rows, :] = (grad * up * (sig + silu * (1.0 - sig))).astype(BF16)
        dup_ref[rows, :] = (grad * silu).astype(BF16)
        return carry

    lax.fori_loop(0, x_ref.shape[0] // step_rows, step, 0)


def middle_part(x, c, gate_up, down):
    tokens, width = x.shape
    own = down.shape[0]
    tile = min(256, own)
    tiles = own // tile
    shape = jax.ShapeDtypeStruct((tokens, own), BF16)
    out = pl.BlockSpec((tokens, tile), lambda f: (0, f))
    return pl.pallas_call(
        functools.partial(middle_kernel, 256),
        grid=(tiles,),
        out_shape=(shape, shape, shape),
        in_specs=[
            pl.BlockSpec((tokens, width), lambda f: (0, 0)),
            pl.BlockSpec((tokens, width), lambda f: (0, 0)),
            pl.BlockSpec((width, tile), lambda f: (0, f)),
            pl.BlockSpec((width, tile), lambda f: (0, f + tiles)),
            pl.BlockSpec((tile, width), lambda f: (f, 0)),
        ],
        out_specs=(out, out, out),
        compiler_params=pltpu.CompilerParams(vmem_limit_bytes=56 << 20),
        cost_estimate=pl.CostEstimate(
            flops=6 * tokens * width * own,
            bytes_accessed=2 * (2 * tokens * width + 3 * width * own + 3 * tokens * own),
            transcendentals=tokens * own,
        ),
    )(x, c, gate_up, gate_up, down)


def gather(x, axis):
    return lax.all_gather(x, axis, axis=0, tiled=True)


def scatter_sum(x, axis):
    return lax.psum_scatter(x, axis, scatter_dimension=0, tiled=True)


def exchange(x, axis):
    return lax.all_to_all(x, axis, split_axis=0, concat_axis=0, tiled=True)


def per_device(tokens, lengths, gain_attn, w_qkv, w_out, gain_mlp, w_gateup, w_down, cotangent):
    rows, width = tokens.shape[1:]
    wide, narrow = lax.axis_size("wide"), lax.axis_size("narrow")
    pack_rows = rows * wide
    query_width, key_width = HEADS * HEAD_DIM, KV_HEADS * HEAD_DIM
    groups = HEADS // wide
    copies = wide // KV_HEADS
    own_ff = FF // narrow
    first, positions = places(lengths[0], pack_rows)
    cos_all, sin_all = rotary(positions.astype(F32), HALF)
    first_row = lax.axis_index("wide") * rows
    cos = lax.dynamic_slice_in_dim(cos_all, first_row, rows, 1)
    sin = lax.dynamic_slice_in_dim(sin_all, first_row, rows, 1)
    cos_all = cos_all.reshape(HALF, wide, rows).transpose(1, 0, 2)
    sin_all = sin_all.reshape(HALF, wide, rows).transpose(1, 0, 2)
    start = first.reshape(wide, 1, rows)

    gains = jnp.stack([gain_attn, gain_mlp], -1)
    with_gains = jnp.concatenate([w_qkv, jnp.pad(gains, ((0, 0), (0, 126)))], -1)
    qkv_gained = gather(with_gains, BOTH)
    qkv_whole = qkv_gained[:, : w_qkv.shape[1]]
    gain_one = qkv_gained[:, w_qkv.shape[1]].astype(F32)
    gain_two = qkv_gained[:, w_qkv.shape[1] + 1].astype(F32)
    out_whole = gather(w_out, BOTH)
    shard = w_gateup.shape[0]
    gateup_cut = w_gateup.reshape(shard, 2, wide, narrow, -1).transpose(3, 0, 1, 2, 4)
    gateup_own = gather(
        exchange(gateup_cut.reshape(narrow, shard, 2 * own_ff), "narrow").reshape(-1, 2 * own_ff),
        "wide",
    )
    down_own = gather(w_down, "wide")
    cot_group = gather(cotangent[0], "narrow")

    inputs = tokens[0].astype(F32)
    scale_one = lax.rsqrt(jnp.mean(inputs * inputs, -1, keepdims=True) + EPS)
    unit_one = inputs * scale_one
    normed_one = (unit_one * gain_one).astype(BF16)
    projected = dot(qkv_whole, normed_one, (((0,), (1,)), ((), ())))
    turning = projected[: query_width + key_width].reshape(HEADS + KV_HEADS, 2, HALF, rows)
    front, back = turning[:, 0], turning[:, 1]
    turned = jnp.stack([front * cos - back * sin, back * cos + front * sin], 1)
    queries = (turned[:HEADS] * SCORE_SCALE).astype(BF16).reshape(wide, groups * HEAD_DIM, rows)
    keys = turned[HEADS:].astype(BF16).reshape(KV_HEADS, HEAD_DIM, rows)
    values = projected[query_width + key_width :].astype(BF16).reshape(KV_HEADS, HEAD_DIM, rows)
    keys_values = jnp.repeat(jnp.concatenate([keys, values], 1), copies, 0)
    heads = exchange(jnp.concatenate([queries, keys_values], 1), "wide")
    attended_heads, attended_full, log_total = attend(heads, start, groups)
    attended_low = exchange(attended_heads, "wide").reshape(query_width, rows)
    middle = inputs + dot(attended_low, out_whole, TN)
    scale_two = lax.rsqrt(jnp.mean(middle * middle, -1, keepdims=True) + EPS)
    unit_two = middle * scale_two
    normed_two = (unit_two * gain_two).astype(BF16)

    normed_group = gather(normed_two, "narrow")
    hidden, grad_gate, grad_up = middle_part(normed_group, cot_group, gateup_own, down_own)
    grad_gate_up = jnp.concatenate([grad_gate, grad_up], -1)
    grad_normed_two = scatter_sum(dot(grad_gate_up, gateup_own, NT, BF16), "narrow").astype(F32)
    layer_out = (middle + scatter_sum(dot(hidden, down_own, NN, BF16), "narrow")).astype(BF16)[None]
    grad_down = scatter_sum(dot(hidden, cot_group, TN, BF16), "wide").astype(F32)
    grad_gateup = scatter_sum(dot(normed_group, grad_gate_up, TN, BF16), "wide")
    grad_gateup = exchange(grad_gateup.reshape(narrow, shard, 2 * own_ff), "narrow")
    grad_gateup = (
        grad_gateup.reshape(narrow, shard, 2, wide, -1)
        .transpose(1, 2, 3, 0, 4)
        .reshape(shard, 2 * FF)
        .astype(F32)
    )

    part_gain_two = jnp.sum(grad_normed_two * unit_two, 0)
    grad_middle = cotangent[0].astype(F32) + norm_back(
        grad_normed_two * gain_two, unit_two, scale_two
    )
    grad_branch = grad_middle.astype(BF16)
    grad_wout = scatter_sum(dot(attended_low, grad_branch, NN, BF16), BOTH).astype(F32)
    grad_attended = dot(out_whole, grad_branch, NT, BF16).reshape(wide, groups * HEAD_DIM, rows)
    grad_heads = attend_back(
        heads, exchange(grad_attended, "wide"), attended_full, log_total, start, cos_all, sin_all,
        groups,
    )
    grad_heads = exchange(grad_heads, "wide")
    grad_queries = grad_heads[:, : groups * HEAD_DIM].reshape(query_width, rows)
    grad_keys_values = (
        grad_heads[:, groups * HEAD_DIM :]
        .reshape(KV_HEADS, copies, 2, HEAD_DIM, rows)
        .astype(F32)
        .sum(1)
        .astype(BF16)
    )
    grad_projected = jnp.concatenate(
        [
            grad_queries,
            grad_keys_values[:, 0].reshape(key_width, rows),
            grad_keys_values[:, 1].reshape(key_width, rows),
        ],
        0,
    )
    grad_normed_one = dot(grad_projected, qkv_whole, (((0,), (1,)), ((), ())))
    part_gain_one = jnp.sum(grad_normed_one * unit_one, 0)
    part_gains = jnp.stack([part_gain_one, part_gain_two], -1)
    part_qkv = dot(normed_one, grad_projected, (((0,), (1,)), ((), ())), BF16)
    grad_qkv = scatter_sum(part_qkv, BOTH).astype(F32)
    grad_gains = scatter_sum(part_gains, BOTH)
    grad_inputs = grad_middle + norm_back(grad_normed_one * gain_one, unit_one, scale_one)
    grad_tokens = grad_inputs.astype(BF16)[None]
    return (
        layer_out,
        grad_tokens,
        grad_gains[:, 0],
        grad_qkv,
        grad_wout,
        grad_gains[:, 1],
        grad_gateup,
        grad_down,
    )


def solution(mesh):
    rows, packs = P("narrow", "wide", None), P("narrow", None)
    weight, gain = P(BOTH, None), P(BOTH)
    return jax.shard_map(
        per_device,
        mesh=mesh,
        in_specs=(rows, packs, gain, weight, weight, gain, weight, weight, rows),
        out_specs=(rows, rows, gain, weight, weight, gain, weight, weight),
        check_vma=False,
    )
```

time: 5960 us -> 1490 us (0.25)
  waiting for transfers between devices: 5510 us -> 1000 us
  matrix products: 275 us -> 118 us
  Pallas kernels: 0 us -> 130 us
    unnamed x12 -> x14, waiting for transfers between devices: 2810 us -> 121 us
    reduce_scatter x4 -> x6, waiting for transfers between devices: 2030 us -> 529 us  [scatter_sum(): return lax.psum_scatter(x, axis, scatter_dimension=0, tiled=True)]
    all_gather x6, waiting for transfers between devices: 668 us -> 322 us  [gather(): return lax.all_gather(x, axis, axis=0, tiled=True)]
    dot_general x19 -> x10, matrix products: 275 us -> 118 us  [dot(): lax.dot_general(left, right, dims, preferred_element_type=F32).astype(kind)]
    all_to_all x0 -> x3, blocking collectives: none -> 133 us  [exchange(): return lax.all_to_all(x, axis, split_axis=0, concat_axis=0, tiled=True)]
    pallas_call x0 -> x3, Pallas kernels: none -> 130 us  [the longest x1 48 us: attend_back(): pl.pallas_call(functools.partial(attend_back_kernel, groups), grid=(block...]
    unnamed x2 -> x0, blocking collectives: 85.9 us -> none
  transfers between devices with their start and end apart: 11 -> 16, of which waited for: 11 -> 13; matrix products, arithmetic and copies ran while one was open for 3% -> 9% of each run, Pallas kernels for 0% -> 6%
where the time goes in v1:
time: 1490 us; the launch traced here: 1480 us
  waiting for transfers between devices  1000 us (67%)
  blocking collectives  133 us (9%)
  Pallas kernels  130 us (9%)
  matrix products  118 us (8%)
  local copies, waits for them, and re-layouts  42.7 us (3%)
  other arithmetic  24.8 us (2%)
    reduce_scatter x6, waiting for transfers between devices, scatter_sum(): return lax.psum_scatter(x, axis, scatter_dimension=0, tiled=True)  529 us
    all_gather x6, waiting for transfers between devices, gather(): return lax.all_gather(x, axis, axis=0, tiled=True)  322 us
    all_to_all x3, blocking collectives, exchange(): return lax.all_to_all(x, axis, split_axis=0, concat_axis=0, tiled=True)  133 us
    unnamed x14, waiting for transfers between devices  121 us
    dot_general x10, matrix products, dot(): lax.dot_general(left, right, dims, preferred_element_type=F32).astype(kind)  118 us
    pallas_call x1, Pallas kernels, attend_back(): pl.pallas_call(functools.partial(attend_back_kernel, groups), grid=(block...  48 us
    pallas_call x1, Pallas kernels, attend(): pl.pallas_call(functools.partial(attend_kernel, groups), grid=(blocks,),...  44.3 us
    pallas_call x1, Pallas kernels, middle_part(): pl.pallas_call(functools.partial(middle_kernel, 256), grid=(tiles,), out_...  37.9 us
  transfers between devices with their start and end apart: 16, of which 13 were waited for; matrix products, arithmetic and copies ran while one was open for 9% of the time, Pallas kernels for 6%

profile of v1, /device:TPU:0, one launch (start us, length us, event | category | flops | bytes accessed | tf_op | source)
XLA Modules:
  0.0 1478.1 jit_solution(11615438816814440911)
XLA Ops:
  8.2 1.8 fusion.32
  12.1 2.8 reshape.180
  14.8 1.9 copy.30
  16.7 2.3 reshape.181
  19.1 79.1 %all_to_all.30 = bf16[4,64,4096]{2,1,0:T(8,128)(2,1)} all-to-all(bf16[4,64,4096]{2,1,0:T(8,128)(2,1)} %reshape.181), channel_id=1, replica_groups=mesh['wide'=8,'narrow'=4] {'narrow'}, dimensions={0} | all-to-all | bytes 4194304 | tf_op jit(solution)/shard_map/all_to_all | solution.py:303
  99.8 38.6 %all-gather.8.cloned.1.call-done = bf16[2048,3200]{1,0:T(8,128)(2,1)} async-done(((bf16[64,3200]{1,0:T(8,128)(2,1)}), bf16[2048,3200]{1,0:T(8,128)(2,1)}) %all-gather.8.cloned.1.call-update) | async-done | bytes 13107216 | tf_op jit(solution)/shard_map/all_gather | solution.py:295
  138.4 1.8 convert_reduce_fusion
  140.2 6.7 fusion.2
  148.1 24.2 %all_to_all.31.x_ref = bf16[8,384,256]{2,1,0:T(8,128)(2,1)S(1)} all-to-all(bf16[8,384,256]{2,1,0:T(8,128)(2,1)S(1)} %pad_maximum_fusion), channel_id=1, replica_groups=mesh['wide'=8,'narrow'=4] {'wide'}, dimensions={0} | all-to-all | bytes 3145728 | tf_op jit(solution)/shard_map/all_to_all | solution.py:303
  172.3 44.3 %shard_map.152 = (bf16[8,256,256]{2,1,0:T(8,128)(2,1)}, f32[8,256,256]{2,1,0:T(8,128)S(1)}, f32[8,4,256]{2,1,0:T(4,128)S(1)}) custom-call(s32[8,1,256]{2,1,0:T(1,128)S(1)} %bitcast.72, bf16[8,384,256]{2,1,0:T(8,128)(2,1)S(1)} %all_to_all.31.x_ref), custom_call_target="tpu_custom_call" | custom-call | flops 17179869184 | bytes 3145728 | tf_op jit(solution)/shard_map/pallas_call | solution.py:110
  217.9 4.2 all-to-all-start.1
  222.2 15.3 %all-to-all-done.1 = bf16[8,256,256]{2,1,0:T(8,128)(2,1)} async-done(((bf16[8,256,256]{2,1,0:T(8,128)(2,1)}), bf16[8,256,256]{2,1,0:T(8,128)(2,1)}, u32[]{:S(2)}, u32[]{:S(2)}) %all-to-all-start.1) | async-done | bytes 1048608 | tf_op jit(solution)/shard_map/all_to_all | solution.py:303
  237.6 6.2 multiply_reduce_fusion
  246.9 53.8 %all-gather.18.cloned.1.call-done = bf16[1,1024,2048]{2,1,0:T(8,128)(2,1)} async-done(((bf16[1,256,2048]{2,1,0:T(8,128)(2,1)}), bf16[1,1024,2048]{2,1,0:T(8,128)(2,1)}) %all-gather.18.cloned.1.call-update) | async-done | bytes 4194320 | tf_op jit(solution)/shard_map/all_gather | solution.py:295
  300.8 54.7 %all-gather.16.cloned.1.call-done.down_ref = bf16[2048,2048]{1,0:T(8,128)(2,1)} async-done(((bf16[256,2048]{1,0:T(8,128)(2,1)}), bf16[2048,2048]{1,0:T(8,128)(2,1)}) %all-gather.16.cloned.1.call-update) | async-done | bytes 8388624 | tf_op jit(solution)/shard_map/all_gather | solution.py:295
  355.5 91.6 %all-gather.14.cloned.1.call-done.gate_ref.up_ref = bf16[2048,4096]{1,0:T(8,128)(2,1)} async-done(((bf16[256,4096]{1,0:T(8,128)(2,1)}), bf16[2048,4096]{1,0:T(8,128)(2,1)}) %all-gather.14.cloned.1.call-update) | async-done | bytes 16777232 | tf_op jit(solution)/shard_map/all_gather | solution.py:295
  447.1 82.8 %all-gather.12.cloned.1.call-done.x_ref = bf16[1024,2048]{1,0:T(8,128)(2,1)} async-done(((bf16[256,2048]{1,0:T(8,128)(2,1)}), bf16[1024,2048]{1,0:T(8,128)(2,1)}) %all-gather.12.cloned.1.call-update) | async-done | bytes 4194320 | tf_op jit(solution)/shard_map/all_gather | solution.py:295
  529.9 37.9 %shard_map.153 = (bf16[1024,2048]{1,0:T(8,128)(2,1)}, bf16[1024,2048]{1,0:T(8,128)(2,1)}, bf16[1024,2048]{1,0:T(8,128)(2,1)}) custom-call(bf16[1024,2048]{1,0:T(8,128)(2,1)} %all-gather.12.cloned.1.call-done.x_ref, bf16[1024,2048]{1,0:T(8,128)(2,1)} %bitcast.96, bf16[2048,4096]{1,0:T(8,128)(2,1)} %all-gather.14.cloned.1.call-done.gate_ref.up_ref, ...), custom_call_target="tpu_custom_call" | custom-call | flops 25769803776 | bytes 46137344 | tf_op jit(solution)/shard_map/pallas_call | solution.py:273
  567.8 2.7 constant_dynamic-update-slice_fusion.1
  571.5 3.3 copy-done.10
  574.9 21.3 %convolution_convert_fusion.4 = bf16[1024,2048]{1,0:T(8,128)(2,1)} fusion(bf16[1024,4096]{1,0:T(8,128)(2,1)S(1)} %constant_dynamic-update-slice_fusion, bf16[2048,4096]{1,0:T(8,128)(2,1)} %all-gather.14.cloned.1.call-done.gate_ref.up_ref), kind=kOutput, calls=%fused_computation.9 | convolution fusion | flops 17181966336 | bytes 29360128 | tf_op jit(solution)/shard_map/dot_general | solution.py:28
  596.2 13.9 convolution_convert_fusion.5
  610.4 24.8 %convolution_convert_fusion = bf16[2048,4096]{1,0:T(8,128)(2,1)} fusion(bf16[1024,2048]{1,0:T(8,128)(2,1)} %all-gather.12.cloned.1.call-done.x_ref, bf16[1024,4096]{1,0:T(8,128)(2,1)} %copy-done.10), kind=kOutput, calls=%fused_computation | convolution fusion | flops 17188257792 | bytes 29360128 | tf_op jit(solution)/shard_map/dot_general | solution.py:28
  635.2 36.4 %reduce-scatter.12.cloned.1.call-done = bf16[256,2048]{1,0:T(8,128)(2,1)} async-done(((bf16[1024,2048]{1,0:T(8,128)(2,1)}), bf16[256,2048]{1,0:T(8,128)(2,1)}) %reduce-scatter.12.cloned.1.call-update) | async-done | bytes 1048592 | tf_op jit(solution)/shard_map/reduce_scatter | solution.py:299
  671.6 2.7 fusion.17
  674.3 77.0 %reduce-scatter.10.cloned.1.call-done = bf16[256,2048]{1,0:T(8,128)(2,1)} async-done(((bf16[1024,2048]{1,0:T(8,128)(2,1)}), bf16[256,2048]{1,0:T(8,128)(2,1)}) %reduce-scatter.10.cloned.1.call-update) | async-done | bytes 1048592 | tf_op jit(solution)/shard_map/reduce_scatter | solution.py:299
  751.3 4.1 fusion.13
  756.7 5.7 fusion.10
  763.8 3.6 all-to-all-start.3
  768.5 14.3 all-to-all-done.3.grad_ref
  784.6 48.0 %shard_map.154 = bf16[8,384,256]{2,1,0:T(8,128)(2,1)S(1)} custom-call(s32[8,1,256]{2,1,0:T(1,128)S(1)} %bitcast.73, bf16[8,384,256]{2,1,0:T(8,128)(2,1)S(1)} %all_to_all.31.x_ref, bf16[8,256,256]{2,1,0:T(8,128)(2,1)S(1)} %all-to-all-done.3.grad_ref, f32[8,256,256]{2,1,0:T(8,128)S(1)} %copy-done.1, f32[8,4,256]{2,1,0:T(4,128)S(1)} %get-tuple-element.19.log_ref, ...), custom_call_target="tpu_custom_call" | custom-call | flops 42949672960 | bytes 6291456 | tf_op jit(solution)/shard_map/pallas_call | solution.py:219
  832.6 29.4 %all_to_all.32 = bf16[8,384,256]{2,1,0:T(8,128)(2,1)S(1)} all-to-all(bf16[8,384,256]{2,1,0:T(8,128)(2,1)S(1)} %shard_map.154), channel_id=1, replica_groups=mesh['wide'=8,'narrow'=4] {'wide'}, dimensions={0} | all-to-all | bytes 3145728 | tf_op jit(solution)/shard_map/all_to_all | solution.py:303
  863.8 10.1 fusion.24
  875.4 14.4 convolution_convert_fusion.2
  891.4 6.8 convolution_convert_fusion.3
  898.3 8.0 convolution_convert_fusion.1
  906.3 4.8 all-to-all-start.5
  911.2 3.2 fusion.27
  914.4 118.5 %reduce-scatter.22.cloned.1.call-done = f32[64,2]{1,0:T(8,128)} async-done(((f32[2048,2]{1,0:T(8,128)}), f32[64,2]{1,0:T(8,128)}) %reduce-scatter.22.cloned.1.call-update) | async-done | bytes 528
  1034.9 73.3 %reduce-scatter.20.cloned.1.call-done = bf16[256,2048]{1,0:T(8,128)(2,1)} async-done(((bf16[2048,2048]{1,0:T(8,128)(2,1)}), bf16[256,2048]{1,0:T(8,128)(2,1)}) %reduce-scatter.20.cloned.1.call-update) | async-done | bytes 1048592 | tf_op jit(solution)/shard_map/reduce_scatter | solution.py:299
  1108.2 2.8 convert_element_type.152
  1111.0 185.2 %reduce-scatter.16.cloned.1.call-done = bf16[64,2048]{1,0:T(8,128)(2,1)} async-done(((bf16[2048,2048]{1,0:T(8,128)(2,1)}), bf16[64,2048]{1,0:T(8,128)(2,1)}) %reduce-scatter.16.cloned.1.call-update) | async-done | bytes 262160 | tf_op jit(solution)/shard_map/reduce_scatter | solution.py:299
  1296.1 1.8 convert_element_type.145
  1297.9 157.3 %reduce-scatter.14.cloned.1.call-done = bf16[64,3072]{1,0:T(8,128)(2,1)} async-done(((bf16[2048,3072]{1,0:T(8,128)(2,1)}), bf16[64,3072]{1,0:T(8,128)(2,1)}) %reduce-scatter.14.cloned.1.call-update) | async-done | bytes 393232 | tf_op jit(solution)/shard_map/reduce_scatter | solution.py:299
  1455.3 1.9 convert_element_type.143
  1457.2 2.2 copy.38
  1459.4 5.9 copy.40
  1465.3 5.8 reshape.190
  (103 shorter events, 24.0 us)
Async XLA Ops:
  7.2 4.9 copy-start.11
  7.2 131.3 %all-gather.8.cloned.1.call-start = ((), (), s32[]{:S(2)}) async-start(), calls=%async_computation.13 | async-start | bytes 13516800 | tf_op jit(solution)/shard_map/all_gather | solution.py:295
  10.0 212.3 %all-gather.10.cloned.1.call-start = ((), (), s32[]{:S(2)}) async-start(), calls=%async_computation.14 | async-start | bytes 8650752 | tf_op jit(solution)/shard_map/all_gather | solution.py:295
  10.7 290.0 %all-gather.18.cloned.1.call-start = ((), (), s32[]{:S(2)}) async-start(), calls=%async_computation.24 | async-start | bytes 5242880 | tf_op jit(solution)/shard_map/all_gather | solution.py:295
  11.4 344.0 %all-gather.16.cloned.1.call-start = ((), (), s32[]{:S(2)}) async-start(), calls=%async_computation.17 | async-start | bytes 9437184 | tf_op jit(solution)/shard_map/all_gather | solution.py:295
  12.0 435.1 %all-gather.14.cloned.1.call-start = ((), (), s32[]{:S(2)}) async-start(), calls=%async_computation.16 | async-start | bytes 18874368 | tf_op jit(solution)/shard_map/all_gather | solution.py:295
  98.2 0.7 copy-start.19
  98.2 1.3 copy-start.5
  99.0 47.8 %copy-start.17 = (f32[32]{0:T(128)}, f32[32]{0:T(128)S(1)}, u32[]{:S(2)}) copy-start(f32[32]{0:T(128)S(1)} %compare_select_fusion.1) | copy-start | bytes 388
  99.8 47.1 %copy-start.15 = (f32[256]{0:T(256)}, f32[256]{0:T(256)S(1)}, u32[]{:S(2)}) copy-start(f32[256]{0:T(256)S(1)} %add_rsqrt_fusion.1) | copy-start | bytes 3076
  140.2 6.7 copy-start.13
  216.6 1.3 copy-start
  217.9 19.7 %all-to-all-start.1 = ((bf16[8,256,256]{2,1,0:T(8,128)(2,1)}), bf16[8,256,256]{2,1,0:T(8,128)(2,1)}, u32[]{:S(2)}, u32[]{:S(2)}) async-start(bf16[8,256,256]{2,1,0:T(8,128)(2,1)} %get-tuple-element.14), calls=%async_computation.1 | async-start | bytes 2097152 | tf_op jit(solution)/shard_map/all_to_all | solution.py:303
  222.2 307.7 %all-gather.12.cloned.1.call-start = ((), (), s32[]{:S(2)}) async-start(), calls=%async_computation.15 | async-start | bytes 5242880 | tf_op jit(solution)/shard_map/all_gather | solution.py:295
  243.8 1.3 copy-start.2
  246.4 425.3 %reduce-scatter.12.cloned.1.call-start = ((), (), s32[]{:S(2)}) async-start(), calls=%async_computation.19 | async-start | bytes 5242880 | tf_op jit(solution)/shard_map/reduce_scatter | solution.py:299
  567.8 3.4 copy-start.8
  571.5 3.3 copy-start.10
  596.2 155.2 %reduce-scatter.10.cloned.1.call-start = ((), (), s32[]{:S(2)}) async-start(), calls=%async_computation.18 | async-start | bytes 5242880 | tf_op jit(solution)/shard_map/reduce_scatter | solution.py:299
  610.2 296.2 %reduce-scatter.18.cloned.1.call-start = ((), (), s32[]{:S(2)}) async-start(), calls=%async_computation.22 | async-start | bytes 18874368 | tf_op jit(solution)/shard_map/reduce_scatter | solution.py:299
  635.2 116.1 %copy-start.9 = (bf16[1,256,2048]{2,1,0:T(8,128)(2,1)S(1)}, bf16[1,256,2048]{2,1,0:T(8,128)(2,1)}, u32[]{:S(2)}) copy-start(bf16[1,256,2048]{2,1,0:T(8,128)(2,1)} %param.17) | copy-start | bytes 3145732
  755.4 1.3 copy-start.3
  762.5 5.0 copy-start.18
  763.8 19.1 %all-to-all-start.3 = ((bf16[8,256,256]{2,1,0:T(8,128)(2,1)}), bf16[8,256,256]{2,1,0:T(8,128)(2,1)S(1)}, u32[]{:S(2)}, u32[]{:S(2)}) async-start(bf16[8,256,256]{2,1,0:T(8,128)(2,1)} %bitcast.82), calls=%async_computation.5 | async-start | bytes 2097152 | tf_op jit(solution)/shard_map/all_to_all | solution.py:303
  767.5 265.4 %reduce-scatter.22.cloned.1.call-start = ((), (), s32[]{:S(2)}) async-start(), calls=%async_computation.25 | async-start | bytes 1081344
  782.9 1.7 copy-start.1
  862.1 1.7 copy-start.6
  862.1 1.7 copy-start.14
  862.1 1.7 copy-start.16
  862.2 11.8 copy-start.7
  862.2 11.7 copy-start.12
  875.4 232.8 %reduce-scatter.20.cloned.1.call-start = ((), (), s32[]{:S(2)}) async-start(), calls=%async_computation.23 | async-start | bytes 9437184 | tf_op jit(solution)/shard_map/reduce_scatter | solution.py:299
  889.8 1.6 copy-start.4
  889.9 406.3 %reduce-scatter.16.cloned.1.call-start = ((), (), s32[]{:S(2)}) async-start(), calls=%async_computation.21 | async-start | bytes 8650752 | tf_op jit(solution)/shard_map/reduce_scatter | solution.py:299
  898.2 557.0 %reduce-scatter.14.cloned.1.call-start = ((), (), s32[]{:S(2)}) async-start(), calls=%async_computation.20 | async-start | bytes 12976128 | tf_op jit(solution)/shard_map/reduce_scatter | solution.py:299
  906.3 550.9 %all-to-all-start.5 = ((bf16[4,64,4096]{2,1,0:T(8,128)(2,1)}), bf16[4,64,4096]{2,1,0:T(8,128)(2,1)}, u32[]{:S(2)}, u32[]{:S(2)}) async-start(bf16[4,64,4096]{2,1,0:T(8,128)(2,1)} %bitcast.83), calls=%async_computation.10 | async-start | bytes 4194304 | tf_op jit(solution)/shard_map/all_to_all | solution.py:303
Sparse Core Ops, SparseCore 0:
  11.4 126.9 all-gather.7
  141.4 78.2 all-gather.9
  221.2 79.4 all-gather.17
  302.5 52.9 all-gather.15
  357.2 89.8 all-gather.13
  449.1 80.7 all-gather.11
  596.3 75.2 reduce-scatter.11
  674.0 77.2 reduce-scatter.9
  754.9 124.4 reduce-scatter.17
  881.5 151.2 reduce-scatter.21
  1036.7 71.4 reduce-scatter.19
  1110.3 185.7 reduce-scatter.15
  1302.2 153.0 reduce-scatter.13

commit v2 on v1

--- a/solution.py
+++ b/solution.py
@@ -246,51 +246,6 @@
     )(start, x, grad, full, log_total, cos, sin)
 
 
-def middle_kernel(step_rows, x_ref, c_ref, gate_ref, up_ref, down_ref, hidden_ref, dgate_ref, dup_ref):
-    def step(t, carry):
-        rows = pl.ds(pl.multiple_of(t * step_rows, step_rows), step_rows)
-        x = x_ref[rows, :]
-        gate = dot(x, gate_ref[...], NN)
-        up = dot(x, up_ref[...], NN)
-        grad = dot(c_ref[rows, :], down_ref[...], NT)
-        sig = 1.0 / (1.0 + jnp.exp(-gate))
-        silu = gate * sig
-        hidden_ref[rows, :] = (silu * up).astype(BF16)
-        dgate_ref[rows, :] = (grad * up * (sig + silu * (1.0 - sig))).astype(BF16)
-        dup_ref[rows, :] = (grad * silu).astype(BF16)
-        return carry
-
-    lax.fori_loop(0, x_ref.shape[0] // step_rows, step, 0)
-
-
-def middle_part(x, c, gate_up, down):
-    tokens, width = x.shape
-    own = down.shape[0]
-    tile = min(256, own)
-    tiles = own // tile
-    shape = jax.ShapeDtypeStruct((tokens, own), BF16)
-    out = pl.BlockSpec((tokens, tile), lambda f: (0, f))
-    return pl.pallas_call(
-        functools.partial(middle_kernel, 256),
-        grid=(tiles,),
-        out_shape=(shape, shape, shape),
-        in_specs=[
-            pl.BlockSpec((tokens, width), lambda f: (0, 0)),
-            pl.BlockSpec((tokens, width), lambda f: (0, 0)),
-            pl.BlockSpec((width, tile), lambda f: (0, f)),
-            pl.BlockSpec((width, tile), lambda f: (0, f + tiles)),
-            pl.BlockSpec((tile, width), lambda f: (f, 0)),
-        ],
-        out_specs=(out, out, out),
-        compiler_params=pltpu.CompilerParams(vmem_limit_bytes=56 << 20),
-        cost_estimate=pl.CostEstimate(
-            flops=6 * tokens * width * own,
-            bytes_accessed=2 * (2 * tokens * width + 3 * width * own + 3 * tokens * own),
-            transcendentals=tokens * own,
-        ),
-    )(x, c, gate_up, gate_up, down)
-
-
 def gather(x, axis):
     return lax.all_gather(x, axis, axis=0, tiled=True)
 
@@ -301,6 +256,555 @@
 
 def exchange(x, axis):
     return lax.all_to_all(x, axis, split_axis=0, concat_axis=0, tiled=True)
+
+
+def across(x, mask):
+    return lax.ppermute(x, "wide", [(i, i ^ mask) for i in range(lax.axis_size("wide"))])
+
+
+def shift(x, step):
+    n = lax.axis_size("narrow")
+    return lax.ppermute(x, "narrow", [(i, (i + step) % n) for i in range(n)])
+
+
+def pick(x, index, axis):
+    return lax.dynamic_index_in_dim(x, index, axis, keepdims=False)
+
+
+def plus(left, right, kind=BF16):
+    return (left.astype(F32) + right.astype(F32)).astype(kind)
+
+
+def shift_exchange(x):
+    n, me = x.shape[0], lax.axis_index("narrow")
+    out = jnp.zeros_like(x)
+    out = lax.dynamic_update_index_in_dim(out, pick(x, me, 0), me, 0)
+    for step in range(1, n):
+        came = shift(pick(x, (me + step) % n, 0), step)
+        out = lax.dynamic_update_index_in_dim(out, came, (me - step) % n, 0)
+    return out
+
+
+def shift_gather(x):
+    n, me = lax.axis_size("narrow"), lax.axis_index("narrow")
+    out = jnp.zeros((n,) + x.shape, x.dtype)
+    out = lax.dynamic_update_index_in_dim(out, x, me, 0)
+    for step in range(1, n):
+        out = lax.dynamic_update_index_in_dim(out, shift(x, step), (me - step) % n, 0)
+    return out.reshape((-1,) + x.shape[1:])
+
+
+def shift_scatter_sum(x):
+    n, me = lax.axis_size("narrow"), lax.axis_index("narrow")
+    x = x.reshape((n, -1) + x.shape[1:])
+    total = pick(x, me, 0).astype(F32)
+    for step in range(1, n):
+        total = total + shift(pick(x, (me + step) % n, 0), step).astype(F32)
+    return total
+
+
+def wide_gather(x):
+    wide, me = lax.axis_size("wide"), lax.axis_index("wide")
+    pieces = {0: x}
+    if wide == 8:
+        half = x.shape[0] // 2
+        pieces[2] = across(x, 2)
+        pieces[4] = across(x, 4)
+        pieces[6] = jnp.concatenate(
+            [across(pieces[2][:half], 4), across(pieces[4][half:], 2)], 0
+        )
+    else:
+        for mask in range(2, wide, 2):
+            pieces[mask] = across(x, mask)
+    for mask in range(0, wide, 2):
+        pieces[mask + 1] = across(pieces[mask], 1)
+    out = jnp.zeros((wide,) + x.shape, x.dtype)
+    for mask in range(wide):
+        out = lax.dynamic_update_index_in_dim(out, pieces[mask], me ^ mask, 0)
+    return out.reshape((-1,) + x.shape[1:])
+
+
+def wide_scatter_sum(make, kind=BF16):
+    wide, me = lax.axis_size("wide"), lax.axis_index("wide")
+    chips = wide // 2
+    core, chip = me % 2, me // 2
+    came = across(make(1 - core), 1)
+    held = plus(make(core), came)
+    if chips == 4:
+        x, y = chip % 2, chip // 2
+        columns = held.shape[2]
+        held = held.reshape((2, 2) + held.shape[1:])
+        left, right = held[..., : columns // 2], held[..., columns // 2 :]
+        left = plus(pick(left, x, 1), across(pick(left, 1 - x, 1), 2))
+        right = plus(pick(right, y, 0), across(pick(right, 1 - y, 0), 4))
+        left = plus(pick(left, y, 0), across(pick(left, 1 - y, 0), 4), kind)
+        right = plus(pick(right, x, 0), across(pick(right, 1 - x, 0), 2), kind)
+        return jnp.concatenate([left, right], -1)
+    bit = 1
+    while held.shape[0] > 1:
+        held = held.reshape((-1, 2) + held.shape[1:])
+        own = (chip // bit) % 2
+        held = plus(pick(held, own, 1), across(pick(held, 1 - own, 1), 2 * bit))
+        bit *= 2
+    return held[0].astype(kind)
+
+
+MESH = pl.DeviceIdType.MESH
+
+
+def gather_kernel(
+    wide, narrow, lag, qkv_ref, out_w_ref, cut_ref, qkv_all, out_all, cut_all,
+    own_sem, x_send, x_recv, z_sends, z_recvs, m_sends, m_recvs, r_sends, r_recvs, c_sends, c_recvs,
+):
+    w, n = lax.axis_index("wide"), lax.axis_index("narrow")
+    relay = wide == 8
+    masks = [2, 4] if relay else list(range(2, wide, 2))
+    chips = wide // 2
+
+    def to_wide(mask):
+        return {"wide": w ^ mask, "narrow": n}
+
+    def to_narrow(other):
+        return {"wide": w, "narrow": other}
+
+    barrier = pltpu.get_barrier_semaphore()
+    for mask in [1] + masks:
+        pl.semaphore_signal(barrier, inc=1, device_id=to_wide(mask), device_id_type=MESH)
+    for step in range(1, narrow):
+        pl.semaphore_signal(
+            barrier, inc=1, device_id=to_narrow(lax.rem(n + step, narrow)), device_id_type=MESH
+        )
+    pl.semaphore_wait(barrier, len(masks) + narrow)
+
+    def owner_of(side, d):
+        return n - d if side == 0 else n + d
+
+    def valid(side, d):
+        return n - d >= 0 if side == 0 else n + d < narrow
+
+    def can_pass(side, d):
+        if side == 0:
+            return (n - (d - 1) >= 0) & (n < narrow - 1)
+        return (n + (d - 1) < narrow) & (n > 0)
+
+    def slot(side, d):
+        return d - 1 + side * (narrow - 1) if d else 2 * (narrow - 1)
+
+    def at_distance(d, action):
+        if d == 0:
+            action(0, 0)
+            return
+        for side in (0, 1):
+            pl.when(valid(side, d))(functools.partial(action, side, d))
+
+    class Flow:
+        def __init__(self, index, x_ref, out_ref):
+            self.x_ref, self.out_ref = x_ref, out_ref
+            self.z_send, self.z_recv = z_sends.at[index], z_recvs.at[index]
+            self.m_send, self.m_recv = m_sends.at[index], m_recvs.at[index]
+            self.r_send, self.r_recv = r_sends.at[index], r_recvs.at[index]
+            self.c_send, self.c_recv = c_sends.at[index], c_recvs.at[index]
+            self.own = pltpu.make_async_copy(x_ref, self.place(w, n), own_sem.at[index])
+
+        def place(self, owner_w, owner_n, part=None):
+            depth = self.x_ref.shape[0]
+            half = depth // 2
+            at = (owner_w * narrow + owner_n) * depth
+            if part is None:
+                return self.out_ref.at[pl.ds(pl.multiple_of(at, depth), depth), :]
+            return self.out_ref.at[pl.ds(pl.multiple_of(at + part * half, half), half), :]
+
+        def z_copy(self, side, d):
+            block = owner_of(side, d - 1)
+            return pltpu.make_async_remote_copy(
+                src_ref=self.x_ref if d == 1 else self.place(w, block),
+                dst_ref=self.place(w, block),
+                send_sem=self.z_send.at[side, d],
+                recv_sem=self.z_recv.at[side, d],
+                device_id=to_narrow(n + 1 if side == 0 else n - 1),
+                device_id_type=MESH,
+            )
+
+        def z_wait(self, side, d):
+            block = self.place(w, owner_of(side, d))
+            pltpu.make_async_copy(block, block, self.z_recv.at[side, d]).wait()
+
+        def m_copy(self, i, side, d):
+            block = self.place(w, owner_of(side, d))
+            return pltpu.make_async_remote_copy(
+                src_ref=self.x_ref if d == 0 else block,
+                dst_ref=block,
+                send_sem=self.m_send.at[i, slot(side, d)],
+                recv_sem=self.m_recv.at[i, slot(side, d)],
+                device_id=to_wide(masks[i]),
+                device_id_type=MESH,
+            )
+
+        def m_wait(self, i, side, d):
+            block = self.place(w ^ masks[i], owner_of(side, d))
+            pltpu.make_async_copy(block, block, self.m_recv.at[i, slot(side, d)]).wait()
+
+        def r_copy(self, part, side, d):
+            block = self.place(w ^ masks[part], owner_of(side, d), part)
+            return pltpu.make_async_remote_copy(
+                src_ref=block,
+                dst_ref=block,
+                send_sem=self.r_send.at[part, slot(side, d)],
+                recv_sem=self.r_recv.at[part, slot(side, d)],
+                device_id=to_wide(masks[1 - part]),
+                device_id_type=MESH,
+            )
+
+        def r_wait(self, part, side, d):
+            block = self.place(w ^ 6, owner_of(side, d), part)
+            pltpu.make_async_copy(block, block, self.r_recv.at[part, slot(side, d)]).wait()
+
+        def c_copy(self, chip, side, d):
+            block = self.place(w ^ (2 * chip), owner_of(side, d))
+            return pltpu.make_async_remote_copy(
+                src_ref=self.x_ref if d == 0 and chip == 0 else block,
+                dst_ref=block,
+                send_sem=self.c_send.at[chip, slot(side, d)],
+                recv_sem=self.c_recv.at[chip, slot(side, d)],
+                device_id=to_wide(1),
+                device_id_type=MESH,
+            )
+
+        def c_wait(self, chip, side, d):
+            block = self.place((w ^ 1) ^ (2 * chip), owner_of(side, d))
+            pltpu.make_async_copy(block, block, self.c_recv.at[chip, slot(side, d)]).wait()
+
+        def send_from_here(self, side, d):
+            if d > 0:
+                self.z_wait(side, d)
+            if 0 < d < narrow - 1:
+                pl.when(can_pass(side, d + 1))(lambda: self.z_copy(side, d + 1).start())
+            for i in range(len(masks)):
+                self.m_copy(i, side, d).start()
+            self.c_copy(0, side, d).start()
+
+        def send_on(self, side, d):
+            for i in range(len(masks)):
+                self.m_wait(i, side, d)
+                if relay:
+                    self.r_copy(i, side, d).start()
+                self.c_copy(masks[i] // 2, side, d).start()
+
+        def send_last(self, side, d):
+            self.r_wait(0, side, d)
+            self.r_wait(1, side, d)
+            self.c_copy(3, side, d).start()
+
+        def step(self, t):
+            if t == 0:
+                self.own.start()
+                for side in (0, 1):
+                    pl.when(can_pass(side, 1))(lambda side=side: self.z_copy(side, 1).start())
+            if 0 <= t < narrow:
+                at_distance(t, self.send_from_here)
+            if 0 <= t - 1 < narrow:
+                at_distance(t - 1, self.send_on)
+            if relay and 0 <= t - 2 < narrow:
+                at_distance(t - 2, self.send_last)
+
+        def finish(self, side, d):
+            for i in range(len(masks)):
+                self.m_copy(i, side, d).wait_send()
+                if relay:
+                    self.r_copy(i, side, d).wait_send()
+            for chip in range(chips):
+                self.c_copy(chip, side, d).wait_send()
+                self.c_wait(chip, side, d)
+
+        def end(self):
+            self.own.wait()
+            for side in (0, 1):
+                for d in range(1, narrow):
+                    pl.when(can_pass(side, d))(
+                        lambda side=side, d=d: self.z_copy(side, d).wait_send()
+                    )
+            for d in range(narrow):
+                at_distance(d, self.finish)
+
+    depth = cut_ref.shape[1]
+
+    def rows_of(owner):
+        return cut_all.at[pl.ds(pl.multiple_of(owner * depth, depth), depth), :]
+
+    def cut_copy(step):
+        other = lax.rem(n + step, narrow)
+        return pltpu.make_async_remote_copy(
+            src_ref=cut_ref.at[other],
+            dst_ref=rows_of(n),
+            send_sem=x_send.at[step],
+            recv_sem=x_recv.at[step],
+            device_id=to_narrow(other),
+            device_id_type=MESH,
+        )
+
+    def cut_wait(step):
+        block = rows_of(lax.rem(n + narrow - step, narrow))
+        pltpu.make_async_copy(block, block, x_recv.at[step]).wait()
+
+    flows = [Flow(0, qkv_ref, qkv_all), Flow(1, out_w_ref, out_all)]
+    own_cut = pltpu.make_async_copy(cut_ref.at[n], rows_of(n), own_sem.at[2])
+    own_cut.start()
+    last = narrow + 2
+    for t in range(last + lag):
+        if t < last:
+            flows[0].step(t)
+        if t == min(2, narrow - 1):
+            for step in range(1, narrow):
+                cut_copy(step).start()
+        if t >= lag:
+            flows[1].step(t - lag)
+    for flow in flows:
+        flow.end()
+    own_cut.wait()
+    for step in range(1, narrow):
+        cut_copy(step).wait_send()
+        cut_wait(step)
+
+
+def gather_weights(qkv, out, cut):
+    wide, narrow = lax.axis_size("wide"), lax.axis_size("narrow")
+    slots = 2 * narrow - 1
+    masks = 2 if wide == 8 else wide // 2 - 1
+    dma = pltpu.SemaphoreType.DMA
+    hbm = pl.BlockSpec(memory_space=pl.ANY)
+    every = wide * narrow
+    return pl.pallas_call(
+        functools.partial(gather_kernel, wide, narrow, 3),
+        out_shape=(
+            jax.ShapeDtypeStruct((every * qkv.shape[0], qkv.shape[1]), BF16),
+            jax.ShapeDtypeStruct((every * out.shape[0], out.shape[1]), BF16),
+            jax.ShapeDtypeStruct((narrow * cut.shape[1], cut.shape[2]), BF16),
+        ),
+        in_specs=[hbm, hbm, hbm],
+        out_specs=(hbm, hbm, hbm),
+        scratch_shapes=[
+            dma((3,)),
+            dma((narrow,)),
+            dma((narrow,)),
+            dma((2, 2, narrow)),
+            dma((2, 2, narrow)),
+            dma((2, masks, slots)),
+            dma((2, masks, slots)),
+            dma((2, 2, slots)),
+            dma((2, 2, slots)),
+            dma((2, wide // 2, slots)),
+            dma((2, wide // 2, slots)),
+        ],
+        compiler_params=pltpu.CompilerParams(collective_id=0, has_side_effects=True),
+        cost_estimate=pl.CostEstimate(flops=0, bytes_accessed=300 << 20, transcendentals=0),
+    )(qkv, out, cut)
+
+
+def feed_kernel(
+    narrow, x_ref, cot_ref, gate_up_ref, down_ref,
+    group_ref, hidden_out, grad_out, low_out, grad_x_ref,
+    gate_up, down, cot, hidden, grads, low, came,
+    load_sem, x_send, x_recv, out_sem, g_send, g_recv,
+):
+    w, n = lax.axis_index("wide"), lax.axis_index("narrow")
+    rows, width = x_ref.shape
+    own = down.shape[0]
+    tile = 256
+    tiles = own // tile
+    wtiles = width // tile
+
+    def to_narrow(other):
+        return {"wide": w, "narrow": other}
+
+    loads = [
+        pltpu.make_async_copy(gate_up_ref, gate_up, load_sem.at[0]),
+        pltpu.make_async_copy(down_ref, down, load_sem.at[1]),
+        pltpu.make_async_copy(cot_ref, cot, load_sem.at[2]),
+        pltpu.make_async_copy(x_ref, group_ref.at[n], load_sem.at[3]),
+    ]
+    for load in loads:
+        load.start()
+
+    barrier = pltpu.get_barrier_semaphore()
+    for step in range(1, narrow):
+        pl.semaphore_signal(
+            barrier, inc=1, device_id=to_narrow(lax.rem(n + step, narrow)), device_id_type=MESH
+        )
+    pl.semaphore_wait(barrier, narrow - 1)
+
+    def owner_of(side, d):
+        return n - d if side == 0 else n + d
+
+    def valid(side, d):
+        return n - d >= 0 if side == 0 else (n + d < narrow) & (d > 0)
+
+    def passes(side, d):
+        if side == 0:
+            return (n - d >= 0) & (n < narrow - 1)
+        return (n + d < narrow) & (n > 0)
+
+    def x_copy(side, d):
+        block = group_ref.at[owner_of(side, d)]
+        return pltpu.make_async_remote_copy(
+            src_ref=block,
+            dst_ref=block,
+            send_sem=x_send.at[side, d],
+            recv_sem=x_recv.at[side, d + 1],
+            device_id=to_narrow(n + 1 if side == 0 else n - 1),
+            device_id_type=MESH,
+        )
+
+    def x_wait(side, d):
+        block = group_ref.at[owner_of(side, d)]
+        pltpu.make_async_copy(block, block, x_recv.at[side, d]).wait()
+
+    def out_copies(at, block):
+        return [
+            pltpu.make_async_copy(hidden.at[at], hidden_out.at[block], out_sem.at[at, 0]),
+            pltpu.make_async_copy(grads.at[at], grad_out.at[block], out_sem.at[at, 1]),
+            pltpu.make_async_copy(low.at[at], low_out.at[block], out_sem.at[at, 2]),
+        ]
+
+    def g_copy(block):
+        return pltpu.make_async_remote_copy(
+            src_ref=cot.at[block],
+            dst_ref=came.at[n],
+            send_sem=g_send.at[block],
+            recv_sem=g_recv.at[n],
+            device_id=to_narrow(block),
+            device_id_type=MESH,
+        )
+
+    def compute(side, d):
+        block = n - d + 2 * d * side
+        before = 1 + jnp.minimum(n, d - 1) + jnp.minimum(narrow - 1 - n, d - 1)
+        before = jnp.where(d == 0, 0, before + jnp.where((side == 1) & (n - d >= 0), 1, 0))
+        at = lax.rem(before, 2)
+
+        @pl.when(before >= 2)
+        def _():
+            for copy in out_copies(at, block):
+                copy.wait()
+
+        def first(f, carry):
+            columns = pl.ds(pl.multiple_of(f * tile, tile), tile)
+            other = pl.ds(pl.multiple_of(own + f * tile, tile), tile)
+            x = group_ref[block]
+            gate = dot(x, gate_up[:, columns], NN)
+            up = dot(x, gate_up[:, other], NN)
+            grad = dot(cot[block], down[columns, :], NT)
+            sig = 1.0 / (1.0 + jnp.exp(-gate))
+            silu = gate * sig
+            hidden[at, :, columns] = (silu * up).astype(BF16)
+            grads[at, :, columns] = (grad * up * (sig + silu * (1.0 - sig))).astype(BF16)
+            grads[at, :, other] = (grad * silu).astype(BF16)
+            return carry
+
+        lax.fori_loop(0, tiles, first, 0)
+
+        def second(f, carry):
+            columns = pl.ds(pl.multiple_of(f * tile, tile), tile)
+            cot[block, :, columns] = dot(grads[at], gate_up[columns, :], NT, BF16)
+            low[at, :, columns] = dot(hidden[at], down[:, columns], NN, BF16)
+            return carry
+
+        lax.fori_loop(0, wtiles, second, 0)
+        for copy in out_copies(at, block):
+            copy.start()
+        pl.when(block != n)(lambda: g_copy(block).start())
+
+    def distance(d, carry):
+        for side in (0, 1):
+
+            @pl.when(valid(side, d) & (d > 0))
+            def _():
+                x_wait(side, d)
+
+            @pl.when(passes(side, d))
+            def _():
+                x_copy(side, d).start()
+
+        @pl.when(d == 0)
+        def _():
+            for load in loads[:3]:
+                load.wait()
+
+        def one(side, carry):
+            ok = jnp.where(side == 0, n - d, jnp.where(d > 0, narrow - 1 - n - d, -1)) >= 0
+            pl.when(ok)(lambda: compute(side, d))
+            return carry
+
+        lax.fori_loop(0, 2, one, 0)
+        return carry
+
+    loads[3].wait()
+    lax.fori_loop(0, narrow, distance, 0)
+
+    for at in range(min(2, narrow)):
+        for copy in out_copies(at, n):
+            copy.wait()
+    for side in (0, 1):
+        for d in range(narrow - 1):
+            pl.when(passes(side, d))(lambda side=side, d=d: x_copy(side, d).wait_send())
+    for step in range(1, narrow):
+        other = lax.rem(n + step, narrow)
+        g_copy(other).wait_send()
+        block = came.at[other]
+        pltpu.make_async_copy(block, block, g_recv.at[other]).wait()
+
+    def add(r, carry):
+        part = pl.ds(pl.multiple_of(r * 16, 16), 16)
+        total = cot[n, part, :].astype(F32)
+        for step in range(1, narrow):
+            total = total + came[lax.rem(n + step, narrow), part, :].astype(F32)
+        grad_x_ref[part, :] = total
+        return carry
+
+    lax.fori_loop(0, rows // 16, add, 0)
+
+
+def feed(x, cot_group, gate_up, down):
+    narrow = lax.axis_size("narrow")
+    rows, width = x.shape
+    own = down.shape[0]
+    dma = pltpu.SemaphoreType.DMA
+    hbm = pl.BlockSpec(memory_space=pl.ANY)
+    vmem = pl.BlockSpec(memory_space=pltpu.VMEM)
+    group, hidden, grads, low, grad_x = pl.pallas_call(
+        functools.partial(feed_kernel, narrow),
+        out_shape=(
+            jax.ShapeDtypeStruct((narrow, rows, width), BF16),
+            jax.ShapeDtypeStruct((narrow, rows, own), BF16),
+            jax.ShapeDtypeStruct((narrow, rows, 2 * own), BF16),
+            jax.ShapeDtypeStruct((narrow, rows, width), BF16),
+            jax.ShapeDtypeStruct((rows, width), F32),
+        ),
+        in_specs=[vmem, hbm, hbm, hbm],
+        out_specs=(vmem, hbm, hbm, hbm, vmem),
+        scratch_shapes=[
+            pltpu.VMEM((width, 2 * own), BF16),
+            pltpu.VMEM((own, width), BF16),
+            pltpu.VMEM((narrow, rows, width), BF16),
+            pltpu.VMEM((2, rows, own), BF16),
+            pltpu.VMEM((2, rows, 2 * own), BF16),
+            pltpu.VMEM((2, rows, width), BF16),
+            pltpu.VMEM((narrow, rows, width), BF16),
+            dma((4,)),
+            dma((2, narrow + 1)),
+            dma((2, narrow + 1)),
+            dma((2, 3)),
+            dma((narrow,)),
+            dma((narrow,)),
+        ],
+        compiler_params=pltpu.CompilerParams(
+            collective_id=1, has_side_effects=True, vmem_limit_bytes=58 << 20
+        ),
+        cost_estimate=pl.CostEstimate(
+            flops=12 * narrow * rows * width * own, bytes_accessed=300 << 20, transcendentals=0
+        ),
+    )(x, cot_group.reshape(narrow, rows, width), gate_up, down)
+    flat = lambda y: y.reshape((-1,) + y.shape[2:])
+    return flat(group), flat(hidden), flat(grads), flat(low), grad_x
 
 
 def per_device(tokens, lengths, gain_attn, w_qkv, w_out, gain_mlp, w_gateup, w_down, cotangent):
@@ -322,19 +826,17 @@
 
     gains = jnp.stack([gain_attn, gain_mlp], -1)
     with_gains = jnp.concatenate([w_qkv, jnp.pad(gains, ((0, 0), (0, 126)))], -1)
-    qkv_gained = gather(with_gains, BOTH)
+    shard = w_gateup.shape[0]
+    gateup_cut = w_gateup.reshape(shard, 2, wide, narrow, -1).transpose(3, 0, 1, 2, 4)
+    qkv_gained, out_whole, gateup_rows = gather_weights(
+        with_gains, w_out, gateup_cut.reshape(narrow, shard, 2 * own_ff)
+    )
     qkv_whole = qkv_gained[:, : w_qkv.shape[1]]
     gain_one = qkv_gained[:, w_qkv.shape[1]].astype(F32)
     gain_two = qkv_gained[:, w_qkv.shape[1] + 1].astype(F32)
-    out_whole = gather(w_out, BOTH)
-    shard = w_gateup.shape[0]
-    gateup_cut = w_gateup.reshape(shard, 2, wide, narrow, -1).transpose(3, 0, 1, 2, 4)
-    gateup_own = gather(
-        exchange(gateup_cut.reshape(narrow, shard, 2 * own_ff), "narrow").reshape(-1, 2 * own_ff),
-        "wide",
-    )
+    gateup_own = gather(gateup_rows, "wide")
     down_own = gather(w_down, "wide")
-    cot_group = gather(cotangent[0], "narrow")
+    cot_group = shift_gather(cotangent[0])
 
     inputs = tokens[0].astype(F32)
     scale_one = lax.rsqrt(jnp.mean(inputs * inputs, -1, keepdims=True) + EPS)
@@ -356,14 +858,24 @@
     unit_two = middle * scale_two
     normed_two = (unit_two * gain_two).astype(BF16)
 
-    normed_group = gather(normed_two, "narrow")
-    hidden, grad_gate, grad_up = middle_part(normed_group, cot_group, gateup_own, down_own)
-    grad_gate_up = jnp.concatenate([grad_gate, grad_up], -1)
-    grad_normed_two = scatter_sum(dot(grad_gate_up, gateup_own, NT, BF16), "narrow").astype(F32)
-    layer_out = (middle + scatter_sum(dot(hidden, down_own, NN, BF16), "narrow")).astype(BF16)[None]
+    normed_group, hidden, grad_gate_up, low_part, grad_normed_two = feed(
+        normed_two, cot_group, gateup_own, down_own
+    )
+    layer_out = (middle + scatter_sum(low_part, "narrow")).astype(BF16)[None]
+    chips = wide // 2
+
+    def of_core(left, right, dims, core):
+        free = 1 - dims[0][0][0]
+        size = left.shape[free] // wide
+        cuts = [lax.slice_in_dim(left, w * size, (w + 1) * size, axis=free) for w in range(wide)]
+        part = jnp.concatenate(
+            [jnp.where(core == 0, cuts[w], cuts[w + 1]) for w in range(0, wide, 2)], free
+        )
+        return dot(part, right, dims, BF16).reshape(chips, size, -1)
+
+    grad_gateup = scatter_sum(dot(normed_group, grad_gate_up, TN, BF16), "wide")
+    grad_gateup = shift_exchange(grad_gateup.reshape(narrow, shard, 2 * own_ff))
     grad_down = scatter_sum(dot(hidden, cot_group, TN, BF16), "wide").astype(F32)
-    grad_gateup = scatter_sum(dot(normed_group, grad_gate_up, TN, BF16), "wide")
-    grad_gateup = exchange(grad_gateup.reshape(narrow, shard, 2 * own_ff), "narrow")
     grad_gateup = (
         grad_gateup.reshape(narrow, shard, 2, wide, -1)
         .transpose(1, 2, 3, 0, 4)
@@ -376,7 +888,9 @@
         grad_normed_two * gain_two, unit_two, scale_two
     )
     grad_branch = grad_middle.astype(BF16)
-    grad_wout = scatter_sum(dot(attended_low, grad_branch, NN, BF16), BOTH).astype(F32)
+    grad_wout = shift_scatter_sum(
+        wide_scatter_sum(lambda core: of_core(attended_low, grad_branch, NN, core))
+    )
     grad_attended = dot(out_whole, grad_branch, NT, BF16).reshape(wide, groups * HEAD_DIM, rows)
     grad_heads = attend_back(
         heads, exchange(grad_attended, "wide"), attended_full, log_total, start, cos_all, sin_all,
@@ -401,19 +915,22 @@
     )
     grad_normed_one = dot(grad_projected, qkv_whole, (((0,), (1,)), ((), ())))
     part_gain_one = jnp.sum(grad_normed_one * unit_one, 0)
-    part_gains = jnp.stack([part_gain_one, part_gain_two], -1)
-    part_qkv = dot(normed_one, grad_projected, (((0,), (1,)), ((), ())), BF16)
-    grad_qkv = scatter_sum(part_qkv, BOTH).astype(F32)
-    grad_gains = scatter_sum(part_gains, BOTH)
+    part_gains = jnp.stack([part_gain_one, part_gain_two], 0).reshape(2, wide, narrow, shard)
+    part_gains = jnp.sum(exchange(part_gains.transpose(1, 2, 0, 3), "wide"), 0)
+    grad_gains = jnp.sum(exchange(part_gains, "narrow"), 0)
+    back_dims = (((0,), (1,)), ((), ()))
+    grad_qkv = shift_scatter_sum(
+        wide_scatter_sum(lambda core: of_core(normed_one, grad_projected, back_dims, core))
+    )
     grad_inputs = grad_middle + norm_back(grad_normed_one * gain_one, unit_one, scale_one)
     grad_tokens = grad_inputs.astype(BF16)[None]
     return (
         layer_out,
         grad_tokens,
-        grad_gains[:, 0],
+        grad_gains[0],
         grad_qkv,
         grad_wout,
-        grad_gains[:, 1],
+        grad_gains[1],
         grad_gateup,
         grad_down,
     )

time: 1490 us -> 918 us (0.62)
  waiting for transfers between devices: 1000 us -> 265 us
  Pallas kernels: 130 us -> 378 us
  blocking collectives: 133 us -> 0 us
  starting transfers between devices: 13.9 us -> 56.9 us
  matrix products: 118 us -> 88.3 us
  other arithmetic: 24.8 us -> 47.8 us
  local copies, waits for them, and re-layouts: 42.7 us -> 58.5 us
    reduce_scatter x6 -> x3, waiting for transfers between devices: 529 us -> 42.3 us  [scatter_sum(): return lax.psum_scatter(x, axis, scatter_dimension=0, tiled=True)]
    all_gather x6 -> x2, waiting for transfers between devices: 322 us -> 0.01 us  [gather(): return lax.all_gather(x, axis, axis=0, tiled=True)]
    pallas_call x1 -> x2, Pallas kernels: 37.9 us -> 284 us  [the longest x1 147 us: feed(): pl.pallas_call(functools.partial(feed_kernel, narrow), out_shape=(jax.Sha...]
    ppermute x0 -> x22, waiting for transfers between devices: none -> 167 us  [the longest x12 87.8 us: shift(): return lax.ppermute(x, 'narrow', [(i, (i + step) % n) for i in range(n)])]
    all_to_all x3 -> x0, blocking collectives: 133 us -> none  [exchange(): return lax.all_to_all(x, axis, split_axis=0, concat_axis=0, tiled=True)]
    unnamed x14 -> x5, waiting for transfers between devices: 121 us -> 0.75 us
    ppermute x0 -> x22, starting transfers between devices: none -> 31.7 us  [the longest x12 21.7 us: shift(): return lax.ppermute(x, 'narrow', [(i, (i + step) % n) for i in range(n)])]
    dot_general x10, matrix products: 118 us -> 88.3 us  [dot(): lax.dot_general(left, right, dims, preferred_element_type=F32).astype(kind)]
  transfers between devices with their start and end apart: 16 -> 33, of which waited for: 13 -> 17; matrix products, arithmetic and copies ran while one was open for 9% -> 19% of each run, Pallas kernels for 6% -> 25%
where the time goes in v2:
time: 918 us; the launch traced here: 909 us
  Pallas kernels  378 us (41%)
  waiting for transfers between devices  265 us (29%)
  matrix products  88.3 us (10%)
  local copies, waits for them, and re-layouts  58.5 us (6%)
  starting transfers between devices  56.9 us (6%)
  other arithmetic  47.8 us (5%)
  between operations  15.1 us (2%)
    pallas_call x1, Pallas kernels, feed(): pl.pallas_call(functools.partial(feed_kernel, narrow), out_shape=(jax.Sha...  147 us
    pallas_call x1, Pallas kernels, gather_weights(): pl.pallas_call(functools.partial(gather_kernel, wide, narrow, 3), out_sha...  138 us
    dot_general x10, matrix products, dot(): lax.dot_general(left, right, dims, preferred_element_type=F32).astype(kind)  88.3 us
    ppermute x12, waiting for transfers between devices, shift(): return lax.ppermute(x, 'narrow', [(i, (i + step) % n) for i in range(n)])  87.8 us
    ppermute x10, waiting for transfers between devices, across(): lax.ppermute(x, 'wide', [(i, i ^ mask) for i in range(lax.axis_size('wide...  78.9 us
    all_to_all x6, waiting for transfers between devices, exchange(): return lax.all_to_all(x, axis, split_axis=0, concat_axis=0, tiled=True)  55.1 us
    pallas_call x1, Pallas kernels, attend_back(): pl.pallas_call(functools.partial(attend_back_kernel, groups), grid=(block...  49.2 us
    pallas_call x1, Pallas kernels, attend(): pl.pallas_call(functools.partial(attend_kernel, groups), grid=(blocks,),...  44.3 us
  transfers between devices with their start and end apart: 33, of which 17 were waited for; matrix products, arithmetic and copies ran while one was open for 19% of the time, Pallas kernels for 25%

profile of v2, /device:TPU:0, one launch (start us, length us, event | category | flops | bytes accessed | tf_op | source)
XLA Modules:
  0.0 909.2 jit_solution(8456800025474285041)
XLA Ops:
  7.9 4.5 reshape.252
  17.6 137.7 %shard_map.152 = (bf16[2048,3200]{1,0:T(8,128)(2,1)}, bf16[2048,2048]{1,0:T(8,128)(2,1)}, bf16[256,4096]{1,0:T(8,128)(2,1)}) custom-call(bf16[64,3200]{1,0:T(8,128)(2,1)} %fusion.65.qkv_ref, bf16[64,2048]{1,0:T(8,128)(2,1)} %out_w_ref.1, bf16[4,64,4096]{2,1,0:T(8,128)(2,1)} %reshape.253.cut_ref), custom_call_target="tpu_custom_call" | custom-call | bytes 314572800 | tf_op jit(solution)/shard_map/pallas_call | solution.py:576
  158.1 6.9 fusion.3
  173.7 3.6 all-to-all-start
  177.3 7.0 collective-permute-start.1
  185.9 2.5 broadcast_in_dim.70
  193.1 16.3 %all-to-all-done.x_ref = bf16[8,384,256]{2,1,0:T(8,128)(2,1)S(1)} async-done(((bf16[8,384,256]{2,1,0:T(8,128)(2,1)}), bf16[8,384,256]{2,1,0:T(8,128)(2,1)S(1)}, u32[]{:S(2)}, u32[]{:S(2)}) %all-to-all-start) | async-done | bytes 1572896 | tf_op jit(solution)/shard_map/all_to_all | solution.py:258
  209.4 44.3 %shard_map.153 = (bf16[8,256,256]{2,1,0:T(8,128)(2,1)}, f32[8,256,256]{2,1,0:T(8,128)S(1)}, f32[8,4,256]{2,1,0:T(4,128)S(1)}) custom-call(s32[8,1,256]{2,1,0:T(1,128)S(1)} %bitcast.175, bf16[8,384,256]{2,1,0:T(8,128)(2,1)S(1)} %all-to-all-done.x_ref), custom_call_target="tpu_custom_call" | custom-call | flops 17179869184 | bytes 3145728 | tf_op jit(solution)/shard_map/pallas_call | solution.py:110
  255.0 4.3 all-to-all-start.1
  261.9 2.4 bitcast_dynamic-update-slice_fusion.cot_ref
  264.3 10.4 %all-to-all-done.1 = bf16[8,256,256]{2,1,0:T(8,128)(2,1)} async-done(((bf16[8,256,256]{2,1,0:T(8,128)(2,1)}), bf16[8,256,256]{2,1,0:T(8,128)(2,1)}, u32[]{:S(2)}, u32[]{:S(2)}) %all-to-all-start.1) | async-done | bytes 1048608 | tf_op jit(solution)/shard_map/all_to_all | solution.py:258
  274.7 6.2 multiply_reduce_fusion.2
  283.4 146.6 %shard_map.154 = (bf16[4,256,2048]{2,1,0:T(8,128)(2,1)}, bf16[4,256,2048]{2,1,0:T(8,128)(2,1)}, bf16[4,256,4096]{2,1,0:T(8,128)(2,1)}, bf16[4,256,2048]{2,1,0:T(8,128)(2,1)}, f32[256,2048]{1,0:T(8,128)}) custom-call(bf16[256,2048]{1,0:T(8,128)(2,1)} %multiply_convert_fusion.x_ref, bf16[4,256,2048]{2,1,0:T(8,128)(2,1)} %bitcast_dynamic-update-slice_fusion.cot_ref, ...), custom_call_target="tpu_custom_call" | custom-call | flops 51539607552 | bytes 314572800 | tf_op jit(solution)/shard_map/pallas_call | solution.py:773
  430.1 14.1 %bitcast_convert_fusion.1 = bf16[2048,2048]{1,0:T(8,128)(2,1)} fusion(bf16[4,256,2048]{2,1,0:T(8,128)(2,1)} %get-tuple-element.29, bf16[4,256,2048]{2,1,0:T(8,128)(2,1)} %bitcast_dynamic-update-slice_fusion.cot_ref), kind=kOutput, calls=%fused_computation.1 | convolution fusion | flops 8594128896 | bytes 16777216 | tf_op jit(solution)/shard_map/dot_general | solution.py:28
  444.4 25.3 %bitcast_convert_fusion = bf16[2048,4096]{1,0:T(8,128)(2,1)} fusion(bf16[4,256,2048]{2,1,0:T(8,128)(2,1)} %get-tuple-element.27, bf16[4,256,4096]{2,1,0:T(8,128)(2,1)} %get-tuple-element.28), kind=kOutput, calls=%fused_computation | convolution fusion | flops 17188257792 | bytes 29360128 | tf_op jit(solution)/shard_map/dot_general | solution.py:28
  469.8 2.8 multiply_reduce_fusion
  472.6 42.3 %reduce-scatter.4.cloned.1.call-done = bf16[256,2048]{1,0:T(8,128)(2,1)} async-done(((bf16[1024,2048]{1,0:T(8,128)(2,1)}), bf16[256,2048]{1,0:T(8,128)(2,1)}) %reduce-scatter.4.cloned.1.call-update) | async-done | bytes 1048592 | tf_op jit(solution)/shard_map/reduce_scatter | solution.py:254
  514.9 4.5 multiply_add_fusion
  519.4 7.5 convolution_convert_fusion.4
  527.0 3.8 all-to-all-start.2
  531.8 14.4 %all-to-all-done.2.grad_ref = bf16[8,256,256]{2,1,0:T(8,128)(2,1)S(1)} async-done(((bf16[8,256,256]{2,1,0:T(8,128)(2,1)}), bf16[8,256,256]{2,1,0:T(8,128)(2,1)S(1)}, u32[]{:S(2)}, u32[]{:S(2)}) %all-to-all-start.2) | async-done | bytes 1048608 | tf_op jit(solution)/shard_map/all_to_all | solution.py:258
  547.7 49.2 %shard_map.155 = bf16[8,384,256]{2,1,0:T(8,128)(2,1)} custom-call(s32[8,1,256]{2,1,0:T(1,128)S(1)} %bitcast.176, bf16[8,384,256]{2,1,0:T(8,128)(2,1)S(1)} %all-to-all-done.x_ref, bf16[8,256,256]{2,1,0:T(8,128)(2,1)S(1)} %all-to-all-done.2.grad_ref, f32[8,256,256]{2,1,0:T(8,128)S(1)} %copy-done.1, f32[8,4,256]{2,1,0:T(4,128)S(1)} %get-tuple-element.26.log_ref, ...), custom_call_target="tpu_custom_call" | custom-call | flops 42949672960 | bytes 6291456 | tf_op jit(solution)/shard_map/pallas_call | solution.py:219
  596.9 4.6 all-to-all-start.3
  603.9 3.5 convolution_convert_fusion.2
  608.6 14.0 %all-to-all-done.3 = bf16[8,384,256]{2,1,0:T(8,128)(2,1)} async-done(((bf16[8,384,256]{2,1,0:T(8,128)(2,1)}), bf16[8,384,256]{2,1,0:T(8,128)(2,1)}, u32[]{:S(2)}, u32[]{:S(2)}) %all-to-all-start.3) | async-done | bytes 1572896 | tf_op jit(solution)/shard_map/all_to_all | solution.py:258
  625.3 4.5 convolution_convert_fusion
  630.7 4.4 convolution_convert_fusion.3
  635.1 9.7 %fusion.21 = (f32[2048]{0:T(1024)S(1)}, f32[256]{0:T(256)S(1)}, f32[256,2048]{1,0:T(8,128)}) fusion(bf16[1,256,2048]{2,1,0:T(8,128)(2,1)S(1)} %copy-done.6, f32[256]{0:T(256)S(1)} %copy-done.31, f32[2048]{0:T(1024)S(1)} %copy-done.28, bf16[2048,3200]{1,0:T(8,128)(2,1)} %get-tuple-element.19, bf16[512,256]{1,0:T(8,128)(2,1)S(1)} %bitcast.204, ...), kind=kOutput, calls=%fused_computation.37 | convolution fusion | flops 3229611776 | bytes 17319936 | tf_op jit(solution)/shard_map/dot_general | solution.py:28
  645.7 4.2 all-to-all-start.4
  649.9 5.7 fusion.5
  666.1 4.1 all-to-all-start.5
  670.2 6.2 convolution_convert_fusion.1
  680.2 2.8 convert_element_type.336
  683.0 21.0 %collective-permute-done.12 = bf16[2,256,1024]{2,1,0:T(8,128)(2,1)} collective-permute-done((bf16[2,256,1024]{2,1,0:T(8,128)(2,1)}, bf16[2,256,1024]{2,1,0:T(8,128)(2,1)}, u32[]{:S(2)}, u32[]{:S(2)}) %collective-permute-start.12) | collective-permute-done | bytes 1048608 | tf_op jit(solution)/shard_map/ppermute | solution.py:262
  708.0 7.4 fusion
  721.1 11.5 %collective-permute-done.13 = bf16[256,1024]{1,0:T(8,128)(2,1)} collective-permute-done((bf16[256,1024]{1,0:T(8,128)(2,1)}, bf16[256,1024]{1,0:T(8,128)(2,1)}, u32[]{:S(2)}, u32[]{:S(2)}) %collective-permute-start.13) | collective-permute-done | bytes 524320 | tf_op jit(solution)/shard_map/ppermute | solution.py:262
  733.8 42.4 %collective-permute-done.15 = bf16[256,1024]{1,0:T(8,128)(2,1)S(1)} collective-permute-done((bf16[256,1024]{1,0:T(8,128)(2,1)S(1)}, bf16[256,1024]{1,0:T(8,128)(2,1)S(1)}, u32[]{:S(2)}, u32[]{:S(2)}) %collective-permute-start.15) | collective-permute-done | bytes 524320 | tf_op jit(solution)/shard_map/ppermute | solution.py:262
  785.3 2.5 collective-permute-done.16
  787.8 9.9 %collective-permute-done.17 = bf16[64,2048]{1,0:T(8,128)(2,1)S(1)} collective-permute-done((bf16[64,2048]{1,0:T(8,128)(2,1)S(1)}, bf16[64,2048]{1,0:T(8,128)(2,1)S(1)}, u32[]{:S(2)}, u32[]{:S(2)}) %collective-permute-start.17) | collective-permute-done | bytes 262176 | tf_op jit(solution)/shard_map/ppermute | solution.py:267
  804.2 2.9 collective-permute-start.10
  809.5 3.9 collective-permute-start.19
  813.3 3.7 collective-permute-done.10
  817.0 8.9 collective-permute-done.8
  825.9 38.8 %collective-permute-done.9 = bf16[64,3072]{1,0:T(8,128)(2,1)S(1)} collective-permute-done((bf16[64,3072]{1,0:T(8,128)(2,1)S(1)}, bf16[64,3072]{1,0:T(8,128)(2,1)S(1)}, u32[]{:S(2)}, u32[]{:S(2)}) %collective-permute-start.9) | collective-permute-done | bytes 393248 | tf_op jit(solution)/shard_map/ppermute | solution.py:267
  865.7 15.7 %collective-permute-done.20 = bf16[64,4096]{1,0:T(8,128)(2,1)S(1)} collective-permute-done((bf16[64,4096]{1,0:T(8,128)(2,1)S(1)}, bf16[64,4096]{1,0:T(8,128)(2,1)S(1)}, u32[]{:S(2)}, u32[]{:S(2)}) %collective-permute-start.20) | collective-permute-done | bytes 524320 | tf_op jit(solution)/shard_map/ppermute | solution.py:267
  881.5 8.4 collective-permute-done.21
  890.6 5.9 copy.53
  896.5 5.8 reshape.285
  (204 shorter events, 85.5 us)
Async XLA Ops:
  7.2 276.2 %all-gather.5.cloned.1.call-start = ((), (), s32[]{:S(2)}) async-start(), calls=%async_computation.10 | async-start | bytes 9437184 | tf_op jit(solution)/shard_map/all_gather | solution.py:250
  7.9 275.5 %all-gather.3.cloned.1.call-start = ((), (), s32[]{:S(2)}) async-start(), calls=%async_computation.9 | async-start | bytes 18874368 | tf_op jit(solution)/shard_map/all_gather | solution.py:250
  17.6 137.8 %copy-start.36 = (s32[1,4]{1,0:T(1,128)S(1)}, s32[1,4]{1,0:T(1,128)}, u32[]{:S(2)}) copy-start(s32[1,4]{1,0:T(1,128)} %param.10) | copy-start | bytes 52
  155.3 35.4 %collective-permute-start = (bf16[256,2048]{1,0:T(8,128)(2,1)}, bf16[256,2048]{1,0:T(8,128)(2,1)}, u32[]{:S(2)}, u32[]{:S(2)}) collective-permute-start(bf16[256,2048]{1,0:T(8,128)(2,1)} %bitcast.15), channel_id=1, source_target_pairs={{0,1},{1,2},{2,3},{3,0},{4,5},{5,6},{6,7},{7,4},{8,9},{9,10},{10,1... | collective-permute-start | bytes 3145736 | tf_op jit(solution)/shard_map/ppermute | solution.py:267
  157.4 7.6 copy-start.27
  157.7 7.3 copy-start.30
  158.1 7.0 copy-start.13
  173.7 35.7 %all-to-all-start = ((bf16[8,384,256]{2,1,0:T(8,128)(2,1)}), bf16[8,384,256]{2,1,0:T(8,128)(2,1)S(1)}, u32[]{:S(2)}, u32[]{:S(2)}) async-start(bf16[8,384,256]{2,1,0:T(8,128)(2,1)} %pad_maximum_fusion), calls=%async_computation | async-start | bytes 3145728 | tf_op jit(solution)/shard_map/all_to_all | solution.py:258
  177.3 82.3 %collective-permute-start.1 = (bf16[256,2048]{1,0:T(8,128)(2,1)}, bf16[256,2048]{1,0:T(8,128)(2,1)}, u32[]{:S(2)}, u32[]{:S(2)}) collective-permute-start(bf16[256,2048]{1,0:T(8,128)(2,1)} %bitcast.15), channel_id=1, source_target_pairs={{0,2},{1,3},{2,0},{3,1},{4,6},{5,7},{6,4},{7,5},{8,10},{9,11},{10,... | collective-permute-start | bytes 3145736 | tf_op jit(solution)/shard_map/ppermute | solution.py:267
  184.3 77.6 %collective-permute-start.2 = (bf16[256,2048]{1,0:T(8,128)(2,1)}, bf16[256,2048]{1,0:T(8,128)(2,1)}, u32[]{:S(2)}, u32[]{:S(2)}) collective-permute-start(bf16[256,2048]{1,0:T(8,128)(2,1)} %bitcast.15), channel_id=1, source_target_pairs={{0,3},{1,0},{2,1},{3,2},{4,7},{5,4},{6,5},{7,6},{8,11},{9,8},{10,9... | collective-permute-start | bytes 3145736 | tf_op jit(solution)/shard_map/ppermute | solution.py:267
  255.0 19.7 %all-to-all-start.1 = ((bf16[8,256,256]{2,1,0:T(8,128)(2,1)}), bf16[8,256,256]{2,1,0:T(8,128)(2,1)}, u32[]{:S(2)}, u32[]{:S(2)}) async-start(bf16[8,256,256]{2,1,0:T(8,128)(2,1)} %get-tuple-element.20), calls=%async_computation.1 | async-start | bytes 2097152 | tf_op jit(solution)/shard_map/all_to_all | solution.py:258
  259.3 255.6 %reduce-scatter.4.cloned.1.call-start = ((), (), s32[]{:S(2)}) async-start(), calls=%async_computation.11 | async-start | bytes 5242880 | tf_op jit(solution)/shard_map/reduce_scatter | solution.py:254
  430.0 250.1 %reduce-scatter.8.cloned.1.call-start = ((), (), s32[]{:S(2)}) async-start(), calls=%async_computation.13 | async-start | bytes 9437184 | tf_op jit(solution)/shard_map/reduce_scatter | solution.py:254
  444.1 363.5 %reduce-scatter.6.cloned.1.call-start = ((), (), s32[]{:S(2)}) async-start(), calls=%async_computation.12 | async-start | bytes 18874368 | tf_op jit(solution)/shard_map/reduce_scatter | solution.py:254
  519.4 7.5 copy-start.2
  527.0 19.2 %all-to-all-start.2 = ((bf16[8,256,256]{2,1,0:T(8,128)(2,1)}), bf16[8,256,256]{2,1,0:T(8,128)(2,1)S(1)}, u32[]{:S(2)}, u32[]{:S(2)}) async-start(bf16[8,256,256]{2,1,0:T(8,128)(2,1)} %bitcast.197), calls=%async_computation.3 | async-start | bytes 2097152 | tf_op jit(solution)/shard_map/all_to_all | solution.py:258
  596.9 7.0 copy-start.3
  596.9 25.7 %all-to-all-start.3 = ((bf16[8,384,256]{2,1,0:T(8,128)(2,1)}), bf16[8,384,256]{2,1,0:T(8,128)(2,1)}, u32[]{:S(2)}, u32[]{:S(2)}) async-start(bf16[8,384,256]{2,1,0:T(8,128)(2,1)} %shard_map.155), calls=%async_computation.4 | async-start | bytes 3145728 | tf_op jit(solution)/shard_map/all_to_all | solution.py:258
  607.4 42.4 %collective-permute-start.11 = (bf16[4,256,2048]{2,1,0:T(8,128)(2,1)}, bf16[4,256,2048]{2,1,0:T(8,128)(2,1)}, u32[]{:S(2)}, u32[]{:S(2)}) collective-permute-start(bf16[4,256,2048]{2,1,0:T(8,128)(2,1)} %bitcast.54), channel_id=1, source_target_pairs={{0,4},{4,0},{8,12},{12,8},{16,20},{20,16},{24,28},{28,24},{1,5},{5... | collective-permute-start | bytes 12582920 | tf_op jit(solution)/shard_map/ppermute | solution.py:262
  625.2 4.6 copy-start.18
  625.3 4.5 copy-start.21
  625.3 4.5 copy-start.24
  629.8 78.2 %collective-permute-start.3 = (bf16[4,256,3072]{2,1,0:T(8,128)(2,1)}, bf16[4,256,3072]{2,1,0:T(8,128)(2,1)}, u32[]{:S(2)}, u32[]{:S(2)}) collective-permute-start(bf16[4,256,3072]{2,1,0:T(8,128)(2,1)} %bitcast.30), channel_id=1, source_target_pairs={{0,4},{4,0},{8,12},{12,8},{16,20},{20,16},{24,28},{28,24},{1,5},{5... | collective-permute-start | bytes 18874376 | tf_op jit(solution)/shard_map/ppermute | solution.py:262
  635.1 9.8 %copy-start.29 = (f32[1,8,4,64]{3,2,0,1:T(4,128)S(1)}, f32[1,8,4,64]{3,2,0,1:T(4,128)}, u32[]{:S(2)}) copy-start(f32[1,8,4,64]{3,2,0,1:T(4,128)} %stack.28) | copy-start | bytes 24580
  645.7 17.7 %all-to-all-start.4 = ((f32[8,1,512]{2,1,0:T(1,128)}), f32[8,1,512]{2,1,0:T(1,128)}, u32[]{:S(2)}, u32[]{:S(2)}) async-start(f32[8,1,512]{2,1,0:T(1,128)} %reshape.291), calls=%async_computation.5 | async-start | bytes 32768 | tf_op jit(solution)/shard_map/all_to_all | solution.py:258
  659.8 44.2 %collective-permute-start.12 = (bf16[2,256,1024]{2,1,0:T(8,128)(2,1)}, bf16[2,256,1024]{2,1,0:T(8,128)(2,1)}, u32[]{:S(2)}, u32[]{:S(2)}) collective-permute-start(bf16[2,256,1024]{2,1,0:T(8,128)(2,1)} %dynamic-slice_bitcast_fusion.3), channel_id=1, source_target_pairs={{0,8},{4,12},{8,0},{12,4},{16,24},{20,28},{24,16},{28,20},{1,9},{5... | collective-permute-start | bytes 3145736 | tf_op jit(solution)/shard_map/ppermute | solution.py:262
  661.7 8.5 copy-start.23
  661.7 8.5 copy-start.26
  666.1 10.3 %all-to-all-start.5 = ((f32[4,1,128]{2,1,0:T(1,128)}), f32[4,1,128]{2,1,0:T(1,128)S(1)}, u32[]{:S(2)}, u32[]{:S(2)}) async-start(f32[4,1,128]{2,1,0:T(1,128)} %reshape.293), calls=%async_computation.6 | async-start | bytes 4096 | tf_op jit(solution)/shard_map/all_to_all | solution.py:258
  670.2 7.5 copy-start.7
  678.7 25.3 %copy-start.10 = (bf16[2,2,256,1024]{3,2,1,0:T(8,128)(2,1)S(1)}, bf16[2,2,256,1024]{3,2,1,0:T(8,128)(2,1)}, u32[]{:S(2)}) copy-start(bf16[2,2,256,1024]{3,2,1,0:T(8,128)(2,1)} %copy-done.9) | copy-start | bytes 6291460
  678.7 38.2 %collective-permute-start.14 = (bf16[2,256,1024]{2,1,0:T(8,128)(2,1)}, bf16[2,256,1024]{2,1,0:T(8,128)(2,1)}, u32[]{:S(2)}, u32[]{:S(2)}) collective-permute-start(bf16[2,256,1024]{2,1,0:T(8,128)(2,1)} %dynamic-slice_bitcast_fusion.2), channel_id=1, source_target_pairs={{0,16},{4,20},{8,24},{12,28},{16,0},{20,4},{24,8},{28,12},{1,17},{... | collective-permute-start | bytes 3145736 | tf_op jit(solution)/shard_map/ppermute | solution.py:262
  706.5 26.1 %collective-permute-start.13 = (bf16[256,1024]{1,0:T(8,128)(2,1)}, bf16[256,1024]{1,0:T(8,128)(2,1)}, u32[]{:S(2)}, u32[]{:S(2)}) collective-permute-start(bf16[256,1024]{1,0:T(8,128)(2,1)} %dynamic-slice_bitcast_fusion.10), channel_id=1, source_target_pairs={{0,16},{4,20},{8,24},{12,28},{16,0},{20,4},{24,8},{28,12},{1,17},{... | collective-permute-start | bytes 1572872 | tf_op jit(solution)/shard_map/ppermute | solution.py:262
  716.1 66.1 %collective-permute-start.4 = (bf16[2,256,1536]{2,1,0:T(8,128)(2,1)S(1)}, bf16[2,256,1536]{2,1,0:T(8,128)(2,1)S(1)}, u32[]{:S(2)}, u32[]{:S(2)}) collective-permute-start(bf16[2,256,1536]{2,1,0:T(8,128)(2,1)S(1)} %dynamic-slice_bitcast_fusion.1), channel_id=1, source_target_pairs={{0,8},{4,12},{8,0},{12,4},{16,24},{20,28},{24,16},{28,20},{1,9},{5... | collective-permute-start | bytes 4718600 | tf_op jit(solution)/shard_map/ppermute | solution.py:262
  719.2 13.4 %copy-start.12 = (bf16[2,256,1024]{2,1,0:T(8,128)(2,1)S(1)}, bf16[2,256,1024]{2,1,0:T(8,128)(2,1)}, u32[]{:S(2)}) copy-start(bf16[2,256,1024]{2,1,0:T(8,128)(2,1)} %copy-done.11) | copy-start | bytes 3145732
  719.3 56.9 %collective-permute-start.15 = (bf16[256,1024]{1,0:T(8,128)(2,1)S(1)}, bf16[256,1024]{1,0:T(8,128)(2,1)S(1)}, u32[]{:S(2)}, u32[]{:S(2)}) collective-permute-start(bf16[256,1024]{1,0:T(8,128)(2,1)S(1)} %dynamic-slice_bitcast_fusion.9), channel_id=1, source_target_pairs={{0,8},{4,12},{8,0},{12,4},{16,24},{20,28},{24,16},{28,20},{1,9},{5... | collective-permute-start | bytes 1572872 | tf_op jit(solution)/shard_map/ppermute | solution.py:262
  720.3 63.9 %collective-permute-start.6 = (bf16[2,256,1536]{2,1,0:T(8,128)(2,1)S(1)}, bf16[2,256,1536]{2,1,0:T(8,128)(2,1)S(1)}, u32[]{:S(2)}, u32[]{:S(2)}) collective-permute-start(bf16[2,256,1536]{2,1,0:T(8,128)(2,1)S(1)} %dynamic-slice_bitcast_fusion), channel_id=1, source_target_pairs={{0,16},{4,20},{8,24},{12,28},{16,0},{20,4},{24,8},{28,12},{1,17},{... | collective-permute-start | bytes 4718600 | tf_op jit(solution)/shard_map/ppermute | solution.py:262
  776.6 11.2 %collective-permute-start.16 = (bf16[64,2048]{1,0:T(8,128)(2,1)S(1)}, bf16[64,2048]{1,0:T(8,128)(2,1)S(1)}, u32[]{:S(2)}, u32[]{:S(2)}) collective-permute-start(bf16[64,2048]{1,0:T(8,128)(2,1)S(1)} %get-tuple-element.51), channel_id=1, source_target_pairs={{0,1},{1,2},{2,3},{3,0},{4,5},{5,6},{6,7},{7,4},{8,9},{9,10},{10,1... | collective-permute-start | bytes 786440 | tf_op jit(solution)/shard_map/ppermute | solution.py:267
  778.1 19.5 %collective-permute-start.17 = (bf16[64,2048]{1,0:T(8,128)(2,1)S(1)}, bf16[64,2048]{1,0:T(8,128)(2,1)S(1)}, u32[]{:S(2)}, u32[]{:S(2)}) collective-permute-start(bf16[64,2048]{1,0:T(8,128)(2,1)S(1)} %get-tuple-element.53), channel_id=1, source_target_pairs={{0,2},{1,3},{2,0},{3,1},{4,6},{5,7},{6,4},{7,5},{8,10},{9,11},{10,... | collective-permute-start | bytes 786440 | tf_op jit(solution)/shard_map/ppermute | solution.py:267
  780.5 17.1 %collective-permute-start.18 = (bf16[64,2048]{1,0:T(8,128)(2,1)S(1)}, bf16[64,2048]{1,0:T(8,128)(2,1)S(1)}, u32[]{:S(2)}, u32[]{:S(2)}) collective-permute-start(bf16[64,2048]{1,0:T(8,128)(2,1)S(1)} %get-tuple-element.52), channel_id=1, source_target_pairs={{0,3},{1,0},{2,1},{3,2},{4,7},{5,4},{6,5},{7,6},{8,11},{9,8},{10,9... | collective-permute-start | bytes 786440 | tf_op jit(solution)/shard_map/ppermute | solution.py:267
  782.7 18.3 %collective-permute-start.5 = (bf16[256,1536]{1,0:T(8,128)(2,1)S(1)}, bf16[256,1536]{1,0:T(8,128)(2,1)S(1)}, u32[]{:S(2)}, u32[]{:S(2)}) collective-permute-start(bf16[256,1536]{1,0:T(8,128)(2,1)S(1)} %dynamic-slice_bitcast_fusion.5), channel_id=1, source_target_pairs={{0,16},{4,20},{8,24},{12,28},{16,0},{20,4},{24,8},{28,12},{1,17},{... | collective-permute-start | bytes 2359304 | tf_op jit(solution)/shard_map/ppermute | solution.py:262
  784.7 18.2 %collective-permute-start.7 = (bf16[256,1536]{1,0:T(8,128)(2,1)S(1)}, bf16[256,1536]{1,0:T(8,128)(2,1)S(1)}, u32[]{:S(2)}, u32[]{:S(2)}) collective-permute-start(bf16[256,1536]{1,0:T(8,128)(2,1)S(1)} %dynamic-slice_bitcast_fusion.4), channel_id=1, source_target_pairs={{0,8},{4,12},{8,0},{12,4},{16,24},{20,28},{24,16},{28,20},{1,9},{5... | collective-permute-start | bytes 2359304 | tf_op jit(solution)/shard_map/ppermute | solution.py:262
  804.2 12.8 %collective-permute-start.10 = (bf16[64,3072]{1,0:T(8,128)(2,1)}, bf16[64,3072]{1,0:T(8,128)(2,1)S(1)}, u32[]{:S(2)}, u32[]{:S(2)}) collective-permute-start(bf16[64,3072]{1,0:T(8,128)(2,1)} %get-tuple-element.49), channel_id=1, source_target_pairs={{0,3},{1,0},{2,1},{3,2},{4,7},{5,4},{6,5},{7,6},{8,11},{9,8},{10,9... | collective-permute-start | bytes 1179656 | tf_op jit(solution)/shard_map/ppermute | solution.py:267
  807.1 18.8 %collective-permute-start.8 = (bf16[64,3072]{1,0:T(8,128)(2,1)S(1)}, bf16[64,3072]{1,0:T(8,128)(2,1)S(1)}, u32[]{:S(2)}, u32[]{:S(2)}) collective-permute-start(bf16[64,3072]{1,0:T(8,128)(2,1)S(1)} %get-tuple-element.48), channel_id=1, source_target_pairs={{0,1},{1,2},{2,3},{3,0},{4,5},{5,6},{6,7},{7,4},{8,9},{9,10},{10,1... | collective-permute-start | bytes 1179656 | tf_op jit(solution)/shard_map/ppermute | solution.py:267
  807.1 57.5 %collective-permute-start.9 = (bf16[64,3072]{1,0:T(8,128)(2,1)S(1)}, bf16[64,3072]{1,0:T(8,128)(2,1)S(1)}, u32[]{:S(2)}, u32[]{:S(2)}) collective-permute-start(bf16[64,3072]{1,0:T(8,128)(2,1)S(1)} %get-tuple-element.50), channel_id=1, source_target_pairs={{0,2},{1,3},{2,0},{3,1},{4,6},{5,7},{6,4},{7,5},{8,10},{9,11},{10,... | collective-permute-start | bytes 1179656 | tf_op jit(solution)/shard_map/ppermute | solution.py:267
  809.5 56.2 %collective-permute-start.19 = (bf16[64,4096]{1,0:T(8,128)(2,1)S(1)}, bf16[64,4096]{1,0:T(8,128)(2,1)S(1)}, u32[]{:S(2)}, u32[]{:S(2)}) collective-permute-start(bf16[64,4096]{1,0:T(8,128)(2,1)S(1)} %get-tuple-element.44), channel_id=1, source_target_pairs={{0,1},{1,2},{2,3},{3,0},{4,5},{5,6},{6,7},{7,4},{8,9},{9,10},{10,1... | collective-permute-start | bytes 1572872 | tf_op jit(solution)/shard_map/ppermute | solution.py:267
  865.7 15.8 %collective-permute-start.20 = (bf16[64,4096]{1,0:T(8,128)(2,1)S(1)}, bf16[64,4096]{1,0:T(8,128)(2,1)S(1)}, u32[]{:S(2)}, u32[]{:S(2)}) collective-permute-start(bf16[64,4096]{1,0:T(8,128)(2,1)S(1)} %get-tuple-element.43), channel_id=1, source_target_pairs={{0,2},{1,3},{2,0},{3,1},{4,6},{5,7},{6,4},{7,5},{8,10},{9,11},{10,... | collective-permute-start | bytes 1572872 | tf_op jit(solution)/shard_map/ppermute | solution.py:267
  865.7 24.2 %collective-permute-start.21 = (bf16[64,4096]{1,0:T(8,128)(2,1)S(1)}, bf16[64,4096]{1,0:T(8,128)(2,1)S(1)}, u32[]{:S(2)}, u32[]{:S(2)}) collective-permute-start(bf16[64,4096]{1,0:T(8,128)(2,1)S(1)} %get-tuple-element.42), channel_id=1, source_target_pairs={{0,3},{1,0},{2,1},{3,2},{4,7},{5,4},{6,5},{7,6},{8,11},{9,8},{10,9... | collective-permute-start | bytes 1572872 | tf_op jit(solution)/shard_map/ppermute | solution.py:267
  (22 other events, 63.8 us)
Sparse Core Ops, SparseCore 0:
  9.9 90.8 all-gather.4
  155.4 108.7 all-gather.2
  430.1 84.7 reduce-scatter.3
  518.6 71.8 reduce-scatter.7
  593.9 160.8 reduce-scatter.5

commit v3 on v1

v3 whole, which is shorter than its diff:
```python
import functools
import math

import jax
import jax.numpy as jnp
from jax import lax
from jax.experimental import pallas as pl
from jax.experimental.pallas import tpu as pltpu
from jax.sharding import PartitionSpec as P

FF = 8192
HEADS = 32
KV_HEADS = 8
HEAD_DIM = 64
HALF = HEAD_DIM // 2
EPS = 1e-05
NEGATIVE = -1e30
SCORE_SCALE = 1.0 / math.sqrt(HEAD_DIM)
BOTH = ("wide", "narrow")
F32 = jnp.float32
BF16 = jnp.bfloat16
NN = (((1,), (0,)), ((), ()))
NT = (((1,), (1,)), ((), ()))
TN = (((0,), (0,)), ((), ()))


def dot(left, right, dims, kind=F32):
    return lax.dot_general(left, right, dims, preferred_element_type=F32).astype(kind)


def places(lengths_row, total_rows):
    seq_ends = jnp.cumsum(lengths_row)
    starts = seq_ends - lengths_row
    row_index = jnp.arange(total_rows, dtype=jnp.int32)
    segments = jnp.sum((row_index[:, None] >= seq_ends[None, :]).astype(jnp.int32), -1)
    slot_index = jnp.arange(lengths_row.shape[0], dtype=jnp.int32)
    owned = segments[:, None] == slot_index[None, :]
    first = jnp.sum(jnp.where(owned, starts[None, :], 0), -1)
    return first, row_index - first


def rotary(positions, half_width):
    channel = jnp.arange(half_width, dtype=jnp.float32)
    inverse_rate = jnp.power(500000.0, -channel / half_width)
    wavelength = 2.0 * math.pi / inverse_rate
    smooth = (8192.0 / wavelength - 1.0) / 3.0
    blended = (1.0 - smooth) * inverse_rate / 32.0 + smooth * inverse_rate
    frequency = jnp.where(
        wavelength < 2048.0,
        inverse_rate,
        jnp.where(wavelength > 8192.0, inverse_rate / 32.0, blended),
    )
    angles = frequency[:, None] * positions[None, :]
    return jnp.cos(angles), jnp.sin(angles)


def norm_back(grad_unit, unit_rows, row_scale):
    return row_scale * (grad_unit - unit_rows * jnp.mean(grad_unit * unit_rows, -1, keepdims=True))


MESH = pl.DeviceIdType.MESH


class Flow:
    def __init__(self, wide, narrow, x_ref, out_ref, sems):
        self.wide, self.narrow, self.x_ref, self.out_ref = wide, narrow, x_ref, out_ref
        self.w, self.n = lax.axis_index("wide"), lax.axis_index("narrow")
        (self.own_sem, self.z_send, self.z_recv, self.m_send, self.m_recv,
         self.r_send, self.r_recv, self.c_send, self.c_recv) = sems
        self.relay = wide == 8
        self.masks = [2, 4] if self.relay else list(range(2, wide, 2))
        self.last = narrow + 2

    def to_wide(self, mask):
        return {"wide": self.w ^ mask, "narrow": self.n}

    def owner_of(self, side, d):
        return self.n - d if side == 0 else self.n + d

    def valid(self, side, d):
        return self.n - d >= 0 if side == 0 else self.n + d < self.narrow

    def can_pass(self, side, d):
        if side == 0:
            return (self.n - (d - 1) >= 0) & (self.n < self.narrow - 1)
        return (self.n + (d - 1) < self.narrow) & (self.n > 0)

    def slot(self, side, d):
        return d - 1 + side * (self.narrow - 1) if d else 2 * (self.narrow - 1)

    def at_distance(self, d, action):
        if d == 0:
            action(0, 0)
            return
        for side in (0, 1):
            pl.when(self.valid(side, d))(functools.partial(action, side, d))

    def place(self, owner_w, owner_n, part=None):
        depth = self.x_ref.shape[0]
        half = depth // 2
        at = (owner_w * self.narrow + owner_n) * depth
        if part is None:
            return self.out_ref.at[pl.ds(pl.multiple_of(at, depth), depth), :]
        return self.out_ref.at[pl.ds(pl.multiple_of(at + part * half, half), half), :]

    def own_copy(self):
        return pltpu.make_async_copy(self.x_ref, self.place(self.w, self.n), self.own_sem)

    def z_copy(self, side, d):
        block = self.place(self.w, self.owner_of(side, d - 1))
        return pltpu.make_async_remote_copy(
            src_ref=self.x_ref if d == 1 else block,
            dst_ref=block,
            send_sem=self.z_send.at[side, d],
            recv_sem=self.z_recv.at[side, d],
            device_id={"wide": self.w, "narrow": self.n + 1 if side == 0 else self.n - 1},
            device_id_type=MESH,
        )

    def z_wait(self, side, d):
        block = self.place(self.w, self.owner_of(side, d))
        pltpu.make_async_copy(block, block, self.z_recv.at[side, d]).wait()

    def m_copy(self, i, side, d):
        block = self.place(self.w, self.owner_of(side, d))
        return pltpu.make_async_remote_copy(
            src_ref=self.x_ref if d == 0 else block,
            dst_ref=block,
            send_sem=self.m_send.at[i, self.slot(side, d)],
            recv_sem=self.m_recv.at[i, self.slot(side, d)],
            device_id=self.to_wide(self.masks[i]),
            device_id_type=MESH,
        )

    def m_wait(self, i, side, d):
        block = self.place(self.w ^ self.masks[i], self.owner_of(side, d))
        pltpu.make_async_copy(block, block, self.m_recv.at[i, self.slot(side, d)]).wait()

    def r_copy(self, part, side, d):
        block = self.place(self.w ^ self.masks[part], self.owner_of(side, d), part)
        return pltpu.make_async_remote_copy(
            src_ref=block,
            dst_ref=block,
            send_sem=self.r_send.at[part, self.slot(side, d)],
            recv_sem=self.r_recv.at[part, self.slot(side, d)],
            device_id=self.to_wide(self.masks[1 - part]),
            device_id_type=MESH,
        )

    def r_wait(self, part, side, d):
        block = self.place(self.w ^ 6, self.owner_of(side, d), part)
        pltpu.make_async_copy(block, block, self.r_recv.at[part, self.slot(side, d)]).wait()

    def c_copy(self, chip, side, d):
        block = self.place(self.w ^ (2 * chip), self.owner_of(side, d))
        return pltpu.make_async_remote_copy(
            src_ref=self.x_ref if d == 0 and chip == 0 else block,
            dst_ref=block,
            send_sem=self.c_send.at[chip, self.slot(side, d)],
            recv_sem=self.c_recv.at[chip, self.slot(side, d)],
            device_id=self.to_wide(1),
            device_id_type=MESH,
        )

    def c_wait(self, chip, side, d):
        block = self.place((self.w ^ 1) ^ (2 * chip), self.owner_of(side, d))
        pltpu.make_async_copy(block, block, self.c_recv.at[chip, self.slot(side, d)]).wait()

    def send_from_here(self, side, d):
        if d > 0:
            self.z_wait(side, d)
        if 0 < d < self.narrow - 1:
            pl.when(self.can_pass(side, d + 1))(lambda: self.z_copy(side, d + 1).start())
        for i in range(len(self.masks)):
            self.m_copy(i, side, d).start()
        self.c_copy(0, side, d).start()

    def send_on(self, side, d):
        for i in range(len(self.masks)):
            self.m_wait(i, side, d)
            if self.relay:
                self.r_copy(i, side, d).start()
            self.c_copy(self.masks[i] // 2, side, d).start()

    def send_last(self, side, d):
        self.r_wait(0, side, d)
        self.r_wait(1, side, d)
        self.c_copy(3, side, d).start()

    def step(self, t):
        if t == 0:
            self.own_copy().start()
            for side in (0, 1):
                pl.when(self.can_pass(side, 1))(lambda side=side: self.z_copy(side, 1).start())
        if 0 <= t < self.narrow:
            self.at_distance(t, self.send_from_here)
        if 0 <= t - 1 < self.narrow:
            self.at_distance(t - 1, self.send_on)
        if self.relay and 0 <= t - 2 < self.narrow:
            self.at_distance(t - 2, self.send_last)

    def finish(self, side, d):
        for i in range(len(self.masks)):
            self.m_copy(i, side, d).wait_send()
            if self.relay:
                self.r_copy(i, side, d).wait_send()
        for chip in range(self.wide // 2):
            self.c_copy(chip, side, d).wait_send()
            self.c_wait(chip, side, d)

    def end(self):
        self.own_copy().wait()
        for side in (0, 1):
            for d in range(1, self.narrow):
                pl.when(self.can_pass(side, d))(
                    lambda side=side, d=d: self.z_copy(side, d).wait_send()
                )
        for d in range(self.narrow):
            self.at_distance(d, self.finish)


class Line:
    def __init__(self, narrow, x_ref, out_ref, sems):
        self.narrow, self.x_ref, self.out_ref = narrow, x_ref, out_ref
        self.w, self.n = lax.axis_index("wide"), lax.axis_index("narrow")
        self.own_sem, self.send, self.recv = sems

    def owner_of(self, side, d):
        return self.n - d if side == 0 else self.n + d

    def valid(self, side, d):
        return self.n - d >= 0 if side == 0 else self.n + d < self.narrow

    def can_pass(self, side, d):
        if side == 0:
            return (self.n - (d - 1) >= 0) & (self.n < self.narrow - 1)
        return (self.n + (d - 1) < self.narrow) & (self.n > 0)

    def own_copy(self):
        return pltpu.make_async_copy(self.x_ref, self.out_ref.at[self.n], self.own_sem)

    def copy(self, side, d):
        block = self.out_ref.at[self.owner_of(side, d - 1)]
        return pltpu.make_async_remote_copy(
            src_ref=self.x_ref if d == 1 else block,
            dst_ref=block,
            send_sem=self.send.at[side, d],
            recv_sem=self.recv.at[side, d],
            device_id={"wide": self.w, "narrow": self.n + 1 if side == 0 else self.n - 1},
            device_id_type=MESH,
        )

    def pass_on(self, side, d):
        arrive(self.out_ref.at[self.owner_of(side, d)], self.recv.at[side, d])
        if d < self.narrow - 1:
            pl.when(self.can_pass(side, d + 1))(lambda: self.copy(side, d + 1).start())

    def step(self, t):
        if t == 0:
            self.own_copy().start()
        for side in (0, 1):
            if t == 0:
                pl.when(self.can_pass(side, 1))(lambda side=side: self.copy(side, 1).start())
            else:
                pl.when(self.valid(side, t))(lambda side=side: self.pass_on(side, t))

    def end(self):
        self.own_copy().wait()
        for side in (0, 1):
            for d in range(1, self.narrow):
                pl.when(self.can_pass(side, d))(lambda side=side, d=d: self.copy(side, d).wait_send())


def flow_sems(wide, narrow):
    slots = 2 * narrow - 1
    masks = 2 if wide == 8 else wide // 2 - 1
    dma = pltpu.SemaphoreType.DMA
    return [
        dma(()),
        dma((2, narrow)),
        dma((2, narrow)),
        dma((masks, slots)),
        dma((masks, slots)),
        dma((2, slots)),
        dma((2, slots)),
        dma((wide // 2, slots)),
        dma((wide // 2, slots)),
    ]


def greet(wide, narrow):
    w, n = lax.axis_index("wide"), lax.axis_index("narrow")
    barrier = pltpu.get_barrier_semaphore()
    for mask in range(1, wide):
        pl.semaphore_signal(
            barrier, inc=1, device_id={"wide": w ^ mask, "narrow": n}, device_id_type=MESH
        )
    for step in range(1, narrow):
        other = lax.rem(n + step, narrow)
        pl.semaphore_signal(
            barrier, inc=1, device_id={"wide": w, "narrow": other}, device_id_type=MESH
        )
    pl.semaphore_wait(barrier, wide + narrow - 2)


def to_owner(source, target, send_sem, recv_sem, mask):
    w, n = lax.axis_index("wide"), lax.axis_index("narrow")
    return pltpu.make_async_remote_copy(
        src_ref=source,
        dst_ref=target,
        send_sem=send_sem,
        recv_sem=recv_sem,
        device_id={"wide": w ^ mask, "narrow": n},
        device_id_type=MESH,
    )


def to_block(source, target, send_sem, recv_sem, owner):
    n = lax.axis_index("narrow")
    return pltpu.make_async_remote_copy(
        src_ref=source,
        dst_ref=target,
        send_sem=send_sem,
        recv_sem=recv_sem,
        device_id={"wide": owner, "narrow": n},
        device_id_type=MESH,
    )


def arrive(block, sem):
    pltpu.make_async_copy(block, block, sem).wait()


def attend_kernel(
    wide, narrow, groups, start_ref, mine_ref, w_ref, c_ref,
    x_ref, low_ref, full_ref, log_ref, w_all, c_all,
    keys, top, total, acc, done, own_sem, in_send, in_recv, out_send, out_recv,
    line_own, line_send, line_recv, *sems,
):
    me = lax.axis_index("wide")
    blocks, _, rows = x_ref.shape
    width = groups * HEAD_DIM
    own_in = pltpu.make_async_copy(mine_ref.at[me], x_ref.at[me], own_sem.at[0])
    own_in.start()
    greet(wide, narrow)
    for mask in range(1, wide):
        to_owner(
            mine_ref.at[me ^ mask], x_ref.at[me], in_send.at[mask], in_recv.at[me], mask
        ).start()
    flow = Flow(wide, narrow, w_ref, w_all, sems)
    line = Line(narrow, c_ref, c_all, (line_own, line_send, line_recv))
    flow.step(0)
    line.step(0)
    spread = {}
    for t in range(1, flow.last):
        spread.setdefault(min(blocks, blocks // 2 - 1 + t), []).append(functools.partial(flow.step, t))
    for t in range(1, narrow):
        spread.setdefault(min(blocks, blocks // 2 + 2 * t - 1), []).append(functools.partial(line.step, t))
    key_row = lax.broadcasted_iota(jnp.int32, (rows, rows), 0)
    column = lax.broadcasted_iota(jnp.int32, (rows, rows), 1)
    own_in.wait()

    def block(i, carry):
        pl.when(i != me)(lambda: arrive(x_ref.at[i], in_recv.at[i]))
        for at, actions in spread.items():
            if at < blocks:

                @pl.when(i == at)
                def _():
                    for action in actions:
                        action()

        keys[i] = x_ref[i, width : width + HEAD_DIM, :].T
        top[...] = jnp.full_like(top, NEGATIVE)
        total[...] = jnp.zeros_like(total)
        acc[...] = jnp.zeros_like(acc)
        start = start_ref[i]
        query_row = i * rows + column

        def step(j, carry):
            key_index = key_row + j * rows
            allowed = (key_index <= query_row) & (key_index >= start)
            key_block = keys[j]
            value_block = x_ref[j, width + HEAD_DIM :, :]
            for h in range(groups):
                own = pl.ds(h * HEAD_DIM, HEAD_DIM)
                scores = dot(key_block, x_ref[i, own, :], NN)
                scores = jnp.where(allowed, scores, NEGATIVE)
                old = top[h : h + 1, :]
                new = jnp.maximum(old, jnp.max(scores, 0, keepdims=True))
                shrink = jnp.exp(old - new)
                prob = jnp.exp(scores - new)
                top[h : h + 1, :] = new
                total[h : h + 1, :] = total[h : h + 1, :] * shrink + jnp.sum(prob, 0, keepdims=True)
                acc[own, :] = acc[own, :] * shrink + dot(value_block, prob.astype(BF16), NN)
            return carry

        lax.fori_loop(0, i + 1, step, 0)
        log_ref[i] = top[...] + jnp.log(total[...])
        for h in range(groups):
            own = pl.ds(h * HEAD_DIM, HEAD_DIM)
            result = acc[own, :] / total[h : h + 1, :]
            full_ref[i, own, :] = result
            done[i, own, :] = result.astype(BF16)

        @pl.when(i != me)
        def _():
            to_block(done.at[i], low_ref.at[me], out_send.at[i], out_recv.at[me], i).start()

        return carry

    lax.fori_loop(0, blocks, block, 0)
    low_ref[me] = done[me]
    for action in spread.get(blocks, []):
        action()
    flow.end()
    line.end()
    for mask in range(1, wide):
        to_owner(
            mine_ref.at[me ^ mask], x_ref.at[me], in_send.at[mask], in_recv.at[me], mask
        ).wait_send()
        other = me ^ mask
        arrive(low_ref.at[other], out_recv.at[other])
        arrive(done.at[other], out_send.at[other])


def attend(mine, start, w_out, cot, groups):
    wide, narrow = lax.axis_size("wide"), lax.axis_size("narrow")
    blocks, features, rows = mine.shape
    width = groups * HEAD_DIM
    dma = pltpu.SemaphoreType.DMA
    hbm = pl.BlockSpec(memory_space=pl.ANY)
    vmem = pl.BlockSpec(memory_space=pltpu.VMEM)
    return pl.pallas_call(
        functools.partial(attend_kernel, wide, narrow, groups),
        out_shape=(
            jax.ShapeDtypeStruct((blocks, features, rows), BF16),
            jax.ShapeDtypeStruct((blocks, width, rows), BF16),
            jax.ShapeDtypeStruct((blocks, width, rows), F32),
            jax.ShapeDtypeStruct((blocks, groups, rows), F32),
            jax.ShapeDtypeStruct((wide * narrow * w_out.shape[0], w_out.shape[1]), BF16),
            jax.ShapeDtypeStruct((narrow,) + cot.shape, BF16),
        ),
        in_specs=[vmem, vmem, hbm, hbm],
        out_specs=(vmem, vmem, vmem, vmem, hbm, hbm),
        scratch_shapes=[
            pltpu.VMEM((blocks, rows, HEAD_DIM), BF16),
            pltpu.VMEM((groups, rows), F32),
            pltpu.VMEM((groups, rows), F32),
            pltpu.VMEM((width, rows), F32),
            pltpu.VMEM((blocks, width, rows), BF16),
            dma((1,)),
            dma((wide,)),
            dma((wide,)),
            dma((wide,)),
            dma((wide,)),
            dma(()),
            dma((2, narrow)),
            dma((2, narrow)),
        ]
        + flow_sems(wide, narrow),
        compiler_params=pltpu.CompilerParams(
            collective_id=3, has_side_effects=True, vmem_limit_bytes=40 << 20
        ),
        cost_estimate=pl.CostEstimate(
            flops=32 * width * (blocks * rows) ** 2,
            bytes_accessed=64 << 20,
            transcendentals=groups * (blocks * rows) ** 2 // 2,
        ),
    )(start, mine, w_out, cot)


def attend_back_kernel(
    wide, narrow, groups, start_ref, x_ref, mine_ref, full_ref, log_ref, cos_ref, sin_ref, part_ref,
    out_ref, came_ref,
    keys, values, acc, acc_keys, acc_values, grad_ref, done, own_sem, in_send, in_recv,
    q_send, q_recv, k_send, k_recv, p_send, p_recv,
):
    me, n = lax.axis_index("wide"), lax.axis_index("narrow")

    def part_copy(step):
        other = lax.rem(n + step, narrow)
        return pltpu.make_async_remote_copy(
            src_ref=part_ref.at[other],
            dst_ref=came_ref.at[step],
            send_sem=p_send.at[step],
            recv_sem=p_recv.at[step],
            device_id={"wide": me, "narrow": other},
            device_id_type=MESH,
        )

    own_part = pltpu.make_async_copy(part_ref.at[n], came_ref.at[0], p_send.at[0])
    blocks, _, rows = x_ref.shape
    width = groups * HEAD_DIM
    own_in = pltpu.make_async_copy(mine_ref.at[me], grad_ref.at[me], own_sem.at[0])
    own_in.start()
    for j in range(blocks):
        keys[j] = x_ref[j, width : width + HEAD_DIM, :].T
        values[j] = x_ref[j, width + HEAD_DIM :, :].T
    acc_keys[...] = jnp.zeros_like(acc_keys)
    acc_values[...] = jnp.zeros_like(acc_values)
    greet(wide, narrow)
    for mask in range(1, wide):
        to_owner(
            mine_ref.at[me ^ mask], grad_ref.at[me], in_send.at[mask], in_recv.at[me], mask
        ).start()
    own_part.start()
    for step in range(1, narrow):
        part_copy(step).start()
    key_row = lax.broadcasted_iota(jnp.int32, (rows, rows), 0)
    column = lax.broadcasted_iota(jnp.int32, (rows, rows), 1)
    own_in.wait()
    of_queries, of_keys = pl.ds(0, width), pl.ds(width, 2 * HEAD_DIM)

    def turn_back(block, cos, sin):
        front, back = block[:HALF, :], block[HALF:, :]
        return (front * cos + back * sin).astype(BF16), (back * cos - front * sin).astype(BF16)

    def block(i, carry):
        pl.when(i != me)(lambda: arrive(grad_ref.at[i], in_recv.at[i]))
        acc[...] = jnp.zeros_like(acc)
        start = start_ref[i]
        query_row = i * rows + column
        deltas = [
            jnp.sum(
                grad_ref[i, pl.ds(h * HEAD_DIM, HEAD_DIM), :].astype(F32)
                * full_ref[i, pl.ds(h * HEAD_DIM, HEAD_DIM), :],
                0,
                keepdims=True,
            )
            for h in range(groups)
        ]

        def step(j, carry):
            key_index = key_row + j * rows
            allowed = (key_index <= query_row) & (key_index >= start)
            key_block = keys[j]
            value_block = values[j]
            key_columns = x_ref[j, width : width + HEAD_DIM, :]
            grad_keys = acc_keys[j]
            grad_values = acc_values[j]
            for h in range(groups):
                own = pl.ds(h * HEAD_DIM, HEAD_DIM)
                query = x_ref[i, own, :]
                grad = grad_ref[i, own, :]
                scores = dot(key_block, query, NN)
                scores = jnp.where(allowed, scores, NEGATIVE)
                prob = jnp.exp(scores - log_ref[i, h : h + 1, :])
                grad_prob = dot(value_block, grad, NN)
                grad_scores = (prob * (grad_prob - deltas[h])).astype(BF16)
                acc[own, :] += dot(key_columns, grad_scores, NN)
                grad_keys = grad_keys + dot(query, grad_scores, NT)
                grad_values = grad_values + dot(grad, prob.astype(BF16), NT)
            acc_keys[j] = grad_keys
            acc_values[j] = grad_values
            return carry

        lax.fori_loop(0, i + 1, step, 0)
        for h in range(groups):
            at = h * HEAD_DIM
            front, back = turn_back(
                acc[pl.ds(at, HEAD_DIM), :] * SCORE_SCALE, cos_ref[i], sin_ref[i]
            )
            done[i, pl.ds(at, HALF), :] = front
            done[i, pl.ds(at + HALF, HALF), :] = back

        @pl.when(i != me)
        def _():
            to_block(
                done.at[i, of_queries], out_ref.at[me, of_queries], q_send.at[i], q_recv.at[me], i
            ).start()

        return carry

    lax.fori_loop(0, blocks, block, 0)

    def last(j, carry):
        front, back = turn_back(acc_keys[j], cos_ref[j], sin_ref[j])
        done[j, pl.ds(width, HALF), :] = front
        done[j, pl.ds(width + HALF, HALF), :] = back
        done[j, pl.ds(width + HEAD_DIM, HEAD_DIM), :] = acc_values[j].astype(BF16)

        @pl.when(j != me)
        def _():
            to_block(
                done.at[j, of_keys], out_ref.at[me, of_keys], k_send.at[j], k_recv.at[me], j
            ).start()

        return carry

    lax.fori_loop(0, blocks, last, 0)
    out_ref[me] = done[me]
    for mask in range(1, wide):
        other = me ^ mask
        arrive(mine_ref.at[other], in_send.at[mask])
        arrive(done.at[other, of_queries], q_send.at[other])
        arrive(done.at[other, of_keys], k_send.at[other])
        arrive(out_ref.at[other, of_queries], q_recv.at[other])
        arrive(out_ref.at[other, of_keys], k_recv.at[other])
    own_part.wait()
    for step in range(1, narrow):
        part_copy(step).wait()


def attend_back(x, mine, full, log_total, start, cos, sin, part, groups):
    wide, narrow = lax.axis_size("wide"), lax.axis_size("narrow")
    blocks, features, rows = x.shape
    width = groups * HEAD_DIM
    dma = pltpu.SemaphoreType.DMA
    hbm = pl.BlockSpec(memory_space=pl.ANY)
    vmem = pl.BlockSpec(memory_space=pltpu.VMEM)
    return pl.pallas_call(
        functools.partial(attend_back_kernel, wide, narrow, groups),
        out_shape=(
            jax.ShapeDtypeStruct(x.shape, BF16),
            jax.ShapeDtypeStruct(part.shape, BF16),
        ),
        in_specs=[vmem] * 7 + [hbm],
        out_specs=(vmem, hbm),
        scratch_shapes=[
            pltpu.VMEM((blocks, rows, HEAD_DIM), BF16),
            pltpu.VMEM((blocks, rows, HEAD_DIM), BF16),
            pltpu.VMEM((width, rows), F32),
            pltpu.VMEM((blocks, HEAD_DIM, rows), F32),
            pltpu.VMEM((blocks, HEAD_DIM, rows), F32),
            pltpu.VMEM((blocks, width, rows), BF16),
            pltpu.VMEM((blocks, features, rows), BF16),
            dma((1,)),
        ]
        + [dma((wide,))] * 6
        + [dma((narrow,))] * 2,
        compiler_params=pltpu.CompilerParams(
            collective_id=4, has_side_effects=True, vmem_limit_bytes=40 << 20
        ),
        cost_estimate=pl.CostEstimate(
            flops=40 * width * (blocks * rows) ** 2,
            bytes_accessed=4 * x.size * 2,
            transcendentals=groups * (blocks * rows) ** 2 // 2,
        ),
    )(start, x, mine, full, log_total, cos, sin, part)


def gather(x, axis):
    return lax.all_gather(x, axis, axis=0, tiled=True)


def scatter_sum(x, axis):
    return lax.psum_scatter(x, axis, scatter_dimension=0, tiled=True)


def shift(x, step):
    n = lax.axis_size("narrow")
    return lax.ppermute(x, "narrow", [(i, (i + step) % n) for i in range(n)])


def pick(x, index, axis):
    return lax.dynamic_index_in_dim(x, index, axis, keepdims=False)


def gather_kernel(wide, narrow, aligned, qkv_ref, cut_ref, qkv_all, cut_all, x_send, x_recv, x_own, *sems):
    w, n = lax.axis_index("wide"), lax.axis_index("narrow")
    greet(wide, narrow)
    flow = Flow(wide, narrow, qkv_ref, qkv_all, sems)
    depth = qkv_ref.shape[0]
    piece = cut_all.shape[1] // (2 * wide)

    def rows_of(owner):
        return cut_all.at[pl.ds(pl.multiple_of(owner * depth, depth), depth), :]

    def pieces(other):
        if not aligned:
            return [(cut_ref.at[other], pl.ds(0, cut_all.shape[1]))]
        return [
            (
                cut_ref.at[:, pl.ds(pl.multiple_of((j * narrow + other) * piece, piece), piece)],
                pl.ds(j * piece, piece),
            )
            for j in range(2 * wide)
        ]

    def target(columns):
        return cut_all.at[pl.ds(pl.multiple_of(n * depth, depth), depth), columns]

    def cut_start(step):
        other = lax.rem(n + step, narrow)
        for source, columns in pieces(other):
            pltpu.make_async_remote_copy(
                src_ref=source,
                dst_ref=target(columns),
                send_sem=x_send.at[step],
                recv_sem=x_recv.at[step],
                device_id={"wide": w, "narrow": other},
                device_id_type=MESH,
            ).start()

    for t in range(flow.last):
        flow.step(t)
        if t == min(1, narrow - 1):
            for source, columns in pieces(n):
                pltpu.make_async_copy(source, target(columns), x_own).start()
            for step in range(1, narrow):
                cut_start(step)
    flow.end()
    own = rows_of(n)
    pltpu.make_async_copy(own, own, x_own).wait()
    for step in range(1, narrow):
        pltpu.make_async_copy(own, own, x_send.at[step]).wait()
        block = rows_of(lax.rem(n + narrow - step, narrow))
        pltpu.make_async_copy(block, block, x_recv.at[step]).wait()


def gather_weights(qkv, gateup):
    wide, narrow = lax.axis_size("wide"), lax.axis_size("narrow")
    dma = pltpu.SemaphoreType.DMA
    hbm = pl.BlockSpec(memory_space=pl.ANY)
    every = wide * narrow
    shard, columns = gateup.shape
    aligned = (columns // (2 * every)) % 128 == 0
    if not aligned:
        gateup = gateup.reshape(shard, 2, wide, narrow, -1).transpose(3, 0, 1, 2, 4)
        gateup = gateup.reshape(narrow, shard, columns // narrow)
    return pl.pallas_call(
        functools.partial(gather_kernel, wide, narrow, aligned),
        out_shape=(
            jax.ShapeDtypeStruct((every * qkv.shape[0], qkv.shape[1]), BF16),
            jax.ShapeDtypeStruct((narrow * shard, columns // narrow), BF16),
        ),
        in_specs=[hbm, hbm],
        out_specs=(hbm, hbm),
        scratch_shapes=[dma((narrow,)), dma((narrow,)), dma(())] + flow_sems(wide, narrow),
        compiler_params=pltpu.CompilerParams(collective_id=0, has_side_effects=True),
        cost_estimate=pl.CostEstimate(flops=0, bytes_accessed=200 << 20, transcendentals=0),
    )(qkv, gateup)


def feed_kernel(
    narrow, x_ref, cot_ref, gate_up_ref, down_ref,
    group_ref, hidden_out, grad_out, low_out, grad_x_ref,
    gate_up, down, cot, hidden, grads, low, came,
    load_sem, x_send, x_recv, out_sem, g_send, g_recv,
):
    w, n = lax.axis_index("wide"), lax.axis_index("narrow")
    rows, width = x_ref.shape
    own = down.shape[0]
    tile = 256
    tiles = own // tile
    wtiles = width // tile

    def to_narrow(other):
        return {"wide": w, "narrow": other}

    loads = [
        pltpu.make_async_copy(gate_up_ref, gate_up, load_sem.at[0]),
        pltpu.make_async_copy(down_ref, down, load_sem.at[1]),
        pltpu.make_async_copy(cot_ref, cot, load_sem.at[2]),
        pltpu.make_async_copy(x_ref, group_ref.at[n], load_sem.at[3]),
    ]
    for load in loads:
        load.start()

    barrier = pltpu.get_barrier_semaphore()
    for step in range(1, narrow):
        pl.semaphore_signal(
            barrier, inc=1, device_id=to_narrow(lax.rem(n + step, narrow)), device_id_type=MESH
        )
    pl.semaphore_wait(barrier, narrow - 1)

    def owner_of(side, d):
        return n - d if side == 0 else n + d

    def valid(side, d):
        return n - d >= 0 if side == 0 else (n + d < narrow) & (d > 0)

    def passes(side, d):
        if side == 0:
            return (n - d >= 0) & (n < narrow - 1)
        return (n + d < narrow) & (n > 0)

    def x_copy(side, d):
        block = group_ref.at[owner_of(side, d)]
        return pltpu.make_async_remote_copy(
            src_ref=block,
            dst_ref=block,
            send_sem=x_send.at[side, d],
            recv_sem=x_recv.at[side, d + 1],
            device_id=to_narrow(n + 1 if side == 0 else n - 1),
            device_id_type=MESH,
        )

    def x_wait(side, d):
        block = group_ref.at[owner_of(side, d)]
        pltpu.make_async_copy(block, block, x_recv.at[side, d]).wait()

    def out_copies(at, block):
        return [
            pltpu.make_async_copy(hidden.at[at], hidden_out.at[block], out_sem.at[at, 0]),
            pltpu.make_async_copy(grads.at[at], grad_out.at[block], out_sem.at[at, 1]),
            pltpu.make_async_copy(low.at[at], low_out.at[block], out_sem.at[at, 2]),
        ]

    def g_copy(block):
        return pltpu.make_async_remote_copy(
            src_ref=cot.at[block],
            dst_ref=came.at[n],
            send_sem=g_send.at[block],
            recv_sem=g_recv.at[n],
            device_id=to_narrow(block),
            device_id_type=MESH,
        )

    def compute(side, d):
        block = n - d + 2 * d * side
        before = 1 + jnp.minimum(n, d - 1) + jnp.minimum(narrow - 1 - n, d - 1)
        before = jnp.where(d == 0, 0, before + jnp.where((side == 1) & (n - d >= 0), 1, 0))
        at = lax.rem(before, 2)

        @pl.when(before >= 2)
        def _():
            for copy in out_copies(at, block):
                copy.wait()

        def first(f, carry):
            columns = pl.ds(pl.multiple_of(f * tile, tile), tile)
            other = pl.ds(pl.multiple_of(own + f * tile, tile), tile)
            x = group_ref[block]
            gate = dot(x, gate_up[:, columns], NN)
            up = dot(x, gate_up[:, other], NN)
            grad = dot(cot[block], down[columns, :], NT)
            sig = 1.0 / (1.0 + jnp.exp(-gate))
            silu = gate * sig
            hidden[at, :, columns] = (silu * up).astype(BF16)
            grads[at, :, columns] = (grad * up * (sig + silu * (1.0 - sig))).astype(BF16)
            grads[at, :, other] = (grad * silu).astype(BF16)
            return carry

        lax.fori_loop(0, tiles, first, 0)

        def second(f, carry):
            columns = pl.ds(pl.multiple_of(f * tile, tile), tile)
            cot[block, :, columns] = dot(grads[at], gate_up[columns, :], NT, BF16)
            low[at, :, columns] = dot(hidden[at], down[:, columns], NN, BF16)
            return carry

        lax.fori_loop(0, wtiles, second, 0)
        for copy in out_copies(at, block):
            copy.start()
        pl.when(block != n)(lambda: g_copy(block).start())

    def distance(d, carry):
        for side in (0, 1):

            @pl.when(valid(side, d) & (d > 0))
            def _():
                x_wait(side, d)

            @pl.when(passes(side, d))
            def _():
                x_copy(side, d).start()

        @pl.when(d == 0)
        def _():
            for load in loads[:3]:
                load.wait()

        def one(side, carry):
            ok = jnp.where(side == 0, n - d, jnp.where(d > 0, narrow - 1 - n - d, -1)) >= 0
            pl.when(ok)(lambda: compute(side, d))
            return carry

        lax.fori_loop(0, 2, one, 0)
        return carry

    loads[3].wait()
    lax.fori_loop(0, narrow, distance, 0)

    for at in range(min(2, narrow)):
        for copy in out_copies(at, n):
            copy.wait()
    for side in (0, 1):
        for d in range(narrow - 1):
            pl.when(passes(side, d))(lambda side=side, d=d: x_copy(side, d).wait_send())
    for step in range(1, narrow):
        other = lax.rem(n + step, narrow)
        g_copy(other).wait_send()
        block = came.at[other]
        pltpu.make_async_copy(block, block, g_recv.at[other]).wait()

    def add(r, carry):
        part = pl.ds(pl.multiple_of(r * 16, 16), 16)
        total = cot[n, part, :].astype(F32)
        for step in range(1, narrow):
            total = total + came[lax.rem(n + step, narrow), part, :].astype(F32)
        grad_x_ref[part, :] = total
        return carry

    lax.fori_loop(0, rows // 16, add, 0)


def feed(x, cot_group, gate_up, down):
    narrow = lax.axis_size("narrow")
    rows, width = x.shape
    own = down.shape[0]
    dma = pltpu.SemaphoreType.DMA
    hbm = pl.BlockSpec(memory_space=pl.ANY)
    vmem = pl.BlockSpec(memory_space=pltpu.VMEM)
    group, hidden, grads, low, grad_x = pl.pallas_call(
        functools.partial(feed_kernel, narrow),
        out_shape=(
            jax.ShapeDtypeStruct((narrow, rows, width), BF16),
            jax.ShapeDtypeStruct((narrow, rows, own), BF16),
            jax.ShapeDtypeStruct((narrow, rows, 2 * own), BF16),
            jax.ShapeDtypeStruct((narrow, rows, width), BF16),
            jax.ShapeDtypeStruct((rows, width), F32),
        ),
        in_specs=[vmem, hbm, hbm, hbm],
        out_specs=(vmem, hbm, hbm, hbm, vmem),
        scratch_shapes=[
            pltpu.VMEM((width, 2 * own), BF16),
            pltpu.VMEM((own, width), BF16),
            pltpu.VMEM((narrow, rows, width), BF16),
            pltpu.VMEM((2, rows, own), BF16),
            pltpu.VMEM((2, rows, 2 * own), BF16),
            pltpu.VMEM((2, rows, width), BF16),
            pltpu.VMEM((narrow, rows, width), BF16),
            dma((4,)),
            dma((2, narrow + 1)),
            dma((2, narrow + 1)),
            dma((2, 3)),
            dma((narrow,)),
            dma((narrow,)),
        ],
        compiler_params=pltpu.CompilerParams(
            collective_id=1, has_side_effects=True, vmem_limit_bytes=58 << 20
        ),
        cost_estimate=pl.CostEstimate(
            flops=12 * narrow * rows * width * own, bytes_accessed=300 << 20, transcendentals=0
        ),
    )(x, cot_group.reshape(narrow, rows, width), gate_up, down)
    flat = lambda y: y.reshape((-1,) + y.shape[2:])
    return flat(group), flat(hidden), flat(grads), flat(low), grad_x


def sum_kernel(
    wide, narrow, chunk, wout_ref, qkv_ref, gains_ref, *refs
):
    cut_refs, refs = refs[:narrow], refs[narrow:]
    (
        wout_out, qkv_out, cut_out, gains_out,
        held, core_in, chip_in, z_in, gain_w, gain_sum, gain_z,
        load_sem, core_send, core_recv, chip_send, chip_recv, z_send, z_recv,
        gw_send, gw_recv, gz_send, gz_recv,
    ) = refs
    w, n = lax.axis_index("wide"), lax.axis_index("narrow")
    core, chip = lax.rem(w, 2), w // 2
    chips = wide // 2
    bits = chips.bit_length() - 1
    rows = held.shape[2]
    shard = rows // narrow
    half = chunk // 2
    first_chunks = wout_ref.shape[3] // chunk
    chunks = first_chunks + qkv_ref.shape[3] // chunk
    orders = [list(range(bits)), list(range(bits))[::-1]]

    def to_wide(mask):
        return {"wide": w ^ mask, "narrow": n}

    def to_narrow(step):
        return {"wide": w, "narrow": lax.rem(n + step, narrow)}

    barrier = pltpu.get_barrier_semaphore()
    for mask in range(1, wide):
        pl.semaphore_signal(barrier, inc=1, device_id=to_wide(mask), device_id_type=MESH)
    for step in range(1, narrow):
        pl.semaphore_signal(barrier, inc=1, device_id=to_narrow(step), device_id_type=MESH)
    pl.semaphore_wait(barrier, wide - 1 + narrow - 1)

    def columns_of(q):
        return pl.ds(pl.multiple_of(q * chunk, chunk), chunk)

    def copies_from(ref, q, at):
        load = pltpu.make_async_copy(
            ref.at[:, core, :, columns_of(at)], held.at[q], load_sem.at[q]
        )
        send = pltpu.make_async_remote_copy(
            src_ref=ref.at[:, 1 - core, :, columns_of(at)],
            dst_ref=core_in.at[q],
            send_sem=core_send.at[q],
            recv_sem=core_recv.at[q],
            device_id=to_wide(1),
            device_id_type=MESH,
        )
        return load, send

    def begin(q):
        @pl.when(q < first_chunks)
        def _():
            for copy in copies_from(wout_ref, q, q):
                copy.start()

        @pl.when(q >= first_chunks)
        def _():
            for copy in copies_from(qkv_ref, q, jnp.maximum(q - first_chunks, 0)):
                copy.start()

    def add_to(target, other, size):
        def one(r, carry):
            part = pl.ds(pl.multiple_of(r * 16, 16), 16)
            target(part)[...] = (
                target(part)[...].astype(F32) + other(part)[...].astype(F32)
            ).astype(BF16)
            return carry

        lax.fori_loop(0, size // 16, one, 0)

    def tiles_of(h, stage):
        order = orders[h]
        rest = order[stage + 1 :]
        offset = sum(chips >> (i + 1) for i in range(stage))
        fixed = sum(1 << b for b in order[: stage + 1])
        result = []
        for v in range(1 << len(rest)):
            extra = sum(((v >> i) & 1) << b for i, b in enumerate(rest))
            result.append((offset + v, (chip & fixed) + extra))
        return result

    def lanes(h):
        return pl.ds(h * half, half)

    def chip_copy(q, h, stage, slot, kept):
        bit = orders[h][stage]
        return pltpu.make_async_remote_copy(
            src_ref=held.at[q, kept ^ (1 << bit), :, lanes(h)],
            dst_ref=chip_in.at[q, h, slot],
            send_sem=chip_send.at[q, h, slot],
            recv_sem=chip_recv.at[q, h, slot],
            device_id=to_wide(2 << bit),
            device_id_type=MESH,
        )

    def send_stage(q, stage):
        for h in (0, 1):
            for slot, kept in tiles_of(h, stage):
                chip_copy(q, h, stage, slot, kept).start()

    def z_copy(q, step):
        other = lax.rem(n + step, narrow)
        return pltpu.make_async_remote_copy(
            src_ref=held.at[q, chip, pl.ds(pl.multiple_of(other * shard, shard), shard), :],
            dst_ref=z_in.at[q, step],
            send_sem=z_send.at[q, step],
            recv_sem=z_recv.at[q, step],
            device_id=to_narrow(step),
            device_id_type=MESH,
        )

    def after_core(q):
        load, _ = copies_from(wout_ref, q, 0)
        load.wait()
        pltpu.make_async_copy(core_in.at[q], core_in.at[q], core_recv.at[q]).wait()
        for k in range(chips):
            add_to(
                lambda part, k=k: held.at[q, k, part, :],
                lambda part, k=k: core_in.at[q, k, part, :],
                rows,
            )
        send_stage(q, 0)

    def after_stage(q, stage):
        for h in (0, 1):
            for slot, kept in tiles_of(h, stage):
                block = chip_in.at[q, h, slot]
                pltpu.make_async_copy(block, block, chip_recv.at[q, h, slot]).wait()
                add_to(
                    lambda part, h=h, kept=kept: held.at[q, kept, part, lanes(h)],
                    lambda part, h=h, slot=slot: chip_in.at[q, h, slot, part, :],
                    rows,
                )
        if stage + 1 < bits:
            send_stage(q, stage + 1)
        else:
            for step in range(1, narrow):
                z_copy(q, step).start()

    def after_z(q):
        for step in range(1, narrow):
            block = z_in.at[q, step]
            pltpu.make_async_copy(block, block, z_recv.at[q, step]).wait()

        def total(r):
            part = pl.ds(pl.multiple_of(n * shard + r * 16, 16), 16)
            value = held[q, chip, part, :].astype(F32)
            for step in range(1, narrow):
                value = value + z_in[q, step, pl.ds(pl.multiple_of(r * 16, 16), 16), :].astype(F32)
            return value

        @pl.when(q < first_chunks)
        def _():
            def one(r, carry):
                to = pl.ds(pl.multiple_of(r * 16, 16), 16)
                wout_out[to, columns_of(jnp.minimum(q, first_chunks - 1))] = total(r)
                return carry

            lax.fori_loop(0, shard // 16, one, 0)

        @pl.when(q >= first_chunks)
        def _():
            def one(r, carry):
                to = pl.ds(pl.multiple_of(r * 16, 16), 16)
                qkv_out[to, columns_of(jnp.maximum(q - first_chunks, 0))] = total(r)
                return carry

            lax.fori_loop(0, shard // 16, one, 0)

    def gw_copy(mask):
        return pltpu.make_async_remote_copy(
            src_ref=gains_ref.at[w ^ mask],
            dst_ref=gain_w.at[mask],
            send_sem=gw_send.at[mask],
            recv_sem=gw_recv.at[mask],
            device_id=to_wide(mask),
            device_id_type=MESH,
        )

    def gz_copy(step):
        return pltpu.make_async_remote_copy(
            src_ref=gain_sum.at[lax.rem(n + step, narrow)],
            dst_ref=gain_z.at[step],
            send_sem=gz_send.at[step],
            recv_sem=gz_recv.at[step],
            device_id=to_narrow(step),
            device_id_type=MESH,
        )

    ahead = min(3, chunks)
    for q in range(ahead):
        begin(q)
    for mask in range(1, wide):
        gw_copy(mask).start()
    piece = cut_refs[0].shape[1] // (2 * wide)
    for step in range(narrow):
        if cut_out.shape[0] == narrow:
            cut_out[lax.rem(n + narrow - step, narrow)] = cut_refs[step][...].astype(F32)
            continue
        for j in range(2 * wide):
            at = (j * narrow + lax.rem(n + narrow - step, narrow)) * piece
            cut_out[:, pl.ds(pl.multiple_of(at, piece), piece)] = cut_refs[step][
                :, pl.ds(j * piece, piece)
            ].astype(F32)

    def turn(t, carry):
        pl.when(t + ahead < chunks)(lambda: begin(t + ahead))
        pl.when(t < chunks)(lambda: after_core(t))
        for stage in range(bits):
            q = t - 1 - stage
            pl.when((q >= 0) & (q < chunks))(lambda q=q, stage=stage: after_stage(q, stage))
        q = t - 1 - bits
        pl.when(q >= 0)(lambda: after_z(q))
        return carry

    lax.fori_loop(0, chunks + bits + 1, turn, 0)

    total = gains_ref[w]
    for mask in range(1, wide):
        block = gain_w.at[mask]
        pltpu.make_async_copy(block, block, gw_recv.at[mask]).wait()
        total = total + gain_w[mask]
    gain_sum[...] = total
    for step in range(1, narrow):
        gz_copy(step).start()

    total = gain_sum[n]
    for step in range(1, narrow):
        block = gain_z.at[step]
        pltpu.make_async_copy(block, block, gz_recv.at[step]).wait()
        total = total + gain_z[step]
    gains_out[...] = total

    for mask in range(1, wide):
        gw_copy(mask).wait_send()
    for step in range(1, narrow):
        gz_copy(step).wait_send()

    def drain(q, carry):
        _, send = copies_from(wout_ref, q, 0)
        send.wait_send()
        for stage in range(bits):
            for h in (0, 1):
                for slot, kept in tiles_of(h, stage):
                    chip_copy(q, h, stage, slot, kept).wait_send()
        for step in range(1, narrow):
            z_copy(q, step).wait_send()
        return carry

    lax.fori_loop(0, chunks, drain, 0)


def sum_all(wout, qkv, cuts, gains):
    wide, narrow = lax.axis_size("wide"), lax.axis_size("narrow")
    chips, _, rows, _ = wout.shape
    chunk = 512
    chunks = (wout.shape[3] + qkv.shape[3]) // chunk
    shard, cut_width = cuts[0].shape
    aligned = (cut_width // (2 * wide)) % 128 == 0
    cut_shape = (shard, narrow * cut_width) if aligned else (narrow, shard, cut_width)
    dma = pltpu.SemaphoreType.DMA
    hbm = pl.BlockSpec(memory_space=pl.ANY)
    vmem = pl.BlockSpec(memory_space=pltpu.VMEM)
    results = pl.pallas_call(
        functools.partial(sum_kernel, wide, narrow, chunk),
        out_shape=(
            jax.ShapeDtypeStruct((shard, wout.shape[3]), F32),
            jax.ShapeDtypeStruct((shard, qkv.shape[3]), F32),
            jax.ShapeDtypeStruct(cut_shape, F32),
            jax.ShapeDtypeStruct((8, 128), F32),
        ),
        in_specs=[hbm, hbm, vmem] + [vmem] * narrow,
        out_specs=(vmem, vmem, vmem, vmem),
        scratch_shapes=[
            pltpu.VMEM((chunks, chips, rows, chunk), BF16),
            pltpu.VMEM((chunks, chips, rows, chunk), BF16),
            pltpu.VMEM((chunks, 2, chips - 1, rows, chunk // 2), BF16),
            pltpu.VMEM((chunks, narrow, shard, chunk), BF16),
            pltpu.VMEM((wide, narrow, 8, 128), F32),
            pltpu.VMEM((narrow, 8, 128), F32),
            pltpu.VMEM((narrow, 8, 128), F32),
            dma((chunks,)),
            dma((chunks,)),
            dma((chunks,)),
            dma((chunks, 2, chips - 1)),
            dma((chunks, 2, chips - 1)),
            dma((chunks, narrow)),
            dma((chunks, narrow)),
            dma((wide,)),
            dma((wide,)),
            dma((narrow,)),
            dma((narrow,)),
        ],
        compiler_params=pltpu.CompilerParams(
            collective_id=2, has_side_effects=True, vmem_limit_bytes=54 << 20
        ),
        cost_estimate=pl.CostEstimate(flops=0, bytes_accessed=300 << 20, transcendentals=0),
    )(wout, qkv, gains, *cuts)
    return results, aligned


def per_device(tokens, lengths, gain_attn, w_qkv, w_out, gain_mlp, w_gateup, w_down, cotangent):
    rows, width = tokens.shape[1:]
    wide, narrow = lax.axis_size("wide"), lax.axis_size("narrow")
    pack_rows = rows * wide
    query_width, key_width = HEADS * HEAD_DIM, KV_HEADS * HEAD_DIM
    groups = HEADS // wide
    copies = wide // KV_HEADS
    own_ff = FF // narrow
    first, positions = places(lengths[0], pack_rows)
    cos_all, sin_all = rotary(positions.astype(F32), HALF)
    first_row = lax.axis_index("wide") * rows
    cos = lax.dynamic_slice_in_dim(cos_all, first_row, rows, 1)
    sin = lax.dynamic_slice_in_dim(sin_all, first_row, rows, 1)
    cos_all = cos_all.reshape(HALF, wide, rows).transpose(1, 0, 2)
    sin_all = sin_all.reshape(HALF, wide, rows).transpose(1, 0, 2)
    start = first.reshape(wide, 1, rows)

    gains = jnp.stack([gain_attn, gain_mlp], -1)
    with_gains = jnp.concatenate([w_qkv, jnp.pad(gains, ((0, 0), (0, 126)))], -1)
    shard = w_gateup.shape[0]
    qkv_gained, gateup_rows = gather_weights(with_gains, w_gateup)
    qkv_whole = qkv_gained[:, : w_qkv.shape[1]]
    gain_one = qkv_gained[:, w_qkv.shape[1]].astype(F32)
    gain_two = qkv_gained[:, w_qkv.shape[1] + 1].astype(F32)
    gateup_own = gather(gateup_rows, "wide")
    down_own = gather(w_down, "wide")

    inputs = tokens[0].astype(F32)
    scale_one = lax.rsqrt(jnp.mean(inputs * inputs, -1, keepdims=True) + EPS)
    unit_one = inputs * scale_one
    normed_one = (unit_one * gain_one).astype(BF16)
    projected = dot(qkv_whole, normed_one, (((0,), (1,)), ((), ())))
    turning = projected[: query_width + key_width].reshape(HEADS + KV_HEADS, 2, HALF, rows)
    front, back = turning[:, 0], turning[:, 1]
    turned = jnp.stack([front * cos - back * sin, back * cos + front * sin], 1)
    queries = (turned[:HEADS] * SCORE_SCALE).astype(BF16).reshape(wide, groups * HEAD_DIM, rows)
    keys = turned[HEADS:].astype(BF16).reshape(KV_HEADS, HEAD_DIM, rows)
    values = projected[query_width + key_width :].astype(BF16).reshape(KV_HEADS, HEAD_DIM, rows)
    keys_values = jnp.repeat(jnp.concatenate([keys, values], 1), copies, 0)
    heads, attended_low, attended_full, log_total, out_whole, cot_group = attend(
        jnp.concatenate([queries, keys_values], 1), start, w_out, cotangent[0], groups
    )
    cot_group = cot_group.reshape(-1, width)
    attended_low = attended_low.reshape(query_width, rows)
    middle = inputs + dot(attended_low, out_whole, TN)
    scale_two = lax.rsqrt(jnp.mean(middle * middle, -1, keepdims=True) + EPS)
    unit_two = middle * scale_two
    normed_two = (unit_two * gain_two).astype(BF16)

    normed_group, hidden, grad_gate_up, low_part, grad_normed_two = feed(
        normed_two, cot_group, gateup_own, down_own
    )
    part_gateup = dot(normed_group, grad_gate_up, TN, BF16)
    hidden, part_gateup = lax.optimization_barrier((hidden, part_gateup))
    grad_gateup = scatter_sum(part_gateup, "wide").reshape(narrow, shard, 2 * own_ff)
    grad_down = scatter_sum(dot(hidden, cot_group, TN, BF16), "wide")
    me = lax.axis_index("narrow")
    cuts = [pick(grad_gateup, me, 0)]
    for step in range(1, narrow):
        cuts.append(shift(pick(grad_gateup, (me + step) % narrow, 0), step))

    part_gain_two = jnp.sum(grad_normed_two * unit_two, 0)
    grad_middle = cotangent[0].astype(F32) + norm_back(
        grad_normed_two * gain_two, unit_two, scale_two
    )
    grad_branch = grad_middle.astype(BF16)
    grad_attended = dot(out_whole, grad_branch, NT, BF16).reshape(wide, groups * HEAD_DIM, rows)
    grad_heads, low_came = attend_back(
        heads, grad_attended, attended_full, log_total, start, cos_all, sin_all,
        low_part.reshape(narrow, rows, width), groups,
    )
    layer_out = (middle + jnp.sum(low_came.astype(F32), 0)).astype(BF16)[None]
    grad_queries = grad_heads[:, : groups * HEAD_DIM].reshape(query_width, rows)
    grad_keys_values = (
        grad_heads[:, groups * HEAD_DIM :]
        .reshape(KV_HEADS, copies, 2, HEAD_DIM, rows)
        .astype(F32)
        .sum(1)
        .astype(BF16)
    )
    grad_projected = jnp.concatenate(
        [
            grad_queries,
            grad_keys_values[:, 0].reshape(key_width, rows),
            grad_keys_values[:, 1].reshape(key_width, rows),
        ],
        0,
    )
    grad_normed_one = dot(grad_projected, qkv_whole, (((0,), (1,)), ((), ())))
    part_gain_one = jnp.sum(grad_normed_one * unit_one, 0)
    part_gains = jnp.stack([part_gain_one, part_gain_two], 0).reshape(2, wide, narrow, shard)
    part_gains = jnp.pad(
        part_gains.transpose(1, 2, 0, 3), ((0, 0), (0, 0), (0, 6), (0, 128 - shard))
    )
    cut = (wide // 2, 2, narrow * shard, -1)
    part_wout = dot(attended_low, grad_branch, NN, BF16).reshape(cut)
    part_qkv = dot(normed_one, grad_projected, (((0,), (1,)), ((), ())), BF16).reshape(cut)
    (grad_wout, grad_qkv, grad_gateup, grad_gains), done = sum_all(
        part_wout, part_qkv, cuts, part_gains
    )
    if not done:
        grad_gateup = (
            grad_gateup.reshape(narrow, shard, 2, wide, -1)
            .transpose(1, 2, 3, 0, 4)
            .reshape(shard, 2 * FF)
        )
    (grad_down, grad_wout) = lax.optimization_barrier((grad_down, grad_wout))
    grad_down = grad_down.astype(F32)
    grad_inputs = grad_middle + norm_back(grad_normed_one * gain_one, unit_one, scale_one)
    grad_tokens = grad_inputs.astype(BF16)[None]
    return (
        layer_out,
        grad_tokens,
        grad_gains[0, :shard],
        grad_qkv,
        grad_wout,
        grad_gains[1, :shard],
        grad_gateup,
        grad_down,
    )


def solution(mesh):
    rows, packs = P("narrow", "wide", None), P("narrow", None)
    weight, gain = P(BOTH, None), P(BOTH)
    return jax.shard_map(
        per_device,
        mesh=mesh,
        in_specs=(rows, packs, gain, weight, weight, gain, weight, weight, rows),
        out_specs=(rows, rows, gain, weight, weight, gain, weight, weight),
        check_vma=False,
    )
```

time: 1490 us -> 793 us (0.53)
  waiting for transfers between devices: 1000 us -> 35.7 us
  Pallas kernels: 130 us -> 594 us
  blocking collectives: 133 us -> 0 us
  matrix products: 118 us -> 87.2 us
  local copies, waits for them, and re-layouts: 42.7 us -> 19.4 us
    reduce_scatter x6 -> x2, waiting for transfers between devices: 529 us -> 8.36 us  [scatter_sum(): return lax.psum_scatter(x, axis, scatter_dimension=0, tiled=True)]
    pallas_call x3 -> x5, Pallas kernels: 130 us -> 594 us  [the longest x1 150 us: feed(): pl.pallas_call(functools.partial(feed_kernel, narrow), out_shape=(jax.Sha...]
    all_gather x6 -> x2, waiting for transfers between devices: 322 us -> 0.01 us  [gather(): return lax.all_gather(x, axis, axis=0, tiled=True)]
    all_to_all x3 -> x0, blocking collectives: 133 us -> none  [exchange(): return lax.all_to_all(x, axis, split_axis=0, concat_axis=0, tiled=True)]
    unnamed x14 -> x4, waiting for transfers between devices: 121 us -> 0.73 us
    dot_general x10 -> x8, matrix products: 118 us -> 87.2 us  [dot(): lax.dot_general(left, right, dims, preferred_element_type=F32).astype(kind)]
    all_to_all x3 -> x0, waiting for transfers between devices: 29.7 us -> none  [exchange(): return lax.all_to_all(x, axis, split_axis=0, concat_axis=0, tiled=True)]
    ppermute x0 -> x3, waiting for transfers between devices: none -> 26.6 us  [shift(): return lax.ppermute(x, 'narrow', [(i, (i + step) % n) for i in range(n)])]
  transfers between devices with their start and end apart: 16 -> 7, of which waited for: 13 -> 3; matrix products, arithmetic and copies ran while one was open for 9% -> 11% of each run, Pallas kernels for 6% -> 57%
where the time goes in v3:
time: 793 us; the launch traced here: 784 us
  Pallas kernels  594 us (75%)
  matrix products  87.2 us (11%)
  waiting for transfers between devices  35.7 us (5%)
  other arithmetic  21.3 us (3%)
  local copies, waits for them, and re-layouts  19.4 us (2%)
  between operations  14.6 us (2%)
  starting transfers between devices  11.4 us (1%)
    pallas_call x1, Pallas kernels, feed(): pl.pallas_call(functools.partial(feed_kernel, narrow), out_shape=(jax.Sha...  150 us
    pallas_call x1, Pallas kernels, attend(): pl.pallas_call(functools.partial(attend_kernel, wide, narrow, groups), ou...  135 us
    pallas_call x1, Pallas kernels, sum_all(): pl.pallas_call(functools.partial(sum_kernel, wide, narrow, chunk), out_sh...  131 us
    pallas_call x1, Pallas kernels, gather_weights(): pl.pallas_call(functools.partial(gather_kernel, wide, narrow, aligned), o...  96.7 us
    dot_general x8, matrix products, dot(): lax.dot_general(left, right, dims, preferred_element_type=F32).astype(kind)  87.2 us
    pallas_call x1, Pallas kernels, attend_back(): pl.pallas_call(functools.partial(attend_back_kernel, wide, narrow, groups...  82.3 us
    ppermute x3, waiting for transfers between devices, shift(): return lax.ppermute(x, 'narrow', [(i, (i + step) % n) for i in range(n)])  26.6 us
  transfers between devices with their start and end apart: 7, of which 3 were waited for; matrix products, arithmetic and copies ran while one was open for 11% of the time, Pallas kernels for 57%

profile of v3, /device:TPU:0, one launch (start us, length us, event | category | flops | bytes accessed | tf_op | source)
XLA Modules:
  0.0 783.9 jit_solution(15834306587711624011)
XLA Ops:
  7.2 0.7 all-gather.5.cloned.1.call-update
  7.9 0.7 pad_maximum_fusion.5
  8.7 1.8 fusion.25.qkv_ref
  10.5 96.7 %shard_map.152 = (bf16[2048,3200]{1,0:T(8,128)(2,1)}, bf16[256,4096]{1,0:T(8,128)(2,1)}) custom-call(bf16[64,3200]{1,0:T(8,128)(2,1)} %fusion.25.qkv_ref, bf16[64,16384]{1,0:T(8,128)(2,1)} %cut_ref.1), custom_call_target="tpu_custom_call" | custom-call | bytes 209715200 | tf_op jit(solution)/shard_map/pallas_call | solution.py:722
  107.3 1.8 convert_reduce_fusion.1
  109.2 0.3 fusion.18
  109.5 0.3 copy-done.27
  110.0 7.8 fusion.2
  118.0 0.4 copy-done.33
  118.9 0.3 copy-done.31
  119.4 0.5 multiply_subtract_fusion
  120.0 0.3 fusion.10
  120.5 1.1 copy-done.3
  121.6 135.1 %shard_map.153 = (bf16[8,384,256]{2,1,0:T(8,128)(2,1)S(1)}, bf16[8,256,256]{2,1,0:T(8,128)(2,1)S(1)}, f32[8,256,256]{2,1,0:T(8,128)S(1)}, f32[8,4,256]{2,1,0:T(4...) custom-call(s32[8,1,256]{2,1,0:T(1,128)S(1)} %bitcast.69, ...), custom_call_target="tpu_custom_call" | custom-call | flops 34359738368 | bytes 67108864 | tf_op jit(solution)/shard_map/pallas_call | solution.py:434
  256.7 8.2 %multiply_reduce_fusion.2 = (f32[256]{0:T(256)S(1)}, f32[256,2048]{1,0:T(8,128)S(1)}) fusion(bf16[2048,256]{1,0:T(8,128)(2,1)S(1)} %bitcast.66, bf16[2048,2048]{1,0:T(8,128)(2,1)} %get-tuple-element.33, bf16[1,256,2048]{2,1,0:T(8,128)(2,1)S(1)} %copy-done.14), kind=kOutput, calls=%fused_computation.35 | convolution fusion | flops 2149580544 | bytes 12583936 | tf_op jit(solution)/shard_map/dot_general | solution.py:28
  265.0 1.3 copy-done.8
  266.3 1.2 multiply_convert_fusion.x_ref
  267.5 149.5 %shard_map.154 = (bf16[4,256,2048]{2,1,0:T(8,128)(2,1)}, bf16[4,256,2048]{2,1,0:T(8,128)(2,1)}, bf16[4,256,4096]{2,1,0:T(8,128)(2,1)}, bf16[4,256,2048]{2,1,0:T(8,128)(2,1)}, f32[256,2048]{1,0:T(8,128)}) custom-call(bf16[256,2048]{1,0:T(8,128)(2,1)} %multiply_convert_fusion.x_ref, bf16[4,256,2048]{2,1,0:T(8,128)(2,1)} %copy-done.5, ...), custom_call_target="tpu_custom_call" | custom-call | flops 51539607552 | bytes 314572800 | tf_op jit(solution)/shard_map/pallas_call | solution.py:906
  417.0 24.8 %bitcast_convert_fusion = bf16[2048,4096]{1,0:T(8,128)(2,1)} fusion(bf16[4,256,2048]{2,1,0:T(8,128)(2,1)} %get-tuple-element.44, bf16[4,256,4096]{2,1,0:T(8,128)(2,1)} %get-tuple-element.45), kind=kOutput, calls=%fused_computation | convolution fusion | flops 17188257792 | bytes 29360128 | tf_op jit(solution)/shard_map/dot_general | solution.py:28
  441.9 14.7 %convolution_convert_fusion.1 = bf16[2048,2048]{1,0:T(8,128)(2,1)} fusion(bf16[1024,2048]{1,0:T(8,128)(2,1)} %bitcast.91, bf16[1024,2048]{1,0:T(8,128)(2,1)} %bitcast.71), kind=kOutput, calls=%fused_computation.7 | convolution fusion | flops 8594128896 | bytes 16777216 | tf_op jit(solution)/shard_map/dot_general | solution.py:28
  456.7 0.5 copy-done.32
  457.3 1.0 multiply_sine_fusion
  458.3 3.8 multiply_reduce_fusion
  462.3 1.1 copy-done.16
  463.3 0.7 multiply_add_fusion
  464.0 8.0 %convolution_convert_fusion.3 = bf16[2048,256]{1,0:T(8,128)(2,1)S(1)} fusion(bf16[2048,2048]{1,0:T(8,128)(2,1)} %get-tuple-element.33, f32[256,2048]{1,0:T(8,128)S(1)} %multiply_add_fusion), kind=kOutput, calls=%fused_computation.18 | convolution fusion | flops 2148532224 | bytes 11534336 | tf_op jit(solution)/shard_map/dot_general | solution.py:28
  472.0 82.3 %shard_map.155 = (bf16[8,384,256]{2,1,0:T(8,128)(2,1)S(1)}, bf16[4,256,2048]{2,1,0:T(8,128)(2,1)S(1)}) custom-call(s32[8,1,256]{2,1,0:T(1,128)S(1)} %bitcast.70, bf16[8,384,256]{2,1,0:T(8,128)(2,1)S(1)} %copy-done.7, bf16[8,256,256]{2,1,0:T(8,128)(2,1)S(1)} %bitcast.72, f32[8,256,256]{2,1,0:T(8,128)S(1)} %get-tuple-element.38.full_ref, ...), custom_call_target="tpu_custom_call" | custom-call | flops 42949672960 | bytes 6291456 | tf_op jit(solution)/shard_map/pallas_call | solution.py:612
  554.6 1.8 copy-done.2
  556.4 9.9 %fusion.17 = (f32[2048]{0:T(1024)S(1)}, f32[256]{0:T(256)S(1)}, f32[256,2048]{1,0:T(8,128)}) fusion(bf16[1,256,2048]{2,1,0:T(8,128)(2,1)S(1)} %copy-done.15, f32[256]{0:T(256)S(1)} %copy-done.30, f32[2048]{0:T(1024)S(1)} %copy-done.28, bf16[2048,3200]{1,0:T(8,128)(2,1)} %get-tuple-element.31, bf16[512,256]{1,0:T(8,128)(2,1)S(1)} %bitcast.83, ...), kind=kOutput, calls=%fused_computation.28 | convolution fusion | flops 3229611776 | bytes 17319936 | tf_op jit(solution)/shard_map/dot_general | solution.py:28
  566.5 3.4 convert_reduce_fusion
  570.0 0.9 copy-done.20
  570.9 2.3 fusion.19
  573.2 7.8 %convolution_convert_fusion = bf16[2048,3072]{1,0:T(8,128)(2,1)} fusion(bf16[512,256]{1,0:T(8,128)(2,1)S(1)} %bitcast.84, bf16[512,256]{1,0:T(8,128)(2,1)S(1)} %bitcast.82, bf16[2048,256]{1,0:T(8,128)(2,1)S(1)} %bitcast.78, bf16[1,256,2048]{2,1,0:T(8,128)(2,1)S(1)} %copy-done.15, f32[2048]{0:T(1024)S(1)} %copy-done.28, f32[256]{0:T(256)S(1)} %copy-done.30), kind=kOutput, calls=%fused_computation.1 | convolution fusion | flops 3234332672 | bytes 15213568 | tf_op jit(solution)/shard_map/dot_general | solution.py:28
  581.0 8.3 %reduce-scatter.3.cloned.1.call-done = bf16[256,4096]{1,0:T(8,128)(2,1)} async-done(((bf16[2048,4096]{1,0:T(8,128)(2,1)}), bf16[256,4096]{1,0:T(8,128)(2,1)}) %reduce-scatter.3.cloned.1.call-update) | async-done | bytes 2097168 | tf_op jit(solution)/shard_map/reduce_scatter | solution.py:648
  589.4 2.6 dynamic-slice_bitcast_fusion
  592.0 7.6 collective-permute-start
  599.6 3.4 collective-permute-start.1
  603.3 0.7 pad.9.gains_ref
  604.0 5.9 convolution_convert_fusion.2
  609.9 5.5 collective-permute-done.refs_1_
  615.4 21.0 %collective-permute-done.1.refs_2_ = bf16[64,4096]{1,0:T(8,128)(2,1)S(1)} collective-permute-done((bf16[64,4096]{1,0:T(8,128)(2,1)S(1)}, bf16[64,4096]{1,0:T(8,128)(2,1)S(1)}, u32[]{:S(2)}, u32[]{:S(2)}) %collective-permute-start.1) | collective-permute-done | bytes 524320 | tf_op jit(solution)/shard_map/ppermute | solution.py:653
  636.5 0.8 copy-done.25
  637.4 130.6 %shard_map.156 = (f32[64,2048]{1,0:T(8,128)}, f32[64,3072]{1,0:T(8,128)}, f32[64,16384]{1,0:T(8,128)}, f32[8,128]{1,0:T(8,128)}) custom-call(bf16[4,2,256,2048]{3,2,1,0:T(8,128)(2,1)} %bitcast.74, bf16[4,2,256,3072]{3,2,1,0:T(8,128)(2,1)} %bitcast.73, f32[8,4,8,128]{3,2,1,0:T(8,128)} %pad.9.gains_ref, bf16[64,4096]{1,0:T(8,128)(2,1)} %get-tuple-element.65.refs_0_, ...), custom_call_target="tpu_custom_call" | custom-call | bytes 314572800 | tf_op jit(solution)/shard_map/pallas_call | solution.py:1208
  768.1 2.9 convert_element_type.114
  771.1 1.3 slice_bitcast_fusion
  772.3 0.9 copy.31
  773.2 1.9 copy.32
  775.1 2.0 copy.33
  (95 shorter events, 2.8 us)
Async XLA Ops:
  7.2 260.3 %all-gather.5.cloned.1.call-start = ((), (), s32[]{:S(2)}) async-start(), calls=%async_computation.3 | async-start | bytes 9437184 | tf_op jit(solution)/shard_map/all_gather | solution.py:644
  7.9 259.6 %all-gather.3.cloned.1.call-start = ((), (), s32[]{:S(2)}) async-start(), calls=%async_computation.2 | async-start | bytes 18874368 | tf_op jit(solution)/shard_map/all_gather | solution.py:644
  107.2 1.9 copy-start.13
  107.3 482.1 %reduce-scatter.3.cloned.1.call-start = ((), (), s32[]{:S(2)}) async-start(), calls=%async_computation.4 | async-start | bytes 18874368 | tf_op jit(solution)/shard_map/reduce_scatter | solution.py:648
  109.2 0.6 copy-start.27
  109.5 0.6 copy-start.29
  117.8 0.7 copy-start.33
  118.7 0.5 copy-start.31
  120.3 1.2 copy-start.3
  120.3 1.3 copy-start.4
  121.6 135.1 %copy-start.14 = (bf16[1,256,2048]{2,1,0:T(8,128)(2,1)S(1)}, bf16[1,256,2048]{2,1,0:T(8,128)(2,1)}, u32[]{:S(2)}) copy-start(bf16[1,256,2048]{2,1,0:T(8,128)(2,1)} %param.9) | copy-start | bytes 3145732
  256.7 8.3 %copy-start = (bf16[8,256,256]{2,1,0:T(8,128)(2,1)}, bf16[8,256,256]{2,1,0:T(8,128)(2,1)S(1)}, u32[]{:S(2)}) copy-start(bf16[8,256,256]{2,1,0:T(8,128)(2,1)S(1)} %get-tuple-element.32) | copy-start | bytes 3145732
  256.7 8.3 %copy-start.5 = (bf16[4,256,2048]{2,1,0:T(8,128)(2,1)}, bf16[4,256,2048]{2,1,0:T(8,128)(2,1)S(1)}, u32[]{:S(2)}) copy-start(bf16[4,256,2048]{2,1,0:T(8,128)(2,1)S(1)} %get-tuple-element.35.cot_ref) | copy-start | bytes 12582916
  256.7 8.3 %copy-start.6 = (bf16[8,384,256]{2,1,0:T(8,128)(2,1)}, bf16[8,384,256]{2,1,0:T(8,128)(2,1)S(1)}, u32[]{:S(2)}) copy-start(bf16[8,384,256]{2,1,0:T(8,128)(2,1)S(1)} %get-tuple-element.34.x_ref) | copy-start | bytes 4718596
  265.0 1.3 copy-start.8
  441.9 326.3 %reduce-scatter.5.cloned.1.call-start = ((), (), s32[]{:S(2)}) async-start(), calls=%async_computation.5 | async-start | bytes 9437184 | tf_op jit(solution)/shard_map/reduce_scatter | solution.py:648
  456.6 0.7 copy-start.32
  458.3 4.0 copy-start.9
  458.3 5.0 copy-start.16
  464.0 8.1 %copy-start.11 = (f32[256,2048]{1,0:T(8,128)}, f32[256,2048]{1,0:T(8,128)S(1)}, u32[]{:S(2)}) copy-start(f32[256,2048]{1,0:T(8,128)S(1)} %multiply_add_fusion) | copy-start | bytes 6291460
  464.0 8.1 %copy-start.7 = (bf16[8,384,256]{2,1,0:T(8,128)(2,1)S(1)}, bf16[8,384,256]{2,1,0:T(8,128)(2,1)}, u32[]{:S(2)}) copy-start(bf16[8,384,256]{2,1,0:T(8,128)(2,1)} %copy-done.6) | copy-start | bytes 4718596
  554.4 2.0 copy-start.2
  554.4 2.0 copy-start.15
  554.4 2.0 copy-start.28
  554.4 2.0 copy-start.30
  554.6 11.8 %copy-start.17 = (bf16[8,256,256]{2,1,0:T(8,128)(2,1)}, bf16[8,256,256]{2,1,0:T(8,128)(2,1)S(1)}, u32[]{:S(2)}) copy-start(bf16[8,256,256]{2,1,0:T(8,128)(2,1)S(1)} %slice.56) | copy-start | bytes 3145732
  556.4 9.9 %copy-start.21 = (bf16[8,1,64,256]{3,2,1,0:T(8,128)(2,1)}, bf16[8,1,64,256]{3,2,1,0:T(8,128)(2,1)S(1)}, u32[]{:S(2)}) copy-start(bf16[8,1,64,256]{3,2,1,0:T(8,128)(2,1)S(1)} %get-tuple-element.67) | copy-start | bytes 786436
  566.5 3.5 copy-start.10
  566.5 3.5 copy-start.12
  566.5 4.4 copy-start.20
  570.9 2.3 copy-start.18
  570.9 2.3 copy-start.22
  589.4 14.6 %copy-start.1 = (bf16[8,256,256]{2,1,0:T(8,128)(2,1)S(1)}, bf16[8,256,256]{2,1,0:T(8,128)(2,1)}, u32[]{:S(2)}) copy-start(bf16[8,256,256]{2,1,0:T(8,128)(2,1)} %copy-done) | copy-start | bytes 3145732
  592.0 23.4 %collective-permute-start = (bf16[64,4096]{1,0:T(8,128)(2,1)S(1)}, bf16[64,4096]{1,0:T(8,128)(2,1)S(1)}, u32[]{:S(2)}, u32[]{:S(2)}) collective-permute-start(bf16[64,4096]{1,0:T(8,128)(2,1)S(1)} %get-tuple-element.64), channel_id=1, source_target_pairs={{0,1},{1,2},{2,3},{3,0},{4,5},{5,6},{6,7},{7,4},{8,9},{9,10},{10,1... | collective-permute-start | bytes 1572872 | tf_op jit(solution)/shard_map/ppermute | solution.py:653
  599.6 36.8 %collective-permute-start.1 = (bf16[64,4096]{1,0:T(8,128)(2,1)S(1)}, bf16[64,4096]{1,0:T(8,128)(2,1)S(1)}, u32[]{:S(2)}, u32[]{:S(2)}) collective-permute-start(bf16[64,4096]{1,0:T(8,128)(2,1)S(1)} %get-tuple-element.63), channel_id=1, source_target_pairs={{0,2},{1,3},{2,0},{3,1},{4,6},{5,7},{6,4},{7,5},{8,10},{9,11},{10,... | collective-permute-start | bytes 1572872 | tf_op jit(solution)/shard_map/ppermute | solution.py:653
  603.0 33.4 %collective-permute-start.2 = (bf16[64,4096]{1,0:T(8,128)(2,1)S(1)}, bf16[64,4096]{1,0:T(8,128)(2,1)S(1)}, u32[]{:S(2)}, u32[]{:S(2)}) collective-permute-start(bf16[64,4096]{1,0:T(8,128)(2,1)S(1)} %get-tuple-element.62), channel_id=1, source_target_pairs={{0,3},{1,0},{2,1},{3,2},{4,7},{5,4},{6,5},{7,6},{8,11},{9,8},{10,9... | collective-permute-start | bytes 1572872 | tf_op jit(solution)/shard_map/ppermute | solution.py:653
  615.4 21.1 %copy-start.24 = (bf16[64,4096]{1,0:T(8,128)(2,1)}, bf16[64,4096]{1,0:T(8,128)(2,1)S(1)}, u32[]{:S(2)}) copy-start(bf16[64,4096]{1,0:T(8,128)(2,1)S(1)} %collective-permute-done.refs_1_) | copy-start | bytes 1572868
  636.5 0.8 copy-start.25
  636.5 1.0 copy-start.26
  768.1 4.3 copy-start.23
  768.1 7.0 copy-start.19
Sparse Core Ops, SparseCore 0:
  9.9 82.8 all-gather.4
  107.4 142.7 all-gather.2
  442.0 147.3 reduce-scatter.2
  592.7 81.0 reduce-scatter.4

commit v4 on v3

--- a/solution.py
+++ b/solution.py
@@ -285,6 +285,159 @@
         dma((2, slots)),
         dma((wide // 2, slots)),
         dma((wide // 2, slots)),
+    ]
+
+
+class Reduce:
+    def __init__(self, wide, narrow, source, out_ref, refs):
+        self.wide, self.narrow, self.source, self.out_ref = wide, narrow, source, out_ref
+        self.w, self.n = lax.axis_index("wide"), lax.axis_index("narrow")
+        self.core, self.chip = lax.rem(self.w, 2), self.w // 2
+        self.chips = wide // 2
+        self.bits = self.chips.bit_length() - 1
+        (self.held, self.core_in, self.chip_in, self.z_in, self.load_sem, self.core_send, self.core_recv,
+         self.chip_send, self.chip_recv, self.z_send, self.z_recv) = refs
+        self.chunks = self.held.shape[0]
+        self.rows, self.chunk = self.held.shape[2:]
+        self.shard = self.rows // narrow
+        self.orders = [list(range(self.bits)), list(range(self.bits))[::-1]]
+
+    def columns_of(self, q):
+        return pl.ds(pl.multiple_of(q * self.chunk, self.chunk), self.chunk)
+
+    def begin(self, q):
+        pltpu.make_async_copy(
+            self.source.at[:, self.core, :, self.columns_of(q)], self.held.at[q], self.load_sem.at[q]
+        ).start()
+        pltpu.make_async_remote_copy(
+            src_ref=self.source.at[:, 1 - self.core, :, self.columns_of(q)],
+            dst_ref=self.core_in.at[q],
+            send_sem=self.core_send.at[q],
+            recv_sem=self.core_recv.at[q],
+            device_id={"wide": self.w ^ 1, "narrow": self.n},
+            device_id_type=MESH,
+        ).start()
+
+    def add_to(self, target, other):
+        def one(r, carry):
+            part = pl.ds(pl.multiple_of(r * 16, 16), 16)
+            target(part)[...] = (
+                target(part)[...].astype(F32) + other(part)[...].astype(F32)
+            ).astype(BF16)
+            return carry
+
+        lax.fori_loop(0, self.rows // 16, one, 0)
+
+    def tiles_of(self, h, stage):
+        order = self.orders[h]
+        rest = order[stage + 1 :]
+        offset = sum(self.chips >> (i + 1) for i in range(stage))
+        fixed = sum(1 << b for b in order[: stage + 1])
+        result = []
+        for v in range(1 << len(rest)):
+            extra = sum(((v >> i) & 1) << b for i, b in enumerate(rest))
+            result.append((offset + v, (self.chip & fixed) + extra))
+        return result
+
+    def lanes(self, h):
+        return pl.ds(h * (self.chunk // 2), self.chunk // 2)
+
+    def chip_copy(self, q, h, stage, slot, kept):
+        bit = self.orders[h][stage]
+        return pltpu.make_async_remote_copy(
+            src_ref=self.held.at[q, kept ^ (1 << bit), :, self.lanes(h)],
+            dst_ref=self.chip_in.at[q, h, slot],
+            send_sem=self.chip_send.at[q, h, slot],
+            recv_sem=self.chip_recv.at[q, h, slot],
+            device_id={"wide": self.w ^ (2 << bit), "narrow": self.n},
+            device_id_type=MESH,
+        )
+
+    def send_stage(self, q, stage):
+        for h in (0, 1):
+            for slot, kept in self.tiles_of(h, stage):
+                self.chip_copy(q, h, stage, slot, kept).start()
+
+    def after_core(self, q):
+        pltpu.make_async_copy(self.held.at[q], self.held.at[q], self.load_sem.at[q]).wait()
+        arrive(self.core_in.at[q], self.core_recv.at[q])
+        for k in range(self.chips):
+            self.add_to(
+                lambda part, k=k: self.held.at[q, k, part, :],
+                lambda part, k=k: self.core_in.at[q, k, part, :],
+            )
+        self.send_stage(q, 0)
+
+    def z_copy(self, q, step):
+        other = lax.rem(self.n + step, self.narrow)
+        own = pl.ds(pl.multiple_of(other * self.shard, self.shard), self.shard)
+        return pltpu.make_async_remote_copy(
+            src_ref=self.held.at[q, self.chip, own, :],
+            dst_ref=self.z_in.at[q, step],
+            send_sem=self.z_send.at[q, step],
+            recv_sem=self.z_recv.at[q, step],
+            device_id={"wide": self.w, "narrow": other},
+            device_id_type=MESH,
+        )
+
+    def after_stage(self, q, stage):
+        for h in (0, 1):
+            for slot, kept in self.tiles_of(h, stage):
+                arrive(self.chip_in.at[q, h, slot], self.chip_recv.at[q, h, slot])
+                self.add_to(
+                    lambda part, h=h, kept=kept: self.held.at[q, kept, part, self.lanes(h)],
+                    lambda part, h=h, slot=slot: self.chip_in.at[q, h, slot, part, :],
+                )
+        if stage + 1 < self.bits:
+            self.send_stage(q, stage + 1)
+        else:
+            for step in range(1, self.narrow):
+                self.z_copy(q, step).start()
+
+    def after_z(self, q):
+        for step in range(1, self.narrow):
+            arrive(self.z_in.at[q, step], self.z_recv.at[q, step])
+
+        def one(r, carry):
+            to = pl.ds(pl.multiple_of(r * 16, 16), 16)
+            own = pl.ds(pl.multiple_of(self.n * self.shard + r * 16, 16), 16)
+            value = self.held[q, self.chip, own, :].astype(F32)
+            for step in range(1, self.narrow):
+                value = value + self.z_in[q, step, to, :].astype(F32)
+            self.out_ref[to, self.columns_of(q)] = value
+            return carry
+
+        lax.fori_loop(0, self.shard // 16, one, 0)
+
+    def drain(self):
+        def one(q, carry):
+            arrive(self.core_in.at[q], self.core_send.at[q])
+            for stage in range(self.bits):
+                for h in (0, 1):
+                    for slot, kept in self.tiles_of(h, stage):
+                        self.chip_copy(q, h, stage, slot, kept).wait_send()
+            for step in range(1, self.narrow):
+                self.z_copy(q, step).wait_send()
+            return carry
+
+        lax.fori_loop(0, self.chunks, one, 0)
+
+
+def reduce_scratch(wide, narrow, source, chunk):
+    chips, rows, chunks = wide // 2, source.shape[2], source.shape[3] // chunk
+    dma = pltpu.SemaphoreType.DMA
+    return [
+        pltpu.VMEM((chunks, chips, rows, chunk), BF16),
+        pltpu.VMEM((chunks, chips, rows, chunk), BF16),
+        pltpu.VMEM((chunks, 2, chips - 1, rows, chunk // 2), BF16),
+        pltpu.VMEM((chunks, narrow, rows // narrow, chunk), BF16),
+        dma((chunks,)),
+        dma((chunks,)),
+        dma((chunks,)),
+        dma((chunks, 2, chips - 1)),
+        dma((chunks, 2, chips - 1)),
+        dma((chunks, narrow)),
+        dma((chunks, narrow)),
     ]
 
 
@@ -472,10 +625,11 @@
 
 def attend_back_kernel(
     wide, narrow, groups, start_ref, x_ref, mine_ref, full_ref, log_ref, cos_ref, sin_ref, part_ref,
-    out_ref, came_ref,
+    weight_ref, out_ref, came_ref, weight_out,
     keys, values, acc, acc_keys, acc_values, grad_ref, done, own_sem, in_send, in_recv,
-    q_send, q_recv, k_send, k_recv, p_send, p_recv,
+    q_send, q_recv, k_send, k_recv, p_send, p_recv, *refs,
 ):
+    reduce = Reduce(wide, narrow, weight_ref, weight_out, refs)
     me, n = lax.axis_index("wide"), lax.axis_index("narrow")
 
     def part_copy(step):
@@ -504,9 +658,25 @@
         to_owner(
             mine_ref.at[me ^ mask], grad_ref.at[me], in_send.at[mask], in_recv.at[me], mask
         ).start()
+    for q in range(reduce.chunks):
+        reduce.begin(q)
     own_part.start()
     for step in range(1, narrow):
         part_copy(step).start()
+
+    def weight_turn(c):
+        chunks = reduce.chunks
+        q = jnp.maximum(c - 2, 0) // 2
+        ready = (c >= 2) & (lax.rem(c, 2) == 0) & (q < chunks)
+        pl.when(ready)(lambda: reduce.after_core(jnp.minimum(q, chunks - 1)))
+        actions = [functools.partial(reduce.after_stage, stage=stage) for stage in range(reduce.bits)]
+        for index, action in enumerate(actions + [reduce.after_z]):
+            since = jnp.maximum(c - (2 * chunks + 6 + 6 * index), -1)
+            q = jnp.maximum(since, 0) // 5
+            ready = (since >= 0) & (lax.rem(jnp.maximum(since, 0), 5) == 0) & (q < chunks)
+            pl.when(ready)(functools.partial(action, jnp.minimum(q, chunks - 1)))
+
+    turns = 2 * reduce.chunks + 6 + 6 * reduce.bits + 5 * (reduce.chunks - 1) + 1
     key_row = lax.broadcasted_iota(jnp.int32, (rows, rows), 0)
     column = lax.broadcasted_iota(jnp.int32, (rows, rows), 1)
     own_in.wait()
@@ -553,6 +723,7 @@
                 grad_values = grad_values + dot(grad, prob.astype(BF16), NT)
             acc_keys[j] = grad_keys
             acc_values[j] = grad_values
+            weight_turn(i * (i + 1) // 2 + j)
             return carry
 
         lax.fori_loop(0, i + 1, step, 0)
@@ -590,6 +761,14 @@
 
     lax.fori_loop(0, blocks, last, 0)
     out_ref[me] = done[me]
+
+    def left(c, carry):
+        weight_turn(c)
+        return carry
+
+    lax.fori_loop(blocks * (blocks + 1) // 2, max(turns, blocks * (blocks + 1) // 2), left, 0)
+
+    reduce.drain()
     for mask in range(1, wide):
         other = me ^ mask
         arrive(mine_ref.at[other], in_send.at[mask])
@@ -602,7 +781,7 @@
         part_copy(step).wait()
 
 
-def attend_back(x, mine, full, log_total, start, cos, sin, part, groups):
+def attend_back(x, mine, full, log_total, start, cos, sin, part, weight, groups):
     wide, narrow = lax.axis_size("wide"), lax.axis_size("narrow")
     blocks, features, rows = x.shape
     width = groups * HEAD_DIM
@@ -614,9 +793,10 @@
         out_shape=(
             jax.ShapeDtypeStruct(x.shape, BF16),
             jax.ShapeDtypeStruct(part.shape, BF16),
+            jax.ShapeDtypeStruct((weight.shape[2] // narrow, weight.shape[3]), F32),
         ),
-        in_specs=[vmem] * 7 + [hbm],
-        out_specs=(vmem, hbm),
+        in_specs=[vmem] * 7 + [hbm, hbm],
+        out_specs=(vmem, hbm, vmem),
         scratch_shapes=[
             pltpu.VMEM((blocks, rows, HEAD_DIM), BF16),
             pltpu.VMEM((blocks, rows, HEAD_DIM), BF16),
@@ -628,16 +808,17 @@
             dma((1,)),
         ]
         + [dma((wide,))] * 6
-        + [dma((narrow,))] * 2,
+        + [dma((narrow,))] * 2
+        + reduce_scratch(wide, narrow, weight, 512),
         compiler_params=pltpu.CompilerParams(
-            collective_id=4, has_side_effects=True, vmem_limit_bytes=40 << 20
+            collective_id=4, has_side_effects=True, vmem_limit_bytes=50 << 20
         ),
         cost_estimate=pl.CostEstimate(
             flops=40 * width * (blocks * rows) ** 2,
             bytes_accessed=4 * x.size * 2,
             transcendentals=groups * (blocks * rows) ** 2 // 2,
         ),
-    )(start, x, mine, full, log_total, cos, sin, part)
+    )(start, x, mine, full, log_total, cos, sin, part, weight)
 
 
 def gather(x, axis):
@@ -646,15 +827,6 @@
 
 def scatter_sum(x, axis):
     return lax.psum_scatter(x, axis, scatter_dimension=0, tiled=True)
-
-
-def shift(x, step):
-    n = lax.axis_size("narrow")
-    return lax.ppermute(x, "narrow", [(i, (i + step) % n) for i in range(n)])
-
-
-def pick(x, index, axis):
-    return lax.dynamic_index_in_dim(x, index, axis, keepdims=False)
 
 
 def gather_kernel(wide, narrow, aligned, qkv_ref, cut_ref, qkv_all, cut_all, x_send, x_recv, x_own, *sems):
@@ -735,8 +907,8 @@
 
 def feed_kernel(
     narrow, x_ref, cot_ref, gate_up_ref, down_ref,
-    group_ref, hidden_out, grad_out, low_out, grad_x_ref,
-    gate_up, down, cot, hidden, grads, low, came,
+    low_out, grad_x_ref, part_gate_up, part_down,
+    group_ref, gate_up, down, cot, hidden, grads, low, came,
     load_sem, x_send, x_recv, out_sem, g_send, g_recv,
 ):
     w, n = lax.axis_index("wide"), lax.axis_index("narrow")
@@ -791,12 +963,8 @@
         block = group_ref.at[owner_of(side, d)]
         pltpu.make_async_copy(block, block, x_recv.at[side, d]).wait()
 
-    def out_copies(at, block):
-        return [
-            pltpu.make_async_copy(hidden.at[at], hidden_out.at[block], out_sem.at[at, 0]),
-            pltpu.make_async_copy(grads.at[at], grad_out.at[block], out_sem.at[at, 1]),
-            pltpu.make_async_copy(low.at[at], low_out.at[block], out_sem.at[at, 2]),
-        ]
+    def out_copy(at, block):
+        return pltpu.make_async_copy(low.at[at], low_out.at[block], out_sem.at[at])
 
     def g_copy(block):
         return pltpu.make_async_remote_copy(
@@ -814,10 +982,7 @@
         before = jnp.where(d == 0, 0, before + jnp.where((side == 1) & (n - d >= 0), 1, 0))
         at = lax.rem(before, 2)
 
-        @pl.when(before >= 2)
-        def _():
-            for copy in out_copies(at, block):
-                copy.wait()
+        pl.when(before >= 2)(lambda: out_copy(at, block).wait())
 
         def first(f, carry):
             columns = pl.ds(pl.multiple_of(f * tile, tile), tile)
@@ -828,22 +993,21 @@
             grad = dot(cot[block], down[columns, :], NT)
             sig = 1.0 / (1.0 + jnp.exp(-gate))
             silu = gate * sig
-            hidden[at, :, columns] = (silu * up).astype(BF16)
-            grads[at, :, columns] = (grad * up * (sig + silu * (1.0 - sig))).astype(BF16)
-            grads[at, :, other] = (grad * silu).astype(BF16)
+            hidden[block, :, columns] = (silu * up).astype(BF16)
+            grads[block, :, columns] = (grad * up * (sig + silu * (1.0 - sig))).astype(BF16)
+            grads[block, :, other] = (grad * silu).astype(BF16)
             return carry
 
         lax.fori_loop(0, tiles, first, 0)
 
         def second(f, carry):
             columns = pl.ds(pl.multiple_of(f * tile, tile), tile)
-            cot[block, :, columns] = dot(grads[at], gate_up[columns, :], NT, BF16)
-            low[at, :, columns] = dot(hidden[at], down[:, columns], NN, BF16)
+            cot[block, :, columns] = dot(grads[block], gate_up[columns, :], NT, BF16)
+            low[at, :, columns] = dot(hidden[block], down[:, columns], NN, BF16)
             return carry
 
         lax.fori_loop(0, wtiles, second, 0)
-        for copy in out_copies(at, block):
-            copy.start()
+        out_copy(at, block).start()
         pl.when(block != n)(lambda: g_copy(block).start())
 
     def distance(d, carry):
@@ -873,9 +1037,61 @@
     loads[3].wait()
     lax.fori_loop(0, narrow, distance, 0)
 
-    for at in range(min(2, narrow)):
-        for copy in out_copies(at, n):
-            copy.wait()
+    tokens = narrow * rows
+    again = [
+        pltpu.make_async_copy(
+            cot_ref.at[o], gate_up.at[pl.ds(o * rows, rows), pl.ds(0, width)], load_sem.at[4 + o]
+        )
+        for o in range(narrow)
+    ]
+    for load in again:
+        load.start()
+    for at in range(2):
+        out_copy(at, n).wait()
+
+    def flipped(ref, columns):
+        return jnp.concatenate([ref[o, :, columns].T for o in range(narrow)], 1)
+
+    def weight_tile(t, left, right, at_row, out_ref, first):
+        at = lax.rem(t, 2)
+        copy = pltpu.make_async_copy(low.at[at], out_ref, out_sem.at[at])
+        pl.when(t >= 2)(lambda: copy.wait())
+        turned = flipped(left, pl.ds(pl.multiple_of(at_row, tile), tile))
+
+        def one(c, carry):
+            columns = pl.ds(pl.multiple_of(c * 512, 512), 512)
+            source = pl.ds(pl.multiple_of(first + c * 512, 512), 512)
+            low[at, :, columns] = dot(turned, right(source), NN, BF16)
+            return carry
+
+        lax.fori_loop(0, width // 512, one, 0)
+        copy.start()
+
+    halves = 2 * own // width
+
+    def gate_up_tile(t, carry):
+        row, half = t // halves * tile, lax.rem(t, halves) * width
+        row, half = pl.multiple_of(row, tile), pl.multiple_of(half, width)
+        weight_tile(
+            t, group_ref, lambda source: grads[:, :, source].reshape(tokens, 512), row,
+            part_gate_up.at[pl.ds(row, tile), pl.ds(half, width)], half,
+        )
+        return carry
+
+    def down_tile(t, carry):
+        row = pl.multiple_of(t * tile, tile)
+        weight_tile(
+            t + 2, hidden, lambda source: gate_up[pl.ds(0, tokens), source], row,
+            part_down.at[pl.ds(row, tile), :], 0,
+        )
+        return carry
+
+    lax.fori_loop(0, wtiles * halves, gate_up_tile, 0)
+    for load in again:
+        load.wait()
+    lax.fori_loop(0, tiles, down_tile, 0)
+    for at in range(2):
+        out_copy(at, n).wait()
     for side in (0, 1):
         for d in range(narrow - 1):
             pl.when(passes(side, d))(lambda side=side, d=d: x_copy(side, d).wait_send())
@@ -903,29 +1119,29 @@
     dma = pltpu.SemaphoreType.DMA
     hbm = pl.BlockSpec(memory_space=pl.ANY)
     vmem = pl.BlockSpec(memory_space=pltpu.VMEM)
-    group, hidden, grads, low, grad_x = pl.pallas_call(
+    return pl.pallas_call(
         functools.partial(feed_kernel, narrow),
         out_shape=(
             jax.ShapeDtypeStruct((narrow, rows, width), BF16),
-            jax.ShapeDtypeStruct((narrow, rows, own), BF16),
-            jax.ShapeDtypeStruct((narrow, rows, 2 * own), BF16),
-            jax.ShapeDtypeStruct((narrow, rows, width), BF16),
             jax.ShapeDtypeStruct((rows, width), F32),
+            jax.ShapeDtypeStruct((width, 2 * own), BF16),
+            jax.ShapeDtypeStruct((own, width), BF16),
         ),
         in_specs=[vmem, hbm, hbm, hbm],
-        out_specs=(vmem, hbm, hbm, hbm, vmem),
+        out_specs=(hbm, vmem, hbm, hbm),
         scratch_shapes=[
+            pltpu.VMEM((narrow, rows, width), BF16),
             pltpu.VMEM((width, 2 * own), BF16),
             pltpu.VMEM((own, width), BF16),
             pltpu.VMEM((narrow, rows, width), BF16),
-            pltpu.VMEM((2, rows, own), BF16),
-            pltpu.VMEM((2, rows, 2 * own), BF16),
+            pltpu.VMEM((narrow, rows, own), BF16),
+            pltpu.VMEM((narrow, rows, 2 * own), BF16),
             pltpu.VMEM((2, rows, width), BF16),
             pltpu.VMEM((narrow, rows, width), BF16),
-            dma((4,)),
+            dma((4 + narrow,)),
             dma((2, narrow + 1)),
             dma((2, narrow + 1)),
-            dma((2, 3)),
+            dma((2,)),
             dma((narrow,)),
             dma((narrow,)),
         ],
@@ -936,30 +1152,16 @@
             flops=12 * narrow * rows * width * own, bytes_accessed=300 << 20, transcendentals=0
         ),
     )(x, cot_group.reshape(narrow, rows, width), gate_up, down)
-    flat = lambda y: y.reshape((-1,) + y.shape[2:])
-    return flat(group), flat(hidden), flat(grads), flat(low), grad_x
 
 
 def sum_kernel(
-    wide, narrow, chunk, wout_ref, qkv_ref, gains_ref, *refs
+    wide, narrow, qkv_ref, cut_ref, gains_ref, qkv_out, cut_out, gains_out,
+    cut_in, gain_w, gain_sum, gain_z, own_sem, cut_send, cut_recv, gw_send, gw_recv, gz_send, gz_recv, *refs,
 ):
-    cut_refs, refs = refs[:narrow], refs[narrow:]
-    (
-        wout_out, qkv_out, cut_out, gains_out,
-        held, core_in, chip_in, z_in, gain_w, gain_sum, gain_z,
-        load_sem, core_send, core_recv, chip_send, chip_recv, z_send, z_recv,
-        gw_send, gw_recv, gz_send, gz_recv,
-    ) = refs
-    w, n = lax.axis_index("wide"), lax.axis_index("narrow")
-    core, chip = lax.rem(w, 2), w // 2
-    chips = wide // 2
-    bits = chips.bit_length() - 1
-    rows = held.shape[2]
-    shard = rows // narrow
-    half = chunk // 2
-    first_chunks = wout_ref.shape[3] // chunk
-    chunks = first_chunks + qkv_ref.shape[3] // chunk
-    orders = [list(range(bits)), list(range(bits))[::-1]]
+    reduce = Reduce(wide, narrow, qkv_ref, qkv_out, refs)
+    w, n = reduce.w, reduce.n
+    chunks, bits = reduce.chunks, reduce.bits
+    greet(wide, narrow)
 
     def to_wide(mask):
         return {"wide": w ^ mask, "narrow": n}
@@ -967,149 +1169,17 @@
     def to_narrow(step):
         return {"wide": w, "narrow": lax.rem(n + step, narrow)}
 
-    barrier = pltpu.get_barrier_semaphore()
-    for mask in range(1, wide):
-        pl.semaphore_signal(barrier, inc=1, device_id=to_wide(mask), device_id_type=MESH)
-    for step in range(1, narrow):
-        pl.semaphore_signal(barrier, inc=1, device_id=to_narrow(step), device_id_type=MESH)
-    pl.semaphore_wait(barrier, wide - 1 + narrow - 1)
-
-    def columns_of(q):
-        return pl.ds(pl.multiple_of(q * chunk, chunk), chunk)
-
-    def copies_from(ref, q, at):
-        load = pltpu.make_async_copy(
-            ref.at[:, core, :, columns_of(at)], held.at[q], load_sem.at[q]
-        )
-        send = pltpu.make_async_remote_copy(
-            src_ref=ref.at[:, 1 - core, :, columns_of(at)],
-            dst_ref=core_in.at[q],
-            send_sem=core_send.at[q],
-            recv_sem=core_recv.at[q],
-            device_id=to_wide(1),
-            device_id_type=MESH,
-        )
-        return load, send
-
-    def begin(q):
-        @pl.when(q < first_chunks)
-        def _():
-            for copy in copies_from(wout_ref, q, q):
-                copy.start()
-
-        @pl.when(q >= first_chunks)
-        def _():
-            for copy in copies_from(qkv_ref, q, jnp.maximum(q - first_chunks, 0)):
-                copy.start()
-
-    def add_to(target, other, size):
-        def one(r, carry):
-            part = pl.ds(pl.multiple_of(r * 16, 16), 16)
-            target(part)[...] = (
-                target(part)[...].astype(F32) + other(part)[...].astype(F32)
-            ).astype(BF16)
-            return carry
-
-        lax.fori_loop(0, size // 16, one, 0)
-
-    def tiles_of(h, stage):
-        order = orders[h]
-        rest = order[stage + 1 :]
-        offset = sum(chips >> (i + 1) for i in range(stage))
-        fixed = sum(1 << b for b in order[: stage + 1])
-        result = []
-        for v in range(1 << len(rest)):
-            extra = sum(((v >> i) & 1) << b for i, b in enumerate(rest))
-            result.append((offset + v, (chip & fixed) + extra))
-        return result
-
-    def lanes(h):
-        return pl.ds(h * half, half)
-
-    def chip_copy(q, h, stage, slot, kept):
-        bit = orders[h][stage]
+    own_cut = pltpu.make_async_copy(cut_ref.at[n], cut_in.at[n], own_sem)
+
+    def cut_copy(step):
         return pltpu.make_async_remote_copy(
-            src_ref=held.at[q, kept ^ (1 << bit), :, lanes(h)],
-            dst_ref=chip_in.at[q, h, slot],
-            send_sem=chip_send.at[q, h, slot],
-            recv_sem=chip_recv.at[q, h, slot],
-            device_id=to_wide(2 << bit),
-            device_id_type=MESH,
-        )
-
-    def send_stage(q, stage):
-        for h in (0, 1):
-            for slot, kept in tiles_of(h, stage):
-                chip_copy(q, h, stage, slot, kept).start()
-
-    def z_copy(q, step):
-        other = lax.rem(n + step, narrow)
-        return pltpu.make_async_remote_copy(
-            src_ref=held.at[q, chip, pl.ds(pl.multiple_of(other * shard, shard), shard), :],
-            dst_ref=z_in.at[q, step],
-            send_sem=z_send.at[q, step],
-            recv_sem=z_recv.at[q, step],
+            src_ref=cut_ref.at[lax.rem(n + step, narrow)],
+            dst_ref=cut_in.at[n],
+            send_sem=cut_send.at[step],
+            recv_sem=cut_recv.at[step],
             device_id=to_narrow(step),
             device_id_type=MESH,
         )
-
-    def after_core(q):
-        load, _ = copies_from(wout_ref, q, 0)
-        load.wait()
-        pltpu.make_async_copy(core_in.at[q], core_in.at[q], core_recv.at[q]).wait()
-        for k in range(chips):
-            add_to(
-                lambda part, k=k: held.at[q, k, part, :],
-                lambda part, k=k: core_in.at[q, k, part, :],
-                rows,
-            )
-        send_stage(q, 0)
-
-    def after_stage(q, stage):
-        for h in (0, 1):
-            for slot, kept in tiles_of(h, stage):
-                block = chip_in.at[q, h, slot]
-                pltpu.make_async_copy(block, block, chip_recv.at[q, h, slot]).wait()
-                add_to(
-                    lambda part, h=h, kept=kept: held.at[q, kept, part, lanes(h)],
-                    lambda part, h=h, slot=slot: chip_in.at[q, h, slot, part, :],
-                    rows,
-                )
-        if stage + 1 < bits:
-            send_stage(q, stage + 1)
-        else:
-            for step in range(1, narrow):
-                z_copy(q, step).start()
-
-    def after_z(q):
-        for step in range(1, narrow):
-            block = z_in.at[q, step]
-            pltpu.make_async_copy(block, block, z_recv.at[q, step]).wait()
-
-        def total(r):
-            part = pl.ds(pl.multiple_of(n * shard + r * 16, 16), 16)
-            value = held[q, chip, part, :].astype(F32)
-            for step in range(1, narrow):
-                value = value + z_in[q, step, pl.ds(pl.multiple_of(r * 16, 16), 16), :].astype(F32)
-            return value
-
-        @pl.when(q < first_chunks)
-        def _():
-            def one(r, carry):
-                to = pl.ds(pl.multiple_of(r * 16, 16), 16)
-                wout_out[to, columns_of(jnp.minimum(q, first_chunks - 1))] = total(r)
-                return carry
-
-            lax.fori_loop(0, shard // 16, one, 0)
-
-        @pl.when(q >= first_chunks)
-        def _():
-            def one(r, carry):
-                to = pl.ds(pl.multiple_of(r * 16, 16), 16)
-                qkv_out[to, columns_of(jnp.maximum(q - first_chunks, 0))] = total(r)
-                return carry
-
-            lax.fori_loop(0, shard // 16, one, 0)
 
     def gw_copy(mask):
         return pltpu.make_async_remote_copy(
@@ -1131,30 +1201,23 @@
             device_id_type=MESH,
         )
 
-    ahead = min(3, chunks)
+    ahead = min(4, chunks)
     for q in range(ahead):
-        begin(q)
+        reduce.begin(q)
+    own_cut.start()
+    for step in range(1, narrow):
+        cut_copy(step).start()
     for mask in range(1, wide):
         gw_copy(mask).start()
-    piece = cut_refs[0].shape[1] // (2 * wide)
-    for step in range(narrow):
-        if cut_out.shape[0] == narrow:
-            cut_out[lax.rem(n + narrow - step, narrow)] = cut_refs[step][...].astype(F32)
-            continue
-        for j in range(2 * wide):
-            at = (j * narrow + lax.rem(n + narrow - step, narrow)) * piece
-            cut_out[:, pl.ds(pl.multiple_of(at, piece), piece)] = cut_refs[step][
-                :, pl.ds(j * piece, piece)
-            ].astype(F32)
 
     def turn(t, carry):
-        pl.when(t + ahead < chunks)(lambda: begin(t + ahead))
-        pl.when(t < chunks)(lambda: after_core(t))
+        pl.when(t + ahead < chunks)(lambda: reduce.begin(t + ahead))
+        pl.when(t < chunks)(lambda: reduce.after_core(t))
         for stage in range(bits):
             q = t - 1 - stage
-            pl.when((q >= 0) & (q < chunks))(lambda q=q, stage=stage: after_stage(q, stage))
+            pl.when((q >= 0) & (q < chunks))(functools.partial(reduce.after_stage, q, stage))
         q = t - 1 - bits
-        pl.when(q >= 0)(lambda: after_z(q))
+        pl.when(q >= 0)(lambda: reduce.after_z(q))
         return carry
 
     lax.fori_loop(0, chunks + bits + 1, turn, 0)
@@ -1168,6 +1231,21 @@
     for step in range(1, narrow):
         gz_copy(step).start()
 
+    own_cut.wait()
+    for step in range(1, narrow):
+        other = lax.rem(n + narrow - step, narrow)
+        arrive(cut_in.at[other], cut_recv.at[step])
+    piece = cut_in.shape[2] // (2 * wide)
+    if cut_out.shape[0] == narrow:
+        for other in range(narrow):
+            cut_out[other] = cut_in[other].astype(F32)
+    else:
+        for j in range(2 * wide):
+            for other in range(narrow):
+                cut_out[:, pl.ds((j * narrow + other) * piece, piece)] = cut_in[
+                    other, :, pl.ds(j * piece, piece)
+                ].astype(F32)
+
     total = gain_sum[n]
     for step in range(1, narrow):
         block = gain_z.at[step]
@@ -1179,67 +1257,46 @@
         gw_copy(mask).wait_send()
     for step in range(1, narrow):
         gz_copy(step).wait_send()
-
-    def drain(q, carry):
-        _, send = copies_from(wout_ref, q, 0)
-        send.wait_send()
-        for stage in range(bits):
-            for h in (0, 1):
-                for slot, kept in tiles_of(h, stage):
-                    chip_copy(q, h, stage, slot, kept).wait_send()
-        for step in range(1, narrow):
-            z_copy(q, step).wait_send()
-        return carry
-
-    lax.fori_loop(0, chunks, drain, 0)
-
-
-def sum_all(wout, qkv, cuts, gains):
+        cut_copy(step).wait_send()
+    reduce.drain()
+
+
+def sum_all(qkv, cut, gains):
     wide, narrow = lax.axis_size("wide"), lax.axis_size("narrow")
-    chips, _, rows, _ = wout.shape
-    chunk = 512
-    chunks = (wout.shape[3] + qkv.shape[3]) // chunk
-    shard, cut_width = cuts[0].shape
+    shard, cut_width = cut.shape[1:]
     aligned = (cut_width // (2 * wide)) % 128 == 0
-    cut_shape = (shard, narrow * cut_width) if aligned else (narrow, shard, cut_width)
+    cut_shape = (shard, narrow * cut_width) if aligned else cut.shape
     dma = pltpu.SemaphoreType.DMA
     hbm = pl.BlockSpec(memory_space=pl.ANY)
     vmem = pl.BlockSpec(memory_space=pltpu.VMEM)
     results = pl.pallas_call(
-        functools.partial(sum_kernel, wide, narrow, chunk),
+        functools.partial(sum_kernel, wide, narrow),
         out_shape=(
-            jax.ShapeDtypeStruct((shard, wout.shape[3]), F32),
             jax.ShapeDtypeStruct((shard, qkv.shape[3]), F32),
             jax.ShapeDtypeStruct(cut_shape, F32),
             jax.ShapeDtypeStruct((8, 128), F32),
         ),
-        in_specs=[hbm, hbm, vmem] + [vmem] * narrow,
-        out_specs=(vmem, vmem, vmem, vmem),
+        in_specs=[hbm, hbm, vmem],
+        out_specs=(vmem, vmem, vmem),
         scratch_shapes=[
-            pltpu.VMEM((chunks, chips, rows, chunk), BF16),
-            pltpu.VMEM((chunks, chips, rows, chunk), BF16),
-            pltpu.VMEM((chunks, 2, chips - 1, rows, chunk // 2), BF16),
-            pltpu.VMEM((chunks, narrow, shard, chunk), BF16),
+            pltpu.VMEM(cut.shape, BF16),
             pltpu.VMEM((wide, narrow, 8, 128), F32),
             pltpu.VMEM((narrow, 8, 128), F32),
             pltpu.VMEM((narrow, 8, 128), F32),
-            dma((chunks,)),
-            dma((chunks,)),
-            dma((chunks,)),
-            dma((chunks, 2, chips - 1)),
-            dma((chunks, 2, chips - 1)),
-            dma((chunks, narrow)),
-            dma((chunks, narrow)),
+            dma(()),
+            dma((narrow,)),
+            dma((narrow,)),
             dma((wide,)),
             dma((wide,)),
             dma((narrow,)),
             dma((narrow,)),
-        ],
+        ]
+        + reduce_scratch(wide, narrow, qkv, 256),
         compiler_params=pltpu.CompilerParams(
             collective_id=2, has_side_effects=True, vmem_limit_bytes=54 << 20
         ),
         cost_estimate=pl.CostEstimate(flops=0, bytes_accessed=300 << 20, transcendentals=0),
-    )(wout, qkv, gains, *cuts)
+    )(qkv, cut, gains)
     return results, aligned
 
 
@@ -1292,27 +1349,22 @@
     unit_two = middle * scale_two
     normed_two = (unit_two * gain_two).astype(BF16)
 
-    normed_group, hidden, grad_gate_up, low_part, grad_normed_two = feed(
+    low_part, grad_normed_two, part_gateup, part_down = feed(
         normed_two, cot_group, gateup_own, down_own
     )
-    part_gateup = dot(normed_group, grad_gate_up, TN, BF16)
-    hidden, part_gateup = lax.optimization_barrier((hidden, part_gateup))
     grad_gateup = scatter_sum(part_gateup, "wide").reshape(narrow, shard, 2 * own_ff)
-    grad_down = scatter_sum(dot(hidden, cot_group, TN, BF16), "wide")
-    me = lax.axis_index("narrow")
-    cuts = [pick(grad_gateup, me, 0)]
-    for step in range(1, narrow):
-        cuts.append(shift(pick(grad_gateup, (me + step) % narrow, 0), step))
-
+    grad_down = scatter_sum(part_down, "wide")
     part_gain_two = jnp.sum(grad_normed_two * unit_two, 0)
     grad_middle = cotangent[0].astype(F32) + norm_back(
         grad_normed_two * gain_two, unit_two, scale_two
     )
     grad_branch = grad_middle.astype(BF16)
     grad_attended = dot(out_whole, grad_branch, NT, BF16).reshape(wide, groups * HEAD_DIM, rows)
-    grad_heads, low_came = attend_back(
-        heads, grad_attended, attended_full, log_total, start, cos_all, sin_all,
-        low_part.reshape(narrow, rows, width), groups,
+    cut = (wide // 2, 2, narrow * shard, -1)
+    part_wout = dot(attended_low, grad_branch, NN, BF16).reshape(cut)
+    grad_heads, low_came, grad_wout = attend_back(
+        heads, grad_attended, attended_full, log_total, start, cos_all, sin_all, low_part, part_wout,
+        groups,
     )
     layer_out = (middle + jnp.sum(low_came.astype(F32), 0)).astype(BF16)[None]
     grad_queries = grad_heads[:, : groups * HEAD_DIM].reshape(query_width, rows)
@@ -1337,19 +1389,15 @@
     part_gains = jnp.pad(
         part_gains.transpose(1, 2, 0, 3), ((0, 0), (0, 0), (0, 6), (0, 128 - shard))
     )
-    cut = (wide // 2, 2, narrow * shard, -1)
-    part_wout = dot(attended_low, grad_branch, NN, BF16).reshape(cut)
     part_qkv = dot(normed_one, grad_projected, (((0,), (1,)), ((), ())), BF16).reshape(cut)
-    (grad_wout, grad_qkv, grad_gateup, grad_gains), done = sum_all(
-        part_wout, part_qkv, cuts, part_gains
-    )
+    (grad_qkv, grad_gateup, grad_gains), done = sum_all(part_qkv, grad_gateup, part_gains)
     if not done:
         grad_gateup = (
             grad_gateup.reshape(narrow, shard, 2, wide, -1)
             .transpose(1, 2, 3, 0, 4)
             .reshape(shard, 2 * FF)
         )
-    (grad_down, grad_wout) = lax.optimization_barrier((grad_down, grad_wout))
+    grad_down, grad_gains = lax.optimization_barrier((grad_down, grad_gains))
     grad_down = grad_down.astype(F32)
     grad_inputs = grad_middle + norm_back(grad_normed_one * gain_one, unit_one, scale_one)
     grad_tokens = grad_inputs.astype(BF16)[None]

time: 793 us -> 756 us (0.953); the launches traced: 784 us -> 756 us
  Pallas kernels: 594 us -> 658 us
  matrix products: 87.2 us -> 41.6 us
  waiting for transfers between devices: 35.7 us -> 7.65 us
  starting transfers between devices: 11.4 us -> 0.34 us
    pallas_call x1, Pallas kernels: 82.3 us -> 142 us  [attend_back(): pl.pallas_call(functools.partial(attend_back_kernel, wide, narrow, groups...]
    dot_general x8 -> x6, matrix products: 87.2 us -> 41.6 us  [dot(): lax.dot_general(left, right, dims, preferred_element_type=F32).astype(kind)]
    ppermute x3 -> x0, waiting for transfers between devices: 26.6 us -> none  [shift(): return lax.ppermute(x, 'narrow', [(i, (i + step) % n) for i in range(n)])]
    pallas_call x1, Pallas kernels: 150 us -> 163 us  [feed(): pl.pallas_call(functools.partial(feed_kernel, narrow), out_shape=(jax.Sha...]
    ppermute x3 -> x0, starting transfers between devices: 11.2 us -> none  [shift(): return lax.ppermute(x, 'narrow', [(i, (i + step) % n) for i in range(n)])]
    pallas_call x1, Pallas kernels: 131 us -> 121 us  [sum_all(): pl.pallas_call(functools.partial(sum_kernel, wide, narrow), out_shape=(ja...]
  transfers between devices with their start and end apart: 7 -> 4, of which waited for: 3 -> 1; matrix products, arithmetic and copies ran while one was open for 11% -> 8% of each run, Pallas kernels for 57% -> 65%
where the time goes in v4:
time: 756 us
  Pallas kernels  658 us (87%)
  matrix products  41.6 us (6%)
  other arithmetic  22.3 us (3%)
  between operations  14.2 us (2%)
  local copies, waits for them, and re-layouts  12.1 us (2%)
  waiting for transfers between devices  7.65 us (1%)
    pallas_call x1, Pallas kernels, feed(): pl.pallas_call(functools.partial(feed_kernel, narrow), out_shape=(jax.Sha...  163 us
    pallas_call x1, Pallas kernels, attend_back(): pl.pallas_call(functools.partial(attend_back_kernel, wide, narrow, groups...  142 us
    pallas_call x1, Pallas kernels, attend(): pl.pallas_call(functools.partial(attend_kernel, wide, narrow, groups), ou...  135 us
    pallas_call x1, Pallas kernels, sum_all(): pl.pallas_call(functools.partial(sum_kernel, wide, narrow), out_shape=(ja...  121 us
    pallas_call x1, Pallas kernels, gather_weights(): pl.pallas_call(functools.partial(gather_kernel, wide, narrow, aligned), o...  96.7 us
    dot_general x6, matrix products, dot(): lax.dot_general(left, right, dims, preferred_element_type=F32).astype(kind)  41.6 us
  transfers between devices with their start and end apart: 4, of which 1 were waited for; matrix products, arithmetic and copies ran while one was open for 8% of the time, Pallas kernels for 65%

profile of v4, /device:TPU:0, one launch (start us, length us, event | category | flops | bytes accessed | tf_op | source)
XLA Modules:
  0.0 756.0 jit_solution(9728720151923184169)
XLA Ops:
  7.2 0.7 all-gather.5.cloned.1.call-update
  7.9 0.7 pad_maximum_fusion.5
  8.6 0.1 copy.22
  8.7 1.8 fusion.25.qkv_ref
  10.5 96.7 %shard_map.152 = (bf16[2048,3200]{1,0:T(8,128)(2,1)}, bf16[256,4096]{1,0:T(8,128)(2,1)}) custom-call(bf16[64,3200]{1,0:T(8,128)(2,1)} %fusion.25.qkv_ref, bf16[64,16384]{1,0:T(8,128)(2,1)} %cut_ref.1), custom_call_target="tpu_custom_call" | custom-call | bytes 209715200 | tf_op jit(solution)/shard_map/pallas_call | solution.py:894
  107.3 1.9 convert_reduce_fusion.1
  109.2 0.3 fusion.18
  109.5 7.6 %fusion.2 = f32[3072,256]{1,0:T(8,128)S(1)} fusion(bf16[2048,3200]{1,0:T(8,128)(2,1)} %get-tuple-element.28, bf16[1,256,2048]{2,1,0:T(8,128)(2,1)S(1)} %copy-done.10, f32[2048]{0:T(1024)S(1)} %get-tuple-element.49, f32[256]{0:T(256)S(1)} %add_rsqrt_fusion.1), kind=kOutput, calls=%fused_computation.3 | convolution fusion | flops 3223322624 | bytes 16786432 | tf_op jit(solution)/shard_map/dot_general | solution.py:28
  117.1 1.7 slice.62
  118.8 0.2 reduce-window.4
  119.0 0.1 convert_reduce_fusion.3
  119.2 0.1 select_reduce_fusion
  119.3 0.1 broadcast_multiply_fusion
  119.4 0.1 dynamic-slice_cosine_fusion
  119.5 2.1 multiply_subtract_fusion
  121.6 0.3 fusion.10
  122.0 0.1 pad_maximum_fusion.mine_ref
  122.1 1.1 copy-done
  123.2 134.9 %shard_map.153 = (bf16[8,384,256]{2,1,0:T(8,128)(2,1)S(1)}, bf16[8,256,256]{2,1,0:T(8,128)(2,1)S(1)}, f32[8,256,256]{2,1,0:T(8,128)S(1)}, f32[8,4,256]{2,1,0:T(4...) custom-call(s32[8,1,256]{2,1,0:T(1,128)S(1)} %bitcast.53, ...), custom_call_target="tpu_custom_call" | custom-call | flops 34359738368 | bytes 67108864 | tf_op jit(solution)/shard_map/pallas_call | solution.py:587
  258.1 8.6 %multiply_reduce_fusion.2 = (f32[256]{0:T(256)S(1)}, f32[256,2048]{1,0:T(8,128)S(1)}) fusion(bf16[2048,256]{1,0:T(8,128)(2,1)S(1)} %bitcast.50, bf16[2048,2048]{1,0:T(8,128)(2,1)} %get-tuple-element.30, bf16[1,256,2048]{2,1,0:T(8,128)(2,1)S(1)} %copy-done.10), kind=kOutput, calls=%fused_computation.33 | convolution fusion | flops 2149580544 | bytes 12583936 | tf_op jit(solution)/shard_map/dot_general | solution.py:28
  266.7 1.3 copy-done.5
  268.0 1.2 multiply_convert_fusion.x_ref
  269.2 163.4 %shard_map.154 = (bf16[4,256,2048]{2,1,0:T(8,128)(2,1)}, f32[256,2048]{1,0:T(8,128)}, bf16[2048,4096]{1,0:T(8,128)(2,1)}, bf16[2048,2048]{1,0:T(8,128)(2,1)}) custom-call(bf16[256,2048]{1,0:T(8,128)(2,1)} %multiply_convert_fusion.x_ref, bf16[4,256,2048]{2,1,0:T(8,128)(2,1)} %copy-done.2, bf16[2048,4096]{1,0:T(8,128)(2,1)} %all-gather.3.cloned.1.call-done.gate_up_ref, ...), custom_call_target="tpu_custom_call" | custom-call | flops 51539607552 | bytes 314572800 | tf_op jit(solution)/shard_map/pallas_call | solution.py:1122
  432.7 0.2 reduce-scatter.3.cloned.1.call-start
  432.9 0.3 reduce-scatter.3.cloned.1.call-update
  433.3 1.0 multiply_sine_fusion
  434.3 2.9 multiply_reduce_fusion
  437.2 0.5 copy-done.11
  437.7 0.6 multiply_add_fusion
  438.3 5.6 convolution_convert_fusion.1
  443.9 2.4 convolution_convert_fusion.2
  446.3 141.7 %shard_map.155 = (bf16[8,384,256]{2,1,0:T(8,128)(2,1)S(1)}, bf16[4,256,2048]{2,1,0:T(8,128)(2,1)}, f32[64,2048]{1,0:T(8,128)S(1)}) custom-call(s32[8,1,256]{2,1,0:T(1,128)S(1)} %bitcast.54, bf16[8,384,256]{2,1,0:T(8,128)(2,1)} %copy-done.4, bf16[8,256,256]{2,1,0:T(8,128)(2,1)S(1)} %bitcast.55, f32[8,256,256]{2,1,0:T(8,128)} %copy-done.3, ...), custom_call_target="tpu_custom_call" | custom-call | flops 42949672960 | bytes 6291456 | tf_op jit(solution)/shard_map/pallas_call | solution.py:791
  588.3 0.5 copy-done.16
  588.8 9.6 %fusion.17 = (f32[2048]{0:T(1024)S(1)}, f32[256]{0:T(256)S(1)}, f32[256,2048]{1,0:T(8,128)}) fusion(bf16[1,256,2048]{2,1,0:T(8,128)(2,1)S(1)} %copy-done.10, f32[256]{0:T(256)S(1)} %copy-done.18, f32[2048]{0:T(1024)S(1)} %copy-done.16, bf16[2048,3200]{1,0:T(8,128)(2,1)} %get-tuple-element.28, bf16[512,256]{1,0:T(8,128)(2,1)S(1)} %bitcast.68, ...), kind=kOutput, calls=%fused_computation.26 | convolution fusion | flops 3229611776 | bytes 17319936 | tf_op jit(solution)/shard_map/dot_general | solution.py:28
  598.4 0.1 stack.27
  598.5 0.1 stack.28
  598.6 0.7 pad.9.gains_ref
  599.3 3.7 convert_reduce_fusion
  603.0 0.6 copy-done.13
  603.7 2.3 fusion.19
  605.9 7.9 %convolution_convert_fusion = bf16[2048,3072]{1,0:T(8,128)(2,1)} fusion(bf16[512,256]{1,0:T(8,128)(2,1)S(1)} %bitcast.69, bf16[512,256]{1,0:T(8,128)(2,1)S(1)} %bitcast.67, bf16[2048,256]{1,0:T(8,128)(2,1)S(1)} %bitcast.63, bf16[1,256,2048]{2,1,0:T(8,128)(2,1)S(1)} %copy-done.10, f32[2048]{0:T(1024)S(1)} %copy-done.16, f32[256]{0:T(256)S(1)} %copy-done.18), kind=kOutput, calls=%fused_computation | convolution fusion | flops 3234332672 | bytes 15213568 | tf_op jit(solution)/shard_map/dot_general | solution.py:28
  613.8 6.6 reduce-scatter.5.cloned.1.call-done
  620.4 121.1 %shard_map.156 = (f32[64,3072]{1,0:T(8,128)}, f32[64,16384]{1,0:T(8,128)}, f32[8,128]{1,0:T(8,128)}) custom-call(bf16[4,2,256,3072]{3,2,1,0:T(8,128)(2,1)} %bitcast.56, bf16[4,64,4096]{2,1,0:T(8,128)(2,1)} %bitcast.64, f32[8,4,8,128]{3,2,1,0:T(8,128)} %pad.9.gains_ref), custom_call_target="tpu_custom_call" | custom-call | bytes 314572800 | tf_op jit(solution)/shard_map/pallas_call | solution.py:1272
  741.5 2.9 convert_element_type.106
  744.5 1.3 slice_bitcast_fusion
  745.8 0.9 copy.26
  746.6 0.8 copy.27
  747.4 2.0 copy.28
  (63 shorter events, 0.7 us)
Async XLA Ops:
  7.2 262.1 %all-gather.5.cloned.1.call-start = ((), (), s32[]{:S(2)}) async-start(), calls=%async_computation.3 | async-start | bytes 9437184 | tf_op jit(solution)/shard_map/all_gather | solution.py:825
  7.9 261.3 %all-gather.3.cloned.1.call-start = ((), (), s32[]{:S(2)}) async-start(), calls=%async_computation.2 | async-start | bytes 18874368 | tf_op jit(solution)/shard_map/all_gather | solution.py:825
  107.2 2.0 copy-start.10
  107.3 513.1 %reduce-scatter.5.cloned.1.call-start = ((), (), s32[]{:S(2)}) async-start(), calls=%async_computation.5 | async-start | bytes 18874368 | tf_op jit(solution)/shard_map/reduce_scatter | solution.py:829
  109.2 7.9 %copy-start.15 = (f32[2048]{0:T(1024)}, f32[2048]{0:T(1024)S(1)}, u32[]{:S(2)}) copy-start(f32[2048]{0:T(1024)S(1)} %get-tuple-element.49) | copy-start | bytes 24580
  109.5 7.6 %copy-start.17 = (f32[256]{0:T(256)}, f32[256]{0:T(256)S(1)}, u32[]{:S(2)}) copy-start(f32[256]{0:T(256)S(1)} %add_rsqrt_fusion.1) | copy-start | bytes 3076
  117.1 1.7 copy-start.19
  122.0 1.2 copy-start
  122.0 1.3 copy-start.1
  258.1 8.6 %copy-start.2 = (bf16[4,256,2048]{2,1,0:T(8,128)(2,1)}, bf16[4,256,2048]{2,1,0:T(8,128)(2,1)S(1)}, u32[]{:S(2)}) copy-start(bf16[4,256,2048]{2,1,0:T(8,128)(2,1)S(1)} %get-tuple-element.32.cot_ref) | copy-start | bytes 12582916
  258.1 8.6 %copy-start.3 = (f32[8,256,256]{2,1,0:T(8,128)}, f32[8,256,256]{2,1,0:T(8,128)S(1)}, u32[]{:S(2)}) copy-start(f32[8,256,256]{2,1,0:T(8,128)S(1)} %get-tuple-element.35.full_ref) | copy-start | bytes 6291460
  258.1 8.6 %copy-start.4 = (bf16[8,384,256]{2,1,0:T(8,128)(2,1)}, bf16[8,384,256]{2,1,0:T(8,128)(2,1)S(1)}, u32[]{:S(2)}) copy-start(bf16[8,384,256]{2,1,0:T(8,128)(2,1)S(1)} %get-tuple-element.31.x_ref) | copy-start | bytes 4718596
  266.7 1.3 copy-start.5
  432.7 308.9 %reduce-scatter.3.cloned.1.call-start = ((), (), s32[]{:S(2)}) async-start(), calls=%async_computation.4 | async-start | bytes 9437184 | tf_op jit(solution)/shard_map/reduce_scatter | solution.py:829
  434.3 3.0 copy-start.6
  434.3 3.5 copy-start.11
  437.7 6.2 slice-start
  438.3 5.6 copy-start.8
  438.3 5.6 slice-start.1
  588.1 0.7 copy-start.16
  588.1 0.7 copy-start.18
  599.3 3.7 copy-start.7
  599.3 3.8 copy-start.9
  599.3 4.4 copy-start.13
  741.5 4.3 copy-start.14
  741.5 5.9 copy-start.12
Sparse Core Ops, SparseCore 0:
  9.9 82.8 all-gather.4
  107.4 142.7 all-gather.2
  432.8 187.5 reduce-scatter.4
  623.7 83.0 reduce-scatter.2

commit v5 on v4

--- a/solution.py
+++ b/solution.py
@@ -408,6 +408,13 @@
             return carry
 
         lax.fori_loop(0, self.shard // 16, one, 0)
+
+    def after_all(self):
+        def one(q, carry):
+            self.after_z(q)
+            return carry
+
+        lax.fori_loop(0, self.chunks, one, 0)
 
     def drain(self):
         def one(q, carry):
@@ -670,13 +677,13 @@
         ready = (c >= 2) & (lax.rem(c, 2) == 0) & (q < chunks)
         pl.when(ready)(lambda: reduce.after_core(jnp.minimum(q, chunks - 1)))
         actions = [functools.partial(reduce.after_stage, stage=stage) for stage in range(reduce.bits)]
-        for index, action in enumerate(actions + [reduce.after_z]):
+        for index, action in enumerate(actions):
             since = jnp.maximum(c - (2 * chunks + 6 + 6 * index), -1)
             q = jnp.maximum(since, 0) // 5
             ready = (since >= 0) & (lax.rem(jnp.maximum(since, 0), 5) == 0) & (q < chunks)
             pl.when(ready)(functools.partial(action, jnp.minimum(q, chunks - 1)))
 
-    turns = 2 * reduce.chunks + 6 + 6 * reduce.bits + 5 * (reduce.chunks - 1) + 1
+    turns = 2 * reduce.chunks + 6 + 6 * (reduce.bits - 1) + 5 * (reduce.chunks - 1) + 1
     key_row = lax.broadcasted_iota(jnp.int32, (rows, rows), 0)
     column = lax.broadcasted_iota(jnp.int32, (rows, rows), 1)
     own_in.wait()
@@ -768,6 +775,7 @@
 
     lax.fori_loop(blocks * (blocks + 1) // 2, max(turns, blocks * (blocks + 1) // 2), left, 0)
 
+    reduce.after_all()
     reduce.drain()
     for mask in range(1, wide):
         other = me ^ mask
@@ -1013,13 +1021,14 @@
     def distance(d, carry):
         for side in (0, 1):
 
-            @pl.when(valid(side, d) & (d > 0))
+            @pl.when(passes(side, d + 1))
+            def _():
+                x_wait(side, d + 1)
+                x_copy(side, d + 1).start()
+
+            @pl.when(valid(side, d) & (d > 0) & jnp.logical_not(passes(side, d)))
             def _():
                 x_wait(side, d)
-
-            @pl.when(passes(side, d))
-            def _():
-                x_copy(side, d).start()
 
         @pl.when(d == 0)
         def _():
@@ -1035,6 +1044,8 @@
         return carry
 
     loads[3].wait()
+    for side in (0, 1):
+        pl.when(passes(side, 0))(lambda side=side: x_copy(side, 0).start())
     lax.fori_loop(0, narrow, distance, 0)
 
     tokens = narrow * rows
@@ -1216,11 +1227,9 @@
         for stage in range(bits):
             q = t - 1 - stage
             pl.when((q >= 0) & (q < chunks))(functools.partial(reduce.after_stage, q, stage))
-        q = t - 1 - bits
-        pl.when(q >= 0)(lambda: reduce.after_z(q))
         return carry
 
-    lax.fori_loop(0, chunks + bits + 1, turn, 0)
+    lax.fori_loop(0, chunks + bits, turn, 0)
 
     total = gains_ref[w]
     for mask in range(1, wide):
@@ -1231,6 +1240,7 @@
     for step in range(1, narrow):
         gz_copy(step).start()
 
+    reduce.after_all()
     own_cut.wait()
     for step in range(1, narrow):
         other = lax.rem(n + narrow - step, narrow)

time: 756 us -> 711 us (0.940)
  Pallas kernels: 658 us -> 617 us
    pallas_call x1, Pallas kernels: 121 us -> 101 us  [sum_all(): pl.pallas_call(functools.partial(sum_kernel, wide, narrow), out_shape=(ja...]
    pallas_call x1, Pallas kernels: 142 us -> 126 us  [attend_back(): pl.pallas_call(functools.partial(attend_back_kernel, wide, narrow, groups...]
  transfers between devices with their start and end apart: 4 -> 4, of which waited for: 1 -> 0; matrix products, arithmetic and copies ran while one was open for 8% -> 9% of each run, Pallas kernels for 65% -> 65%
where the time goes in v5:
time: 711 us; the launch traced here: 710 us
  Pallas kernels  617 us (87%)
  matrix products  43.2 us (6%)
  other arithmetic  22.3 us (3%)
  between operations  14.2 us (2%)
  local copies, waits for them, and re-layouts  12.2 us (2%)
    pallas_call x1, Pallas kernels, feed(): pl.pallas_call(functools.partial(feed_kernel, narrow), out_shape=(jax.Sha...  158 us
    pallas_call x1, Pallas kernels, attend(): pl.pallas_call(functools.partial(attend_kernel, wide, narrow, groups), ou...  135 us
    pallas_call x1, Pallas kernels, attend_back(): pl.pallas_call(functools.partial(attend_back_kernel, wide, narrow, groups...  126 us
    pallas_call x1, Pallas kernels, sum_all(): pl.pallas_call(functools.partial(sum_kernel, wide, narrow), out_shape=(ja...  101 us
    pallas_call x1, Pallas kernels, gather_weights(): pl.pallas_call(functools.partial(gather_kernel, wide, narrow, aligned), o...  96.7 us
    dot_general x6, matrix products, dot(): lax.dot_general(left, right, dims, preferred_element_type=F32).astype(kind)  43.2 us
  transfers between devices with their start and end apart: 4, of which 0 were waited for; matrix products, arithmetic and copies ran while one was open for 9% of the time, Pallas kernels for 65%

profile of v5, /device:TPU:0, one launch (start us, length us, event | category | flops | bytes accessed | tf_op | source)
XLA Modules:
  0.0 710.4 jit_solution(1858688822171811993)
XLA Ops:
  7.2 0.7 all-gather.5.cloned.1.call-update
  7.9 0.7 pad_maximum_fusion.5
  8.6 0.1 copy.22
  8.7 1.8 fusion.25.qkv_ref
  10.5 96.7 %shard_map.152 = (bf16[2048,3200]{1,0:T(8,128)(2,1)}, bf16[256,4096]{1,0:T(8,128)(2,1)}) custom-call(bf16[64,3200]{1,0:T(8,128)(2,1)} %fusion.25.qkv_ref, bf16[64,16384]{1,0:T(8,128)(2,1)} %cut_ref.1), custom_call_target="tpu_custom_call" | custom-call | bytes 209715200 | tf_op jit(solution)/shard_map/pallas_call | solution.py:902
  107.3 1.9 convert_reduce_fusion.1
  109.2 0.3 fusion.18
  109.5 7.6 %fusion.2 = f32[3072,256]{1,0:T(8,128)S(1)} fusion(bf16[2048,3200]{1,0:T(8,128)(2,1)} %get-tuple-element.28, bf16[1,256,2048]{2,1,0:T(8,128)(2,1)S(1)} %copy-done.10, f32[2048]{0:T(1024)S(1)} %get-tuple-element.49, f32[256]{0:T(256)S(1)} %add_rsqrt_fusion.1), kind=kOutput, calls=%fused_computation.3 | convolution fusion | flops 3223322624 | bytes 16786432 | tf_op jit(solution)/shard_map/dot_general | solution.py:28
  117.1 1.7 slice.62
  118.8 0.2 reduce-window.4
  119.0 0.1 convert_reduce_fusion.3
  119.2 0.1 select_reduce_fusion
  119.3 0.1 broadcast_multiply_fusion
  119.4 0.1 dynamic-slice_cosine_fusion
  119.5 2.1 multiply_subtract_fusion
  121.6 0.3 fusion.10
  122.0 0.1 pad_maximum_fusion.mine_ref
  122.1 1.1 copy-done
  123.2 134.9 %shard_map.153 = (bf16[8,384,256]{2,1,0:T(8,128)(2,1)S(1)}, bf16[8,256,256]{2,1,0:T(8,128)(2,1)S(1)}, f32[8,256,256]{2,1,0:T(8,128)S(1)}, f32[8,4,256]{2,1,0:T(4...) custom-call(s32[8,1,256]{2,1,0:T(1,128)S(1)} %bitcast.53, ...), custom_call_target="tpu_custom_call" | custom-call | flops 34359738368 | bytes 67108864 | tf_op jit(solution)/shard_map/pallas_call | solution.py:594
  258.1 8.6 %multiply_reduce_fusion.2 = (f32[256]{0:T(256)S(1)}, f32[256,2048]{1,0:T(8,128)S(1)}) fusion(bf16[2048,256]{1,0:T(8,128)(2,1)S(1)} %bitcast.50, bf16[2048,2048]{1,0:T(8,128)(2,1)} %get-tuple-element.30, bf16[1,256,2048]{2,1,0:T(8,128)(2,1)S(1)} %copy-done.10), kind=kOutput, calls=%fused_computation.33 | convolution fusion | flops 2149580544 | bytes 12583936 | tf_op jit(solution)/shard_map/dot_general | solution.py:28
  266.7 1.3 copy-done.5
  268.0 1.2 multiply_convert_fusion.x_ref
  269.2 157.6 %shard_map.154 = (bf16[4,256,2048]{2,1,0:T(8,128)(2,1)}, f32[256,2048]{1,0:T(8,128)}, bf16[2048,4096]{1,0:T(8,128)(2,1)}, bf16[2048,2048]{1,0:T(8,128)(2,1)}) custom-call(bf16[256,2048]{1,0:T(8,128)(2,1)} %multiply_convert_fusion.x_ref, bf16[4,256,2048]{2,1,0:T(8,128)(2,1)} %copy-done.2, bf16[2048,4096]{1,0:T(8,128)(2,1)} %all-gather.3.cloned.1.call-done.gate_up_ref, ...), custom_call_target="tpu_custom_call" | custom-call | flops 51539607552 | bytes 314572800 | tf_op jit(solution)/shard_map/pallas_call | solution.py:1133
  426.9 0.2 reduce-scatter.3.cloned.1.call-start
  427.1 0.3 reduce-scatter.3.cloned.1.call-update
  427.5 1.0 multiply_sine_fusion
  428.5 2.9 multiply_reduce_fusion
  431.5 0.5 copy-done.11
  432.0 0.6 multiply_add_fusion
  432.6 7.0 convolution_convert_fusion.1
  439.5 2.4 convolution_convert_fusion.2
  441.9 126.5 %shard_map.155 = (bf16[8,384,256]{2,1,0:T(8,128)(2,1)S(1)}, bf16[4,256,2048]{2,1,0:T(8,128)(2,1)}, f32[64,2048]{1,0:T(8,128)S(1)}) custom-call(s32[8,1,256]{2,1,0:T(1,128)S(1)} %bitcast.54, bf16[8,384,256]{2,1,0:T(8,128)(2,1)} %copy-done.4, bf16[8,256,256]{2,1,0:T(8,128)(2,1)S(1)} %bitcast.55, f32[8,256,256]{2,1,0:T(8,128)} %copy-done.3, ...), custom_call_target="tpu_custom_call" | custom-call | flops 42949672960 | bytes 6291456 | tf_op jit(solution)/shard_map/pallas_call | solution.py:799
  568.6 0.5 copy-done.16
  569.1 9.9 %fusion.17 = (f32[2048]{0:T(1024)S(1)}, f32[256]{0:T(256)S(1)}, f32[256,2048]{1,0:T(8,128)}) fusion(bf16[1,256,2048]{2,1,0:T(8,128)(2,1)S(1)} %copy-done.10, f32[256]{0:T(256)S(1)} %copy-done.18, f32[2048]{0:T(1024)S(1)} %copy-done.16, bf16[2048,3200]{1,0:T(8,128)(2,1)} %get-tuple-element.28, bf16[512,256]{1,0:T(8,128)(2,1)S(1)} %bitcast.68, ...), kind=kOutput, calls=%fused_computation.26 | convolution fusion | flops 3229611776 | bytes 17319936 | tf_op jit(solution)/shard_map/dot_general | solution.py:28
  579.0 0.1 stack.27
  579.1 0.1 stack.28
  579.2 0.7 pad.9.gains_ref
  579.9 3.6 convert_reduce_fusion
  583.6 0.1 copy-done.9
  583.7 0.7 copy-done.13
  584.4 2.3 fusion.19
  586.6 7.9 %convolution_convert_fusion = bf16[2048,3072]{1,0:T(8,128)(2,1)} fusion(bf16[512,256]{1,0:T(8,128)(2,1)S(1)} %bitcast.69, bf16[512,256]{1,0:T(8,128)(2,1)S(1)} %bitcast.67, bf16[2048,256]{1,0:T(8,128)(2,1)S(1)} %bitcast.63, bf16[1,256,2048]{2,1,0:T(8,128)(2,1)S(1)} %copy-done.10, f32[2048]{0:T(1024)S(1)} %copy-done.16, f32[256]{0:T(256)S(1)} %copy-done.18), kind=kOutput, calls=%fused_computation | convolution fusion | flops 3234332672 | bytes 15213568 | tf_op jit(solution)/shard_map/dot_general | solution.py:28
  594.5 101.4 %shard_map.156 = (f32[64,3072]{1,0:T(8,128)}, f32[64,16384]{1,0:T(8,128)}, f32[8,128]{1,0:T(8,128)}) custom-call(bf16[4,2,256,3072]{3,2,1,0:T(8,128)(2,1)} %bitcast.56, bf16[4,64,4096]{2,1,0:T(8,128)(2,1)} %bitcast.64, f32[8,4,8,128]{3,2,1,0:T(8,128)} %pad.9.gains_ref), custom_call_target="tpu_custom_call" | custom-call | bytes 314572800 | tf_op jit(solution)/shard_map/pallas_call | solution.py:1282
  696.0 2.9 convert_element_type.106
  698.9 1.3 slice_bitcast_fusion
  700.2 0.9 copy.26
  701.1 0.8 copy.27
  701.9 2.0 copy.28
  (63 shorter events, 0.6 us)
Async XLA Ops:
  7.2 262.1 %all-gather.5.cloned.1.call-start = ((), (), s32[]{:S(2)}) async-start(), calls=%async_computation.3 | async-start | bytes 9437184 | tf_op jit(solution)/shard_map/all_gather | solution.py:833
  7.9 261.3 %all-gather.3.cloned.1.call-start = ((), (), s32[]{:S(2)}) async-start(), calls=%async_computation.2 | async-start | bytes 18874368 | tf_op jit(solution)/shard_map/all_gather | solution.py:833
  107.2 2.0 copy-start.10
  107.3 487.3 %reduce-scatter.5.cloned.1.call-start = ((), (), s32[]{:S(2)}) async-start(), calls=%async_computation.5 | async-start | bytes 18874368 | tf_op jit(solution)/shard_map/reduce_scatter | solution.py:837
  109.2 7.9 %copy-start.15 = (f32[2048]{0:T(1024)}, f32[2048]{0:T(1024)S(1)}, u32[]{:S(2)}) copy-start(f32[2048]{0:T(1024)S(1)} %get-tuple-element.49) | copy-start | bytes 24580
  109.5 7.6 %copy-start.17 = (f32[256]{0:T(256)}, f32[256]{0:T(256)S(1)}, u32[]{:S(2)}) copy-start(f32[256]{0:T(256)S(1)} %add_rsqrt_fusion.1) | copy-start | bytes 3076
  117.1 1.7 copy-start.19
  122.0 1.2 copy-start
  122.0 1.3 copy-start.1
  258.1 8.6 %copy-start.2 = (bf16[4,256,2048]{2,1,0:T(8,128)(2,1)}, bf16[4,256,2048]{2,1,0:T(8,128)(2,1)S(1)}, u32[]{:S(2)}) copy-start(bf16[4,256,2048]{2,1,0:T(8,128)(2,1)S(1)} %get-tuple-element.32.cot_ref) | copy-start | bytes 12582916
  258.1 8.6 %copy-start.3 = (f32[8,256,256]{2,1,0:T(8,128)}, f32[8,256,256]{2,1,0:T(8,128)S(1)}, u32[]{:S(2)}) copy-start(f32[8,256,256]{2,1,0:T(8,128)S(1)} %get-tuple-element.35.full_ref) | copy-start | bytes 6291460
  258.1 8.6 %copy-start.4 = (bf16[8,384,256]{2,1,0:T(8,128)(2,1)}, bf16[8,384,256]{2,1,0:T(8,128)(2,1)S(1)}, u32[]{:S(2)}) copy-start(bf16[8,384,256]{2,1,0:T(8,128)(2,1)S(1)} %get-tuple-element.31.x_ref) | copy-start | bytes 4718596
  266.7 1.3 copy-start.5
  426.9 269.1 %reduce-scatter.3.cloned.1.call-start = ((), (), s32[]{:S(2)}) async-start(), calls=%async_computation.4 | async-start | bytes 9437184 | tf_op jit(solution)/shard_map/reduce_scatter | solution.py:837
  428.5 3.0 copy-start.6
  428.5 3.5 copy-start.11
  432.0 7.5 %slice-start = ((s8[8388608]{0:T(1024)(128)(4,1)}), s8[4194304]{0:T(1024)(128)(4,1)S(1)}, s32[]{:S(2)}) async-start(s8[8388608]{0:T(1024)(128)(4,1)} %bitcast.58), calls=%async_computation.6 | async-start | bytes 8388608
  432.6 7.0 copy-start.8
  432.6 7.0 slice-start.1
  568.4 0.7 copy-start.16
  568.5 0.7 copy-start.18
  579.9 3.7 copy-start.7
  579.9 3.8 copy-start.9
  579.9 4.5 copy-start.13
  696.0 4.3 copy-start.14
  696.0 5.9 copy-start.12
Sparse Core Ops, SparseCore 0:
  9.9 82.8 all-gather.4
  107.4 142.7 all-gather.2
  427.0 164.9 reduce-scatter.4
  595.3 100.0 reduce-scatter.2

commit v6 on v5

--- a/solution.py
+++ b/solution.py
@@ -289,13 +289,14 @@
 
 
 class Reduce:
-    def __init__(self, wide, narrow, source, out_ref, refs):
-        self.wide, self.narrow, self.source, self.out_ref = wide, narrow, source, out_ref
+    def __init__(self, wide, narrow, left, right, dims, out_ref, refs):
+        self.wide, self.narrow, self.left, self.right, self.dims = wide, narrow, left, right, dims
+        self.out_ref = out_ref
         self.w, self.n = lax.axis_index("wide"), lax.axis_index("narrow")
         self.core, self.chip = lax.rem(self.w, 2), self.w // 2
         self.chips = wide // 2
         self.bits = self.chips.bit_length() - 1
-        (self.held, self.core_in, self.chip_in, self.z_in, self.load_sem, self.core_send, self.core_recv,
+        (self.turned, self.held, self.away, self.core_in, self.chip_in, self.z_in, self.core_send, self.core_recv,
          self.chip_send, self.chip_recv, self.z_send, self.z_recv) = refs
         self.chunks = self.held.shape[0]
         self.rows, self.chunk = self.held.shape[2:]
@@ -305,12 +306,24 @@
     def columns_of(self, q):
         return pl.ds(pl.multiple_of(q * self.chunk, self.chunk), self.chunk)
 
+    def arrange(self):
+        for k in range(self.chips):
+            for core in (0, 1):
+                at = (2 * k + core) * self.rows
+                if self.dims == NT:
+                    tile = self.left[:, at : at + self.rows].T
+                else:
+                    tile = self.left[at : at + self.rows, :]
+                self.turned[core, k * self.rows : (k + 1) * self.rows, :] = tile
+
     def begin(self, q):
-        pltpu.make_async_copy(
-            self.source.at[:, self.core, :, self.columns_of(q)], self.held.at[q], self.load_sem.at[q]
-        ).start()
+        columns = self.columns_of(q)
+        right = self.right[columns, :] if self.dims == NT else self.right[:, columns]
+        shape = self.held.shape[1:]
+        self.away[q] = dot(self.turned[1 - self.core], right, self.dims, BF16).reshape(shape)
+        self.held[q] = dot(self.turned[self.core], right, self.dims, BF16).reshape(shape)
         pltpu.make_async_remote_copy(
-            src_ref=self.source.at[:, 1 - self.core, :, self.columns_of(q)],
+            src_ref=self.away.at[q],
             dst_ref=self.core_in.at[q],
             send_sem=self.core_send.at[q],
             recv_sem=self.core_recv.at[q],
@@ -359,7 +372,6 @@
                 self.chip_copy(q, h, stage, slot, kept).start()
 
     def after_core(self, q):
-        pltpu.make_async_copy(self.held.at[q], self.held.at[q], self.load_sem.at[q]).wait()
         arrive(self.core_in.at[q], self.core_recv.at[q])
         for k in range(self.chips):
             self.add_to(
@@ -430,15 +442,16 @@
         lax.fori_loop(0, self.chunks, one, 0)
 
 
-def reduce_scratch(wide, narrow, source, chunk):
-    chips, rows, chunks = wide // 2, source.shape[2], source.shape[3] // chunk
+def reduce_scratch(wide, narrow, rows, tokens, columns, chunk):
+    chips, rows, chunks = wide // 2, rows // wide, columns // chunk
     dma = pltpu.SemaphoreType.DMA
     return [
+        pltpu.VMEM((2, chips * rows, tokens), BF16),
+        pltpu.VMEM((chunks, chips, rows, chunk), BF16),
         pltpu.VMEM((chunks, chips, rows, chunk), BF16),
         pltpu.VMEM((chunks, chips, rows, chunk), BF16),
         pltpu.VMEM((chunks, 2, chips - 1, rows, chunk // 2), BF16),
         pltpu.VMEM((chunks, narrow, rows // narrow, chunk), BF16),
-        dma((chunks,)),
         dma((chunks,)),
         dma((chunks,)),
         dma((chunks, 2, chips - 1)),
@@ -632,11 +645,11 @@
 
 def attend_back_kernel(
     wide, narrow, groups, start_ref, x_ref, mine_ref, full_ref, log_ref, cos_ref, sin_ref, part_ref,
-    weight_ref, out_ref, came_ref, weight_out,
+    left_ref, right_ref, out_ref, came_ref, weight_out,
     keys, values, acc, acc_keys, acc_values, grad_ref, done, own_sem, in_send, in_recv,
     q_send, q_recv, k_send, k_recv, p_send, p_recv, *refs,
 ):
-    reduce = Reduce(wide, narrow, weight_ref, weight_out, refs)
+    reduce = Reduce(wide, narrow, left_ref, right_ref, NN, weight_out, refs)
     me, n = lax.axis_index("wide"), lax.axis_index("narrow")
 
     def part_copy(step):
@@ -665,8 +678,8 @@
         to_owner(
             mine_ref.at[me ^ mask], grad_ref.at[me], in_send.at[mask], in_recv.at[me], mask
         ).start()
-    for q in range(reduce.chunks):
-        reduce.begin(q)
+    reduce.arrange()
+    lax.fori_loop(0, reduce.chunks, lambda q, carry: (reduce.begin(q), carry)[1], 0)
     own_part.start()
     for step in range(1, narrow):
         part_copy(step).start()
@@ -789,7 +802,7 @@
         part_copy(step).wait()
 
 
-def attend_back(x, mine, full, log_total, start, cos, sin, part, weight, groups):
+def attend_back(x, mine, full, log_total, start, cos, sin, part, left, right, groups):
     wide, narrow = lax.axis_size("wide"), lax.axis_size("narrow")
     blocks, features, rows = x.shape
     width = groups * HEAD_DIM
@@ -801,9 +814,9 @@
         out_shape=(
             jax.ShapeDtypeStruct(x.shape, BF16),
             jax.ShapeDtypeStruct(part.shape, BF16),
-            jax.ShapeDtypeStruct((weight.shape[2] // narrow, weight.shape[3]), F32),
+            jax.ShapeDtypeStruct((left.shape[0] // (wide * narrow), right.shape[1]), F32),
         ),
-        in_specs=[vmem] * 7 + [hbm, hbm],
+        in_specs=[vmem] * 7 + [hbm, vmem, vmem],
         out_specs=(vmem, hbm, vmem),
         scratch_shapes=[
             pltpu.VMEM((blocks, rows, HEAD_DIM), BF16),
@@ -817,7 +830,7 @@
         ]
         + [dma((wide,))] * 6
         + [dma((narrow,))] * 2
-        + reduce_scratch(wide, narrow, weight, 512),
+        + reduce_scratch(wide, narrow, left.shape[0], left.shape[1], right.shape[1], 512),
         compiler_params=pltpu.CompilerParams(
             collective_id=4, has_side_effects=True, vmem_limit_bytes=50 << 20
         ),
@@ -826,7 +839,7 @@
             bytes_accessed=4 * x.size * 2,
             transcendentals=groups * (blocks * rows) ** 2 // 2,
         ),
-    )(start, x, mine, full, log_total, cos, sin, part, weight)
+    )(start, x, mine, full, log_total, cos, sin, part, left, right)
 
 
 def gather(x, axis):
@@ -1166,12 +1179,13 @@
 
 
 def sum_kernel(
-    wide, narrow, qkv_ref, cut_ref, gains_ref, qkv_out, cut_out, gains_out,
+    wide, narrow, left_ref, right_ref, cut_ref, gains_ref, qkv_out, cut_out, gains_out,
     cut_in, gain_w, gain_sum, gain_z, own_sem, cut_send, cut_recv, gw_send, gw_recv, gz_send, gz_recv, *refs,
 ):
-    reduce = Reduce(wide, narrow, qkv_ref, qkv_out, refs)
+    reduce = Reduce(wide, narrow, left_ref, right_ref, NT, qkv_out, refs)
     w, n = reduce.w, reduce.n
     chunks, bits = reduce.chunks, reduce.bits
+    reduce.arrange()
     greet(wide, narrow)
 
     def to_wide(mask):
@@ -1213,8 +1227,7 @@
         )
 
     ahead = min(4, chunks)
-    for q in range(ahead):
-        reduce.begin(q)
+    lax.fori_loop(0, ahead, lambda q, carry: (reduce.begin(q), carry)[1], 0)
     own_cut.start()
     for step in range(1, narrow):
         cut_copy(step).start()
@@ -1271,7 +1284,7 @@
     reduce.drain()
 
 
-def sum_all(qkv, cut, gains):
+def sum_all(left, right, cut, gains):
     wide, narrow = lax.axis_size("wide"), lax.axis_size("narrow")
     shard, cut_width = cut.shape[1:]
     aligned = (cut_width // (2 * wide)) % 128 == 0
@@ -1282,11 +1295,11 @@
     results = pl.pallas_call(
         functools.partial(sum_kernel, wide, narrow),
         out_shape=(
-            jax.ShapeDtypeStruct((shard, qkv.shape[3]), F32),
+            jax.ShapeDtypeStruct((shard, right.shape[0]), F32),
             jax.ShapeDtypeStruct(cut_shape, F32),
             jax.ShapeDtypeStruct((8, 128), F32),
         ),
-        in_specs=[hbm, hbm, vmem],
+        in_specs=[vmem, vmem, hbm, vmem],
         out_specs=(vmem, vmem, vmem),
         scratch_shapes=[
             pltpu.VMEM(cut.shape, BF16),
@@ -1301,12 +1314,12 @@
             dma((narrow,)),
             dma((narrow,)),
         ]
-        + reduce_scratch(wide, narrow, qkv, 256),
+        + reduce_scratch(wide, narrow, left.shape[1], left.shape[0], right.shape[0], 256),
         compiler_params=pltpu.CompilerParams(
             collective_id=2, has_side_effects=True, vmem_limit_bytes=54 << 20
         ),
         cost_estimate=pl.CostEstimate(flops=0, bytes_accessed=300 << 20, transcendentals=0),
-    )(qkv, cut, gains)
+    )(left, right, cut, gains)
     return results, aligned
 
 
@@ -1370,11 +1383,9 @@
     )
     grad_branch = grad_middle.astype(BF16)
     grad_attended = dot(out_whole, grad_branch, NT, BF16).reshape(wide, groups * HEAD_DIM, rows)
-    cut = (wide // 2, 2, narrow * shard, -1)
-    part_wout = dot(attended_low, grad_branch, NN, BF16).reshape(cut)
     grad_heads, low_came, grad_wout = attend_back(
-        heads, grad_attended, attended_full, log_total, start, cos_all, sin_all, low_part, part_wout,
-        groups,
+        heads, grad_attended, attended_full, log_total, start, cos_all, sin_all, low_part,
+        attended_low, grad_branch, groups,
     )
     layer_out = (middle + jnp.sum(low_came.astype(F32), 0)).astype(BF16)[None]
     grad_queries = grad_heads[:, : groups * HEAD_DIM].reshape(query_width, rows)
@@ -1399,8 +1410,9 @@
     part_gains = jnp.pad(
         part_gains.transpose(1, 2, 0, 3), ((0, 0), (0, 0), (0, 6), (0, 128 - shard))
     )
-    part_qkv = dot(normed_one, grad_projected, (((0,), (1,)), ((), ())), BF16).reshape(cut)
-    (grad_qkv, grad_gateup, grad_gains), done = sum_all(part_qkv, grad_gateup, part_gains)
+    (grad_qkv, grad_gateup, grad_gains), done = sum_all(
+        normed_one, grad_projected, grad_gateup, part_gains
+    )
     if not done:
         grad_gateup = (
             grad_gateup.reshape(narrow, shard, 2, wide, -1)

time: 711 us -> 707 us (level)
  matrix products: 43.2 us -> 33.8 us
    dot_general x6 -> x4, matrix products: 43.2 us -> 33.8 us  [dot(): lax.dot_general(left, right, dims, preferred_element_type=F32).astype(kind)]
  transfers between devices with their start and end apart: 4 -> 4, of which waited for: 0 -> 2; matrix products, arithmetic and copies ran while one was open for 9% -> 9% of each run, Pallas kernels for 65% -> 64%
where the time goes in v6:
time: 707 us; the launch traced here: 706 us
  Pallas kernels  611 us (86%)
  matrix products  33.8 us (5%)
  other arithmetic  24.4 us (3%)
  local copies, waits for them, and re-layouts  14.4 us (2%)
  between operations  14.2 us (2%)
  waiting for transfers between devices  7.28 us (1%)
    pallas_call x1, Pallas kernels, feed(): pl.pallas_call(functools.partial(feed_kernel, narrow), out_shape=(jax.Sha...  157 us
    pallas_call x1, Pallas kernels, attend(): pl.pallas_call(functools.partial(attend_kernel, wide, narrow, groups), ou...  134 us
    pallas_call x1, Pallas kernels, attend_back(): pl.pallas_call(functools.partial(attend_back_kernel, wide, narrow, groups...  128 us
    pallas_call x1, Pallas kernels, gather_weights(): pl.pallas_call(functools.partial(gather_kernel, wide, narrow, aligned), o...  96.7 us
    pallas_call x1, Pallas kernels, sum_all(): pl.pallas_call(functools.partial(sum_kernel, wide, narrow), out_shape=(ja...  95.5 us
    dot_general x4, matrix products, dot(): lax.dot_general(left, right, dims, preferred_element_type=F32).astype(kind)  33.8 us
  transfers between devices with their start and end apart: 4, of which 2 were waited for; matrix products, arithmetic and copies ran while one was open for 9% of the time, Pallas kernels for 64%

profile of v6, /device:TPU:0, one launch (start us, length us, event | category | flops | bytes accessed | tf_op | source)
XLA Modules:
  0.0 706.0 jit_solution(12199233259106395742)
XLA Ops:
  7.2 0.7 all-gather.5.cloned.1.call-update
  7.9 0.7 pad_maximum_fusion.3
  8.6 0.1 copy.28
  8.7 1.8 fusion.23.qkv_ref
  10.5 96.7 %shard_map.152 = (bf16[2048,3200]{1,0:T(8,128)(2,1)}, bf16[256,4096]{1,0:T(8,128)(2,1)}) custom-call(bf16[64,3200]{1,0:T(8,128)(2,1)} %fusion.23.qkv_ref, bf16[64,16384]{1,0:T(8,128)(2,1)} %cut_ref.1), custom_call_target="tpu_custom_call" | custom-call | bytes 209715200 | tf_op jit(solution)/shard_map/pallas_call | solution.py:915
  107.3 1.9 convert_reduce_fusion.1
  109.2 0.3 fusion.18
  109.5 0.3 fusion.11.left_ref
  109.9 8.2 %fusion.2 = f32[3072,256]{1,0:T(8,128)S(1)} fusion(bf16[256,2048]{1,0:T(8,128)(2,1)S(1)} %fusion.11.left_ref, bf16[2048,3200]{1,0:T(8,128)(2,1)} %get-tuple-element.28), kind=kOutput, calls=%fused_computation.2 | convolution fusion | flops 3221225472 | bytes 16777216 | tf_op jit(solution)/shard_map/dot_general | solution.py:28
  118.1 1.7 slice.62
  119.8 0.2 reduce-window.4
  120.0 0.1 convert_reduce_fusion.3
  120.1 0.1 select_reduce_fusion
  120.2 0.1 broadcast_multiply_fusion
  120.3 0.1 dynamic-slice_cosine_fusion
  120.5 2.1 multiply_subtract_fusion
  122.6 0.3 fusion.10
  122.9 0.1 pad_maximum_fusion.mine_ref
  123.1 1.1 copy-done
  124.2 134.5 %shard_map.153 = (bf16[8,384,256]{2,1,0:T(8,128)(2,1)S(1)}, bf16[8,256,256]{2,1,0:T(8,128)(2,1)S(1)}, f32[8,256,256]{2,1,0:T(8,128)S(1)}, f32[8,4,256]{2,1,0:T(4...) custom-call(s32[8,1,256]{2,1,0:T(1,128)S(1)} %bitcast.58, ...), custom_call_target="tpu_custom_call" | custom-call | flops 34359738368 | bytes 67108864 | tf_op jit(solution)/shard_map/pallas_call | solution.py:607
  258.7 8.6 %multiply_reduce_fusion.2 = (f32[256]{0:T(256)S(1)}, f32[256,2048]{1,0:T(8,128)S(1)}) fusion(bf16[2048,256]{1,0:T(8,128)(2,1)S(1)} %bitcast.56, bf16[2048,2048]{1,0:T(8,128)(2,1)} %get-tuple-element.30, bf16[1,256,2048]{2,1,0:T(8,128)(2,1)S(1)} %copy-done.10), kind=kOutput, calls=%fused_computation.31 | convolution fusion | flops 2149580544 | bytes 12583936 | tf_op jit(solution)/shard_map/dot_general | solution.py:28
  267.3 1.3 copy-done.5
  268.6 1.2 multiply_convert_fusion.x_ref
  269.8 157.0 %shard_map.154 = (bf16[4,256,2048]{2,1,0:T(8,128)(2,1)}, f32[256,2048]{1,0:T(8,128)}, bf16[2048,4096]{1,0:T(8,128)(2,1)}, bf16[2048,2048]{1,0:T(8,128)(2,1)}) custom-call(bf16[256,2048]{1,0:T(8,128)(2,1)} %multiply_convert_fusion.x_ref, bf16[4,256,2048]{2,1,0:T(8,128)(2,1)} %copy-done.2, bf16[2048,4096]{1,0:T(8,128)(2,1)} %all-gather.3.cloned.1.call-done.gate_up_ref, ...), custom_call_target="tpu_custom_call" | custom-call | flops 51539607552 | bytes 314572800 | tf_op jit(solution)/shard_map/pallas_call | solution.py:1146
  426.8 0.2 reduce-scatter.3.cloned.1.call-start
  427.1 0.3 reduce-scatter.3.cloned.1.call-update
  427.4 1.0 multiply_sine_fusion
  428.4 3.0 multiply_reduce_fusion
  431.4 0.5 copy-done.8
  431.9 0.7 fusion.25.right_ref
  432.6 6.7 convolution_convert_fusion
  439.4 127.8 %shard_map.155 = (bf16[8,384,256]{2,1,0:T(8,128)(2,1)}, bf16[4,256,2048]{2,1,0:T(8,128)(2,1)}, f32[64,2048]{1,0:T(8,128)S(1)}) custom-call(s32[8,1,256]{2,1,0:T(1,128)S(1)} %bitcast.59, bf16[8,384,256]{2,1,0:T(8,128)(2,1)} %copy-done.4, bf16[8,256,256]{2,1,0:T(8,128)(2,1)S(1)} %bitcast.60, f32[8,256,256]{2,1,0:T(8,128)} %copy-done.3, ...), custom_call_target="tpu_custom_call" | custom-call | flops 42949672960 | bytes 6291456 | tf_op jit(solution)/shard_map/pallas_call | solution.py:812
  567.3 1.3 slice.57
  568.6 1.3 slice.56
  570.0 10.3 %fusion.17 = (f32[2048]{0:T(1024)S(1)}, f32[256]{0:T(256)S(1)}, f32[256,2048]{1,0:T(8,128)}) fusion(bf16[1,256,2048]{2,1,0:T(8,128)(2,1)S(1)} %copy-done.11, f32[256]{0:T(256)S(1)} %copy-done.22, f32[2048]{0:T(1024)S(1)} %copy-done.20, bf16[2048,3200]{1,0:T(8,128)(2,1)} %get-tuple-element.28, bf16[512,256]{1,0:T(8,128)(2,1)S(1)} %bitcast.70, ...), kind=kOutput, calls=%fused_computation.24 | convolution fusion | flops 3229611776 | bytes 17319936 | tf_op jit(solution)/shard_map/dot_general | solution.py:28
  580.5 0.7 pad.9.gains_ref
  581.2 3.7 convert_reduce_fusion
  584.9 1.3 pad_maximum_fusion.1.right_ref
  586.2 1.0 copy-done.7
  587.2 2.6 fusion.20
  589.8 3.9 reduce-scatter.5.cloned.1.call-done
  593.7 95.5 %shard_map.156 = (f32[64,3072]{1,0:T(8,128)}, f32[64,16384]{1,0:T(8,128)}, f32[8,128]{1,0:T(8,128)}) custom-call(bf16[256,2048]{1,0:T(8,128)(2,1)} %copy-done.14, bf16[3072,256]{1,0:T(8,128)(2,1)} %pad_maximum_fusion.1.right_ref, bf16[4,64,4096]{2,1,0:T(8,128)(2,1)} %bitcast.65, f32[8,4,8,128]{3,2,1,0:T(8,128)} %pad.9.gains_ref), custom_call_target="tpu_custom_call" | custom-call | bytes 314572800 | tf_op jit(solution)/shard_map/pallas_call | solution.py:1295
  689.2 2.3 reduce-scatter.3.cloned.1.call-done
  691.6 2.9 convert_element_type.98
  694.5 1.3 slice_bitcast_fusion
  695.8 0.9 copy.36
  696.6 0.8 copy.37
  697.4 2.0 copy.38
  (66 shorter events, 0.7 us)
Async XLA Ops:
  7.2 262.6 %all-gather.5.cloned.1.call-start = ((), (), s32[]{:S(2)}) async-start(), calls=%async_computation.3 | async-start | bytes 9437184 | tf_op jit(solution)/shard_map/all_gather | solution.py:846
  7.9 261.9 %all-gather.3.cloned.1.call-start = ((), (), s32[]{:S(2)}) async-start(), calls=%async_computation.2 | async-start | bytes 18874368 | tf_op jit(solution)/shard_map/all_gather | solution.py:846
  107.2 2.0 copy-start.10
  107.3 486.4 %reduce-scatter.5.cloned.1.call-start = ((), (), s32[]{:S(2)}) async-start(), calls=%async_computation.5 | async-start | bytes 18874368 | tf_op jit(solution)/shard_map/reduce_scatter | solution.py:850
  109.2 8.8 %copy-start.19 = (f32[2048]{0:T(1024)}, f32[2048]{0:T(1024)S(1)}, u32[]{:S(2)}) copy-start(f32[2048]{0:T(1024)S(1)} %get-tuple-element.49) | copy-start | bytes 24580
  109.5 8.5 %copy-start.21 = (f32[256]{0:T(256)}, f32[256]{0:T(256)S(1)}, u32[]{:S(2)}) copy-start(f32[256]{0:T(256)S(1)} %add_rsqrt_fusion.1) | copy-start | bytes 3076
  109.8 8.2 %copy-start.14 = (bf16[256,2048]{1,0:T(8,128)(2,1)}, bf16[256,2048]{1,0:T(8,128)(2,1)S(1)}, u32[]{:S(2)}) copy-start(bf16[256,2048]{1,0:T(8,128)(2,1)S(1)} %fusion.11.left_ref) | copy-start | bytes 3145732
  118.1 1.7 copy-start.23
  122.9 1.2 copy-start
  122.9 1.3 copy-start.1
  258.6 8.6 %copy-start.2 = (bf16[4,256,2048]{2,1,0:T(8,128)(2,1)}, bf16[4,256,2048]{2,1,0:T(8,128)(2,1)S(1)}, u32[]{:S(2)}) copy-start(bf16[4,256,2048]{2,1,0:T(8,128)(2,1)S(1)} %get-tuple-element.32.cot_ref) | copy-start | bytes 12582916
  258.7 8.6 %copy-start.3 = (f32[8,256,256]{2,1,0:T(8,128)}, f32[8,256,256]{2,1,0:T(8,128)S(1)}, u32[]{:S(2)}) copy-start(f32[8,256,256]{2,1,0:T(8,128)S(1)} %get-tuple-element.35.full_ref) | copy-start | bytes 6291460
  258.7 8.6 %copy-start.4 = (bf16[8,384,256]{2,1,0:T(8,128)(2,1)}, bf16[8,384,256]{2,1,0:T(8,128)(2,1)S(1)}, u32[]{:S(2)}) copy-start(bf16[8,384,256]{2,1,0:T(8,128)(2,1)S(1)} %get-tuple-element.31.x_ref) | copy-start | bytes 4718596
  267.3 1.3 copy-start.5
  426.8 264.7 %reduce-scatter.3.cloned.1.call-start = ((), (), s32[]{:S(2)}) async-start(), calls=%async_computation.4 | async-start | bytes 9437184 | tf_op jit(solution)/shard_map/reduce_scatter | solution.py:850
  428.4 3.0 copy-start.6
  428.4 3.5 copy-start.8
  432.6 6.8 copy-start.17
  567.2 2.7 copy-start.11
  567.2 2.7 copy-start.20
  567.2 2.7 copy-start.22
  569.9 10.4 %copy-start.12 = (bf16[8,256,256]{2,1,0:T(8,128)(2,1)}, bf16[8,256,256]{2,1,0:T(8,128)(2,1)S(1)}, u32[]{:S(2)}) copy-start(bf16[8,256,256]{2,1,0:T(8,128)(2,1)S(1)} %slice.56) | copy-start | bytes 3145732
  581.2 3.7 copy-start.13
  581.2 5.0 copy-start.9
  581.2 5.0 copy-start.16
  584.9 2.3 copy-start.7
  689.2 6.5 copy-start.18
  691.6 5.9 copy-start.15
Sparse Core Ops, SparseCore 0:
  9.9 82.8 all-gather.4
  107.4 142.7 all-gather.2
  427.0 166.6 reduce-scatter.4
  597.0 94.5 reduce-scatter.2

commit v7 on v6

--- a/solution.py
+++ b/solution.py
@@ -987,12 +987,13 @@
     def out_copy(at, block):
         return pltpu.make_async_copy(low.at[at], low_out.at[block], out_sem.at[at])
 
-    def g_copy(block):
+    def g_copy(block, half):
+        columns = pl.ds(half * (width // 2), width // 2)
         return pltpu.make_async_remote_copy(
-            src_ref=cot.at[block],
-            dst_ref=came.at[n],
-            send_sem=g_send.at[block],
-            recv_sem=g_recv.at[n],
+            src_ref=cot.at[block, :, columns],
+            dst_ref=came.at[n, :, columns],
+            send_sem=g_send.at[block, half],
+            recv_sem=g_recv.at[n, half],
             device_id=to_narrow(block),
             device_id_type=MESH,
         )
@@ -1027,9 +1028,10 @@
             low[at, :, columns] = dot(hidden[block], down[:, columns], NN, BF16)
             return carry
 
-        lax.fori_loop(0, wtiles, second, 0)
+        for half in (0, 1):
+            lax.fori_loop(half * (wtiles // 2), (half + 1) * (wtiles // 2), second, 0)
+            pl.when(block != n)(lambda half=half: g_copy(block, half).start())
         out_copy(at, block).start()
-        pl.when(block != n)(lambda: g_copy(block).start())
 
     def distance(d, carry):
         for side in (0, 1):
@@ -1121,9 +1123,9 @@
             pl.when(passes(side, d))(lambda side=side, d=d: x_copy(side, d).wait_send())
     for step in range(1, narrow):
         other = lax.rem(n + step, narrow)
-        g_copy(other).wait_send()
-        block = came.at[other]
-        pltpu.make_async_copy(block, block, g_recv.at[other]).wait()
+        for half in (0, 1):
+            g_copy(other, half).wait_send()
+            arrive(came.at[other, :, pl.ds(half * (width // 2), width // 2)], g_recv.at[other, half])
 
     def add(r, carry):
         part = pl.ds(pl.multiple_of(r * 16, 16), 16)
@@ -1166,8 +1168,8 @@
             dma((2, narrow + 1)),
             dma((2, narrow + 1)),
             dma((2,)),
-            dma((narrow,)),
-            dma((narrow,)),
+            dma((narrow, 2)),
+            dma((narrow, 2)),
         ],
         compiler_params=pltpu.CompilerParams(
             collective_id=1, has_side_effects=True, vmem_limit_bytes=58 << 20

time: 707 us -> 703 us (level)
  transfers between devices with their start and end apart: 4 -> 4, of which waited for: 2 -> 2; matrix products, arithmetic and copies ran while one was open for 9% -> 9% of each run, Pallas kernels for 64% -> 65%
where the time goes in v7:
time: 703 us; the launch traced here: 702 us
  Pallas kernels  607 us (86%)
  matrix products  33.9 us (5%)
  other arithmetic  24.4 us (3%)
  local copies, waits for them, and re-layouts  14.4 us (2%)
  between operations  14.2 us (2%)
  waiting for transfers between devices  7.24 us (1%)
    pallas_call x1, Pallas kernels, feed(): pl.pallas_call(functools.partial(feed_kernel, narrow), out_shape=(jax.Sha...  153 us
    pallas_call x1, Pallas kernels, attend(): pl.pallas_call(functools.partial(attend_kernel, wide, narrow, groups), ou...  134 us
    pallas_call x1, Pallas kernels, attend_back(): pl.pallas_call(functools.partial(attend_back_kernel, wide, narrow, groups...  128 us
    pallas_call x1, Pallas kernels, gather_weights(): pl.pallas_call(functools.partial(gather_kernel, wide, narrow, aligned), o...  96.7 us
    pallas_call x1, Pallas kernels, sum_all(): pl.pallas_call(functools.partial(sum_kernel, wide, narrow), out_shape=(ja...  95.6 us
    dot_general x4, matrix products, dot(): lax.dot_general(left, right, dims, preferred_element_type=F32).astype(kind)  33.9 us
  transfers between devices with their start and end apart: 4, of which 2 were waited for; matrix products, arithmetic and copies ran while one was open for 9% of the time, Pallas kernels for 65%

profile of v7, /device:TPU:0, one launch (start us, length us, event | category | flops | bytes accessed | tf_op | source)
XLA Modules:
  0.0 702.0 jit_solution(2304145180811686331)
XLA Ops:
  7.2 0.7 all-gather.5.cloned.1.call-update
  7.9 0.7 pad_maximum_fusion.3
  8.6 0.1 copy.28
  8.7 1.8 fusion.23.qkv_ref
  10.5 96.7 %shard_map.152 = (bf16[2048,3200]{1,0:T(8,128)(2,1)}, bf16[256,4096]{1,0:T(8,128)(2,1)}) custom-call(bf16[64,3200]{1,0:T(8,128)(2,1)} %fusion.23.qkv_ref, bf16[64,16384]{1,0:T(8,128)(2,1)} %cut_ref.1), custom_call_target="tpu_custom_call" | custom-call | bytes 209715200 | tf_op jit(solution)/shard_map/pallas_call | solution.py:915
  107.3 1.9 convert_reduce_fusion.1
  109.2 0.3 fusion.18
  109.5 0.3 fusion.11.left_ref
  109.9 8.2 %fusion.2 = f32[3072,256]{1,0:T(8,128)S(1)} fusion(bf16[256,2048]{1,0:T(8,128)(2,1)S(1)} %fusion.11.left_ref, bf16[2048,3200]{1,0:T(8,128)(2,1)} %get-tuple-element.28), kind=kOutput, calls=%fused_computation.2 | convolution fusion | flops 3221225472 | bytes 16777216 | tf_op jit(solution)/shard_map/dot_general | solution.py:28
  118.1 1.7 slice.62
  119.8 0.2 reduce-window.4
  120.0 0.1 convert_reduce_fusion.3
  120.1 0.1 select_reduce_fusion
  120.2 0.1 broadcast_multiply_fusion
  120.3 0.1 dynamic-slice_cosine_fusion
  120.4 2.1 multiply_subtract_fusion
  122.6 0.3 fusion.10
  122.9 0.1 pad_maximum_fusion.mine_ref
  123.0 1.1 copy-done
  124.2 134.5 %shard_map.153 = (bf16[8,384,256]{2,1,0:T(8,128)(2,1)S(1)}, bf16[8,256,256]{2,1,0:T(8,128)(2,1)S(1)}, f32[8,256,256]{2,1,0:T(8,128)S(1)}, f32[8,4,256]{2,1,0:T(4...) custom-call(s32[8,1,256]{2,1,0:T(1,128)S(1)} %bitcast.58, ...), custom_call_target="tpu_custom_call" | custom-call | flops 34359738368 | bytes 67108864 | tf_op jit(solution)/shard_map/pallas_call | solution.py:607
  258.7 8.6 %multiply_reduce_fusion.2 = (f32[256]{0:T(256)S(1)}, f32[256,2048]{1,0:T(8,128)S(1)}) fusion(bf16[2048,256]{1,0:T(8,128)(2,1)S(1)} %bitcast.56, bf16[2048,2048]{1,0:T(8,128)(2,1)} %get-tuple-element.30, bf16[1,256,2048]{2,1,0:T(8,128)(2,1)S(1)} %copy-done.10), kind=kOutput, calls=%fused_computation.31 | convolution fusion | flops 2149580544 | bytes 12583936 | tf_op jit(solution)/shard_map/dot_general | solution.py:28
  267.3 1.3 copy-done.5
  268.6 1.2 multiply_convert_fusion.x_ref
  269.8 153.0 %shard_map.154 = (bf16[4,256,2048]{2,1,0:T(8,128)(2,1)}, f32[256,2048]{1,0:T(8,128)}, bf16[2048,4096]{1,0:T(8,128)(2,1)}, bf16[2048,2048]{1,0:T(8,128)(2,1)}) custom-call(bf16[256,2048]{1,0:T(8,128)(2,1)} %multiply_convert_fusion.x_ref, bf16[4,256,2048]{2,1,0:T(8,128)(2,1)} %copy-done.2, bf16[2048,4096]{1,0:T(8,128)(2,1)} %all-gather.3.cloned.1.call-done.gate_up_ref, ...), custom_call_target="tpu_custom_call" | custom-call | flops 51539607552 | bytes 314572800 | tf_op jit(solution)/shard_map/pallas_call | solution.py:1148
  422.9 0.3 reduce-scatter.3.cloned.1.call-start
  423.1 0.3 reduce-scatter.3.cloned.1.call-update
  423.5 1.0 multiply_sine_fusion
  424.5 3.0 multiply_reduce_fusion
  427.5 0.5 copy-done.8
  427.9 0.7 fusion.25.right_ref
  428.7 6.8 convolution_convert_fusion
  435.5 127.7 %shard_map.155 = (bf16[8,384,256]{2,1,0:T(8,128)(2,1)}, bf16[4,256,2048]{2,1,0:T(8,128)(2,1)}, f32[64,2048]{1,0:T(8,128)S(1)}) custom-call(s32[8,1,256]{2,1,0:T(1,128)S(1)} %bitcast.59, bf16[8,384,256]{2,1,0:T(8,128)(2,1)} %copy-done.4, bf16[8,256,256]{2,1,0:T(8,128)(2,1)S(1)} %bitcast.60, f32[8,256,256]{2,1,0:T(8,128)} %copy-done.3, ...), custom_call_target="tpu_custom_call" | custom-call | flops 42949672960 | bytes 6291456 | tf_op jit(solution)/shard_map/pallas_call | solution.py:812
  563.2 1.3 slice.57
  564.6 1.3 slice.56
  565.9 10.3 %fusion.17 = (f32[2048]{0:T(1024)S(1)}, f32[256]{0:T(256)S(1)}, f32[256,2048]{1,0:T(8,128)}) fusion(bf16[1,256,2048]{2,1,0:T(8,128)(2,1)S(1)} %copy-done.11, f32[256]{0:T(256)S(1)} %copy-done.22, f32[2048]{0:T(1024)S(1)} %copy-done.20, bf16[2048,3200]{1,0:T(8,128)(2,1)} %get-tuple-element.28, bf16[512,256]{1,0:T(8,128)(2,1)S(1)} %bitcast.70, ...), kind=kOutput, calls=%fused_computation.24 | convolution fusion | flops 3229611776 | bytes 17319936 | tf_op jit(solution)/shard_map/dot_general | solution.py:28
  576.5 0.7 pad.9.gains_ref
  577.2 3.7 convert_reduce_fusion
  580.9 1.3 pad_maximum_fusion.1.right_ref
  582.2 1.0 copy-done.7
  583.2 2.6 fusion.20
  585.8 3.9 reduce-scatter.5.cloned.1.call-done
  589.7 95.6 %shard_map.156 = (f32[64,3072]{1,0:T(8,128)}, f32[64,16384]{1,0:T(8,128)}, f32[8,128]{1,0:T(8,128)}) custom-call(bf16[256,2048]{1,0:T(8,128)(2,1)} %copy-done.14, bf16[3072,256]{1,0:T(8,128)(2,1)} %pad_maximum_fusion.1.right_ref, bf16[4,64,4096]{2,1,0:T(8,128)(2,1)} %bitcast.65, f32[8,4,8,128]{3,2,1,0:T(8,128)} %pad.9.gains_ref), custom_call_target="tpu_custom_call" | custom-call | bytes 314572800 | tf_op jit(solution)/shard_map/pallas_call | solution.py:1297
  685.2 2.3 reduce-scatter.3.cloned.1.call-done
  687.6 2.9 convert_element_type.98
  690.5 1.3 slice_bitcast_fusion
  691.8 0.9 copy.36
  692.7 0.8 copy.37
  693.5 2.0 copy.38
  (66 shorter events, 0.7 us)
Async XLA Ops:
  7.2 262.7 %all-gather.5.cloned.1.call-start = ((), (), s32[]{:S(2)}) async-start(), calls=%async_computation.3 | async-start | bytes 9437184 | tf_op jit(solution)/shard_map/all_gather | solution.py:846
  7.9 261.9 %all-gather.3.cloned.1.call-start = ((), (), s32[]{:S(2)}) async-start(), calls=%async_computation.2 | async-start | bytes 18874368 | tf_op jit(solution)/shard_map/all_gather | solution.py:846
  107.2 2.0 copy-start.10
  107.3 482.4 %reduce-scatter.5.cloned.1.call-start = ((), (), s32[]{:S(2)}) async-start(), calls=%async_computation.5 | async-start | bytes 18874368 | tf_op jit(solution)/shard_map/reduce_scatter | solution.py:850
  109.2 8.8 %copy-start.19 = (f32[2048]{0:T(1024)}, f32[2048]{0:T(1024)S(1)}, u32[]{:S(2)}) copy-start(f32[2048]{0:T(1024)S(1)} %get-tuple-element.49) | copy-start | bytes 24580
  109.5 8.5 %copy-start.21 = (f32[256]{0:T(256)}, f32[256]{0:T(256)S(1)}, u32[]{:S(2)}) copy-start(f32[256]{0:T(256)S(1)} %add_rsqrt_fusion.1) | copy-start | bytes 3076
  109.8 8.2 %copy-start.14 = (bf16[256,2048]{1,0:T(8,128)(2,1)}, bf16[256,2048]{1,0:T(8,128)(2,1)S(1)}, u32[]{:S(2)}) copy-start(bf16[256,2048]{1,0:T(8,128)(2,1)S(1)} %fusion.11.left_ref) | copy-start | bytes 3145732
  118.1 1.7 copy-start.23
  122.9 1.2 copy-start
  122.9 1.3 copy-start.1
  258.7 8.6 %copy-start.2 = (bf16[4,256,2048]{2,1,0:T(8,128)(2,1)}, bf16[4,256,2048]{2,1,0:T(8,128)(2,1)S(1)}, u32[]{:S(2)}) copy-start(bf16[4,256,2048]{2,1,0:T(8,128)(2,1)S(1)} %get-tuple-element.32.cot_ref) | copy-start | bytes 12582916
  258.7 8.6 %copy-start.3 = (f32[8,256,256]{2,1,0:T(8,128)}, f32[8,256,256]{2,1,0:T(8,128)S(1)}, u32[]{:S(2)}) copy-start(f32[8,256,256]{2,1,0:T(8,128)S(1)} %get-tuple-element.35.full_ref) | copy-start | bytes 6291460
  258.7 8.6 %copy-start.4 = (bf16[8,384,256]{2,1,0:T(8,128)(2,1)}, bf16[8,384,256]{2,1,0:T(8,128)(2,1)S(1)}, u32[]{:S(2)}) copy-start(bf16[8,384,256]{2,1,0:T(8,128)(2,1)S(1)} %get-tuple-element.31.x_ref) | copy-start | bytes 4718596
  267.3 1.3 copy-start.5
  422.9 264.7 %reduce-scatter.3.cloned.1.call-start = ((), (), s32[]{:S(2)}) async-start(), calls=%async_computation.4 | async-start | bytes 9437184 | tf_op jit(solution)/shard_map/reduce_scatter | solution.py:850
  424.5 3.0 copy-start.6
  424.5 3.5 copy-start.8
  428.6 6.8 copy-start.17
  563.2 2.7 copy-start.11
  563.2 2.7 copy-start.20
  563.2 2.7 copy-start.22
  565.9 10.4 %copy-start.12 = (bf16[8,256,256]{2,1,0:T(8,128)(2,1)}, bf16[8,256,256]{2,1,0:T(8,128)(2,1)S(1)}, u32[]{:S(2)}) copy-start(bf16[8,256,256]{2,1,0:T(8,128)(2,1)S(1)} %slice.56) | copy-start | bytes 3145732
  577.2 3.7 copy-start.13
  577.2 5.0 copy-start.9
  577.2 5.0 copy-start.16
  580.9 2.3 copy-start.7
  685.2 6.6 copy-start.18
  687.6 5.9 copy-start.15
Sparse Core Ops, SparseCore 0:
  9.9 82.8 all-gather.4
  107.4 142.7 all-gather.2
  423.0 166.6 reduce-scatter.4
  593.0 94.5 reduce-scatter.2

commit v8 on v7

--- a/solution.py
+++ b/solution.py
@@ -888,7 +888,7 @@
 
     for t in range(flow.last):
         flow.step(t)
-        if t == min(1, narrow - 1):
+        if t == min(2, narrow - 1):
             for source, columns in pieces(n):
                 pltpu.make_async_copy(source, target(columns), x_own).start()
             for step in range(1, narrow):

time: 703 us -> 704 us (level)
  transfers between devices with their start and end apart: 4 -> 4, of which waited for: 2 -> 2; matrix products, arithmetic and copies ran while one was open for 9% -> 8% of each run, Pallas kernels for 65% -> 65%
where the time goes in v8:
time: 704 us
  Pallas kernels  610 us (87%)
  matrix products  31.7 us (5%)
  other arithmetic  24.7 us (4%)
  local copies, waits for them, and re-layouts  14.5 us (2%)
  between operations  14.2 us (2%)
  waiting for transfers between devices  8.09 us (1%)
    pallas_call x1, Pallas kernels, feed(): pl.pallas_call(functools.partial(feed_kernel, narrow), out_shape=(jax.Sha...  151 us
    pallas_call x1, Pallas kernels, attend(): pl.pallas_call(functools.partial(attend_kernel, wide, narrow, groups), ou...  137 us
    pallas_call x1, Pallas kernels, attend_back(): pl.pallas_call(functools.partial(attend_back_kernel, wide, narrow, groups...  130 us
    pallas_call x1, Pallas kernels, gather_weights(): pl.pallas_call(functools.partial(gather_kernel, wide, narrow, aligned), o...  96.7 us
    pallas_call x1, Pallas kernels, sum_all(): pl.pallas_call(functools.partial(sum_kernel, wide, narrow), out_shape=(ja...  95.5 us
    dot_general x4, matrix products, dot(): lax.dot_general(left, right, dims, preferred_element_type=F32).astype(kind)  31.7 us
  transfers between devices with their start and end apart: 4, of which 2 were waited for; matrix products, arithmetic and copies ran while one was open for 8% of the time, Pallas kernels for 65%

profile of v8, /device:TPU:0, one launch (start us, length us, event | category | flops | bytes accessed | tf_op | source)
XLA Modules:
  0.0 703.9 jit_solution(5923024171338498599)
XLA Ops:
  7.2 0.7 all-gather.5.cloned.1.call-update
  7.9 0.7 pad_maximum_fusion.3
  8.6 0.1 copy.28
  8.7 1.8 fusion.23.qkv_ref
  10.5 96.7 %shard_map.152 = (bf16[2048,3200]{1,0:T(8,128)(2,1)}, bf16[256,4096]{1,0:T(8,128)(2,1)}) custom-call(bf16[64,3200]{1,0:T(8,128)(2,1)} %fusion.23.qkv_ref, bf16[64,16384]{1,0:T(8,128)(2,1)} %cut_ref.1), custom_call_target="tpu_custom_call" | custom-call | bytes 209715200 | tf_op jit(solution)/shard_map/pallas_call | solution.py:915
  107.3 1.9 convert_reduce_fusion.1
  109.2 0.3 fusion.18
  109.5 0.3 fusion.11.left_ref
  109.9 6.9 fusion.2
  116.8 1.7 slice.62
  118.5 0.2 reduce-window.4
  118.7 0.1 convert_reduce_fusion.3
  118.8 0.1 select_reduce_fusion
  118.9 0.1 broadcast_multiply_fusion
  119.0 0.1 dynamic-slice_cosine_fusion
  119.2 2.6 multiply_subtract_fusion
  121.8 0.3 fusion.10
  122.1 0.1 pad_maximum_fusion.mine_ref
  122.3 1.1 copy-done
  123.4 136.8 %shard_map.153 = (bf16[8,384,256]{2,1,0:T(8,128)(2,1)S(1)}, bf16[8,256,256]{2,1,0:T(8,128)(2,1)S(1)}, f32[8,256,256]{2,1,0:T(8,128)S(1)}, f32[8,4,256]{2,1,0:T(4...) custom-call(s32[8,1,256]{2,1,0:T(1,128)S(1)} %bitcast.58, ...), custom_call_target="tpu_custom_call" | custom-call | flops 34359738368 | bytes 67108864 | tf_op jit(solution)/shard_map/pallas_call | solution.py:607
  260.2 8.6 %multiply_reduce_fusion.2 = (f32[256]{0:T(256)S(1)}, f32[256,2048]{1,0:T(8,128)S(1)}) fusion(bf16[2048,256]{1,0:T(8,128)(2,1)S(1)} %bitcast.56, bf16[2048,2048]{1,0:T(8,128)(2,1)} %get-tuple-element.30, bf16[1,256,2048]{2,1,0:T(8,128)(2,1)S(1)} %copy-done.10), kind=kOutput, calls=%fused_computation.31 | convolution fusion | flops 2149580544 | bytes 12583936 | tf_op jit(solution)/shard_map/dot_general | solution.py:28
  268.9 1.3 copy-done.5
  270.2 1.2 multiply_convert_fusion.x_ref
  271.4 151.4 %shard_map.154 = (bf16[4,256,2048]{2,1,0:T(8,128)(2,1)}, f32[256,2048]{1,0:T(8,128)}, bf16[2048,4096]{1,0:T(8,128)(2,1)}, bf16[2048,2048]{1,0:T(8,128)(2,1)}) custom-call(bf16[256,2048]{1,0:T(8,128)(2,1)} %multiply_convert_fusion.x_ref, bf16[4,256,2048]{2,1,0:T(8,128)(2,1)} %copy-done.2, bf16[2048,4096]{1,0:T(8,128)(2,1)} %all-gather.3.cloned.1.call-done.gate_up_ref, ...), custom_call_target="tpu_custom_call" | custom-call | flops 51539607552 | bytes 314572800 | tf_op jit(solution)/shard_map/pallas_call | solution.py:1148
  422.8 0.3 reduce-scatter.3.cloned.1.call-start
  423.0 0.3 reduce-scatter.3.cloned.1.call-update
  423.4 1.0 multiply_sine_fusion
  424.4 3.0 multiply_reduce_fusion
  427.4 0.5 copy-done.8
  427.9 0.7 fusion.25.right_ref
  428.6 6.1 convolution_convert_fusion
  434.7 129.8 %shard_map.155 = (bf16[8,384,256]{2,1,0:T(8,128)(2,1)}, bf16[4,256,2048]{2,1,0:T(8,128)(2,1)}, f32[64,2048]{1,0:T(8,128)S(1)}) custom-call(s32[8,1,256]{2,1,0:T(1,128)S(1)} %bitcast.59, bf16[8,384,256]{2,1,0:T(8,128)(2,1)} %copy-done.4, bf16[8,256,256]{2,1,0:T(8,128)(2,1)S(1)} %bitcast.60, f32[8,256,256]{2,1,0:T(8,128)} %copy-done.3, ...), custom_call_target="tpu_custom_call" | custom-call | flops 42949672960 | bytes 6291456 | tf_op jit(solution)/shard_map/pallas_call | solution.py:812
  564.6 1.3 slice.57
  565.9 1.3 slice.56
  567.3 10.1 %fusion.17 = (f32[2048]{0:T(1024)S(1)}, f32[256]{0:T(256)S(1)}, f32[256,2048]{1,0:T(8,128)}) fusion(bf16[1,256,2048]{2,1,0:T(8,128)(2,1)S(1)} %copy-done.11, f32[256]{0:T(256)S(1)} %copy-done.22, f32[2048]{0:T(1024)S(1)} %copy-done.20, bf16[2048,3200]{1,0:T(8,128)(2,1)} %get-tuple-element.28, bf16[512,256]{1,0:T(8,128)(2,1)S(1)} %bitcast.70, ...), kind=kOutput, calls=%fused_computation.24 | convolution fusion | flops 3229611776 | bytes 17319936 | tf_op jit(solution)/shard_map/dot_general | solution.py:28
  577.7 0.7 pad.9.gains_ref
  578.4 3.5 convert_reduce_fusion
  581.9 1.3 pad_maximum_fusion.1.right_ref
  583.2 1.0 copy-done.7
  584.2 2.6 fusion.20
  586.9 4.7 reduce-scatter.5.cloned.1.call-done
  591.6 95.5 %shard_map.156 = (f32[64,3072]{1,0:T(8,128)}, f32[64,16384]{1,0:T(8,128)}, f32[8,128]{1,0:T(8,128)}) custom-call(bf16[256,2048]{1,0:T(8,128)(2,1)} %copy-done.14, bf16[3072,256]{1,0:T(8,128)(2,1)} %pad_maximum_fusion.1.right_ref, bf16[4,64,4096]{2,1,0:T(8,128)(2,1)} %bitcast.65, f32[8,4,8,128]{3,2,1,0:T(8,128)} %pad.9.gains_ref), custom_call_target="tpu_custom_call" | custom-call | bytes 314572800 | tf_op jit(solution)/shard_map/pallas_call | solution.py:1297
  687.1 2.4 reduce-scatter.3.cloned.1.call-done
  689.5 2.9 convert_element_type.98
  692.4 1.3 slice_bitcast_fusion
  693.7 0.9 copy.36
  694.5 0.8 copy.37
  695.3 2.0 copy.38
  (66 shorter events, 0.7 us)
Async XLA Ops:
  7.2 264.2 %all-gather.5.cloned.1.call-start = ((), (), s32[]{:S(2)}) async-start(), calls=%async_computation.3 | async-start | bytes 9437184 | tf_op jit(solution)/shard_map/all_gather | solution.py:846
  7.9 263.5 %all-gather.3.cloned.1.call-start = ((), (), s32[]{:S(2)}) async-start(), calls=%async_computation.2 | async-start | bytes 18874368 | tf_op jit(solution)/shard_map/all_gather | solution.py:846
  107.2 2.0 copy-start.10
  107.3 484.3 %reduce-scatter.5.cloned.1.call-start = ((), (), s32[]{:S(2)}) async-start(), calls=%async_computation.5 | async-start | bytes 18874368 | tf_op jit(solution)/shard_map/reduce_scatter | solution.py:850
  109.2 7.6 %copy-start.19 = (f32[2048]{0:T(1024)}, f32[2048]{0:T(1024)S(1)}, u32[]{:S(2)}) copy-start(f32[2048]{0:T(1024)S(1)} %get-tuple-element.49) | copy-start | bytes 24580
  109.5 7.3 %copy-start.21 = (f32[256]{0:T(256)}, f32[256]{0:T(256)S(1)}, u32[]{:S(2)}) copy-start(f32[256]{0:T(256)S(1)} %add_rsqrt_fusion.1) | copy-start | bytes 3076
  109.8 6.9 copy-start.14
  116.8 1.7 copy-start.23
  122.1 1.2 copy-start
  122.1 1.3 copy-start.1
  260.2 8.6 %copy-start.2 = (bf16[4,256,2048]{2,1,0:T(8,128)(2,1)}, bf16[4,256,2048]{2,1,0:T(8,128)(2,1)S(1)}, u32[]{:S(2)}) copy-start(bf16[4,256,2048]{2,1,0:T(8,128)(2,1)S(1)} %get-tuple-element.32.cot_ref) | copy-start | bytes 12582916
  260.2 8.6 %copy-start.3 = (f32[8,256,256]{2,1,0:T(8,128)}, f32[8,256,256]{2,1,0:T(8,128)S(1)}, u32[]{:S(2)}) copy-start(f32[8,256,256]{2,1,0:T(8,128)S(1)} %get-tuple-element.35.full_ref) | copy-start | bytes 6291460
  260.2 8.6 %copy-start.4 = (bf16[8,384,256]{2,1,0:T(8,128)(2,1)}, bf16[8,384,256]{2,1,0:T(8,128)(2,1)S(1)}, u32[]{:S(2)}) copy-start(bf16[8,384,256]{2,1,0:T(8,128)(2,1)S(1)} %get-tuple-element.31.x_ref) | copy-start | bytes 4718596
  268.8 1.3 copy-start.5
  422.8 266.7 %reduce-scatter.3.cloned.1.call-start = ((), (), s32[]{:S(2)}) async-start(), calls=%async_computation.4 | async-start | bytes 9437184 | tf_op jit(solution)/shard_map/reduce_scatter | solution.py:850
  424.4 3.0 copy-start.6
  424.4 3.5 copy-start.8
  428.6 6.2 copy-start.17
  564.6 2.7 copy-start.11
  564.6 2.7 copy-start.20
  564.6 2.7 copy-start.22
  567.3 10.2 %copy-start.12 = (bf16[8,256,256]{2,1,0:T(8,128)(2,1)}, bf16[8,256,256]{2,1,0:T(8,128)(2,1)S(1)}, u32[]{:S(2)}) copy-start(bf16[8,256,256]{2,1,0:T(8,128)(2,1)S(1)} %slice.56) | copy-start | bytes 3145732
  578.4 3.5 copy-start.13
  578.4 4.8 copy-start.9
  578.4 4.8 copy-start.16
  581.9 2.3 copy-start.7
  687.1 6.6 copy-start.18
  689.5 5.9 copy-start.15
Sparse Core Ops, SparseCore 0:
  9.9 90.8 all-gather.4
  107.4 145.4 all-gather.2
  422.9 168.6 reduce-scatter.4
  594.9 94.5 reduce-scatter.2

commit v9 on v7

--- a/solution.py
+++ b/solution.py
@@ -988,7 +988,7 @@
         return pltpu.make_async_copy(low.at[at], low_out.at[block], out_sem.at[at])
 
     def g_copy(block, half):
-        columns = pl.ds(half * (width // 2), width // 2)
+        columns = pl.ds(half * (width // 4), width // 4)
         return pltpu.make_async_remote_copy(
             src_ref=cot.at[block, :, columns],
             dst_ref=came.at[n, :, columns],
@@ -1028,8 +1028,8 @@
             low[at, :, columns] = dot(hidden[block], down[:, columns], NN, BF16)
             return carry
 
-        for half in (0, 1):
-            lax.fori_loop(half * (wtiles // 2), (half + 1) * (wtiles // 2), second, 0)
+        for half in range(4):
+            lax.fori_loop(half * (wtiles // 4), (half + 1) * (wtiles // 4), second, 0)
             pl.when(block != n)(lambda half=half: g_copy(block, half).start())
         out_copy(at, block).start()
 
@@ -1123,9 +1123,9 @@
             pl.when(passes(side, d))(lambda side=side, d=d: x_copy(side, d).wait_send())
     for step in range(1, narrow):
         other = lax.rem(n + step, narrow)
-        for half in (0, 1):
+        for half in range(4):
             g_copy(other, half).wait_send()
-            arrive(came.at[other, :, pl.ds(half * (width // 2), width // 2)], g_recv.at[other, half])
+            arrive(came.at[other, :, pl.ds(half * (width // 4), width // 4)], g_recv.at[other, half])
 
     def add(r, carry):
         part = pl.ds(pl.multiple_of(r * 16, 16), 16)
@@ -1168,8 +1168,8 @@
             dma((2, narrow + 1)),
             dma((2, narrow + 1)),
             dma((2,)),
-            dma((narrow, 2)),
-            dma((narrow, 2)),
+            dma((narrow, 4)),
+            dma((narrow, 4)),
         ],
         compiler_params=pltpu.CompilerParams(
             collective_id=1, has_side_effects=True, vmem_limit_bytes=58 << 20

time: 703 us -> 701 us (level)
  no operation moved by 1% of the time
where the time goes in v9:
time: 701 us; the launch traced here: 700 us
  Pallas kernels  606 us (86%)
  matrix products  33.9 us (5%)
  other arithmetic  24.4 us (3%)
  local copies, waits for them, and re-layouts  14.4 us (2%)
  between operations  14.2 us (2%)
  waiting for transfers between devices  7.49 us (1%)
    pallas_call x1, Pallas kernels, feed(): pl.pallas_call(functools.partial(feed_kernel, narrow), out_shape=(jax.Sha...  151 us
    pallas_call x1, Pallas kernels, attend(): pl.pallas_call(functools.partial(attend_kernel, wide, narrow, groups), ou...  134 us
    pallas_call x1, Pallas kernels, attend_back(): pl.pallas_call(functools.partial(attend_back_kernel, wide, narrow, groups...  128 us
    pallas_call x1, Pallas kernels, gather_weights(): pl.pallas_call(functools.partial(gather_kernel, wide, narrow, aligned), o...  96.7 us
    pallas_call x1, Pallas kernels, sum_all(): pl.pallas_call(functools.partial(sum_kernel, wide, narrow), out_shape=(ja...  95.6 us
    dot_general x4, matrix products, dot(): lax.dot_general(left, right, dims, preferred_element_type=F32).astype(kind)  33.9 us
  transfers between devices with their start and end apart: 4, of which 2 were waited for; matrix products, arithmetic and copies ran while one was open for 9% of the time, Pallas kernels for 65%

profile of v9, /device:TPU:0, one launch (start us, length us, event | category | flops | bytes accessed | tf_op | source)
XLA Modules:
  0.0 700.1 jit_solution(8217948418091285329)
XLA Ops:
  7.2 0.7 all-gather.5.cloned.1.call-update
  7.9 0.7 pad_maximum_fusion.3
  8.6 0.1 copy.28
  8.7 1.8 fusion.23.qkv_ref
  10.5 96.7 %shard_map.152 = (bf16[2048,3200]{1,0:T(8,128)(2,1)}, bf16[256,4096]{1,0:T(8,128)(2,1)}) custom-call(bf16[64,3200]{1,0:T(8,128)(2,1)} %fusion.23.qkv_ref, bf16[64,16384]{1,0:T(8,128)(2,1)} %cut_ref.1), custom_call_target="tpu_custom_call" | custom-call | bytes 209715200 | tf_op jit(solution)/shard_map/pallas_call | solution.py:915
  107.3 1.9 convert_reduce_fusion.1
  109.2 0.3 fusion.18
  109.5 0.3 fusion.11.left_ref
  109.9 8.2 %fusion.2 = f32[3072,256]{1,0:T(8,128)S(1)} fusion(bf16[256,2048]{1,0:T(8,128)(2,1)S(1)} %fusion.11.left_ref, bf16[2048,3200]{1,0:T(8,128)(2,1)} %get-tuple-element.28), kind=kOutput, calls=%fused_computation.2 | convolution fusion | flops 3221225472 | bytes 16777216 | tf_op jit(solution)/shard_map/dot_general | solution.py:28
  118.1 1.7 slice.62
  119.8 0.2 reduce-window.4
  120.0 0.1 convert_reduce_fusion.3
  120.1 0.1 select_reduce_fusion
  120.2 0.1 broadcast_multiply_fusion
  120.3 0.1 dynamic-slice_cosine_fusion
  120.4 2.1 multiply_subtract_fusion
  122.6 0.3 fusion.10
  122.9 0.1 pad_maximum_fusion.mine_ref
  123.0 1.1 copy-done
  124.2 134.5 %shard_map.153 = (bf16[8,384,256]{2,1,0:T(8,128)(2,1)S(1)}, bf16[8,256,256]{2,1,0:T(8,128)(2,1)S(1)}, f32[8,256,256]{2,1,0:T(8,128)S(1)}, f32[8,4,256]{2,1,0:T(4...) custom-call(s32[8,1,256]{2,1,0:T(1,128)S(1)} %bitcast.58, ...), custom_call_target="tpu_custom_call" | custom-call | flops 34359738368 | bytes 67108864 | tf_op jit(solution)/shard_map/pallas_call | solution.py:607
  258.7 8.6 %multiply_reduce_fusion.2 = (f32[256]{0:T(256)S(1)}, f32[256,2048]{1,0:T(8,128)S(1)}) fusion(bf16[2048,256]{1,0:T(8,128)(2,1)S(1)} %bitcast.56, bf16[2048,2048]{1,0:T(8,128)(2,1)} %get-tuple-element.30, bf16[1,256,2048]{2,1,0:T(8,128)(2,1)S(1)} %copy-done.10), kind=kOutput, calls=%fused_computation.31 | convolution fusion | flops 2149580544 | bytes 12583936 | tf_op jit(solution)/shard_map/dot_general | solution.py:28
  267.3 1.3 copy-done.5
  268.6 1.2 multiply_convert_fusion.x_ref
  269.8 151.1 %shard_map.154 = (bf16[4,256,2048]{2,1,0:T(8,128)(2,1)}, f32[256,2048]{1,0:T(8,128)}, bf16[2048,4096]{1,0:T(8,128)(2,1)}, bf16[2048,2048]{1,0:T(8,128)(2,1)}) custom-call(bf16[256,2048]{1,0:T(8,128)(2,1)} %multiply_convert_fusion.x_ref, bf16[4,256,2048]{2,1,0:T(8,128)(2,1)} %copy-done.2, bf16[2048,4096]{1,0:T(8,128)(2,1)} %all-gather.3.cloned.1.call-done.gate_up_ref, ...), custom_call_target="tpu_custom_call" | custom-call | flops 51539607552 | bytes 314572800 | tf_op jit(solution)/shard_map/pallas_call | solution.py:1148
  421.0 0.5 reduce-scatter.3.cloned.1.call-update
  421.5 1.0 multiply_sine_fusion
  422.6 3.0 multiply_reduce_fusion
  425.5 0.5 copy-done.8
  426.0 0.7 fusion.25.right_ref
  426.7 6.8 convolution_convert_fusion
  433.5 127.7 %shard_map.155 = (bf16[8,384,256]{2,1,0:T(8,128)(2,1)}, bf16[4,256,2048]{2,1,0:T(8,128)(2,1)}, f32[64,2048]{1,0:T(8,128)S(1)}) custom-call(s32[8,1,256]{2,1,0:T(1,128)S(1)} %bitcast.59, bf16[8,384,256]{2,1,0:T(8,128)(2,1)} %copy-done.4, bf16[8,256,256]{2,1,0:T(8,128)(2,1)S(1)} %bitcast.60, f32[8,256,256]{2,1,0:T(8,128)} %copy-done.3, ...), custom_call_target="tpu_custom_call" | custom-call | flops 42949672960 | bytes 6291456 | tf_op jit(solution)/shard_map/pallas_call | solution.py:812
  561.3 1.3 slice.57
  562.6 1.3 slice.56
  564.0 10.3 %fusion.17 = (f32[2048]{0:T(1024)S(1)}, f32[256]{0:T(256)S(1)}, f32[256,2048]{1,0:T(8,128)}) fusion(bf16[1,256,2048]{2,1,0:T(8,128)(2,1)S(1)} %copy-done.11, f32[256]{0:T(256)S(1)} %copy-done.22, f32[2048]{0:T(1024)S(1)} %copy-done.20, bf16[2048,3200]{1,0:T(8,128)(2,1)} %get-tuple-element.28, bf16[512,256]{1,0:T(8,128)(2,1)S(1)} %bitcast.70, ...), kind=kOutput, calls=%fused_computation.24 | convolution fusion | flops 3229611776 | bytes 17319936 | tf_op jit(solution)/shard_map/dot_general | solution.py:28
  574.4 0.1 stack.28
  574.6 0.7 pad.9.gains_ref
  575.2 3.7 convert_reduce_fusion
  579.0 1.3 pad_maximum_fusion.1.right_ref
  580.2 1.0 copy-done.7
  581.2 2.6 fusion.20
  583.8 3.9 reduce-scatter.5.cloned.1.call-done
  587.7 95.6 %shard_map.156 = (f32[64,3072]{1,0:T(8,128)}, f32[64,16384]{1,0:T(8,128)}, f32[8,128]{1,0:T(8,128)}) custom-call(bf16[256,2048]{1,0:T(8,128)(2,1)} %copy-done.14, bf16[3072,256]{1,0:T(8,128)(2,1)} %pad_maximum_fusion.1.right_ref, bf16[4,64,4096]{2,1,0:T(8,128)(2,1)} %bitcast.65, f32[8,4,8,128]{3,2,1,0:T(8,128)} %pad.9.gains_ref), custom_call_target="tpu_custom_call" | custom-call | bytes 314572800 | tf_op jit(solution)/shard_map/pallas_call | solution.py:1297
  683.3 2.3 reduce-scatter.3.cloned.1.call-done
  685.7 2.9 convert_element_type.98
  688.6 1.3 slice_bitcast_fusion
  689.9 0.9 copy.36
  690.8 0.8 copy.37
  691.5 2.0 copy.38
  (66 shorter events, 0.6 us)
Async XLA Ops:
  7.2 262.7 %all-gather.5.cloned.1.call-start = ((), (), s32[]{:S(2)}) async-start(), calls=%async_computation.3 | async-start | bytes 9437184 | tf_op jit(solution)/shard_map/all_gather | solution.py:846
  7.9 261.9 %all-gather.3.cloned.1.call-start = ((), (), s32[]{:S(2)}) async-start(), calls=%async_computation.2 | async-start | bytes 18874368 | tf_op jit(solution)/shard_map/all_gather | solution.py:846
  107.2 2.0 copy-start.10
  107.3 480.5 %reduce-scatter.5.cloned.1.call-start = ((), (), s32[]{:S(2)}) async-start(), calls=%async_computation.5 | async-start | bytes 18874368 | tf_op jit(solution)/shard_map/reduce_scatter | solution.py:850
  109.2 8.8 %copy-start.19 = (f32[2048]{0:T(1024)}, f32[2048]{0:T(1024)S(1)}, u32[]{:S(2)}) copy-start(f32[2048]{0:T(1024)S(1)} %get-tuple-element.49) | copy-start | bytes 24580
  109.5 8.5 %copy-start.21 = (f32[256]{0:T(256)}, f32[256]{0:T(256)S(1)}, u32[]{:S(2)}) copy-start(f32[256]{0:T(256)S(1)} %add_rsqrt_fusion.1) | copy-start | bytes 3076
  109.8 8.2 %copy-start.14 = (bf16[256,2048]{1,0:T(8,128)(2,1)}, bf16[256,2048]{1,0:T(8,128)(2,1)S(1)}, u32[]{:S(2)}) copy-start(bf16[256,2048]{1,0:T(8,128)(2,1)S(1)} %fusion.11.left_ref) | copy-start | bytes 3145732
  118.1 1.7 copy-start.23
  122.9 1.2 copy-start
  122.9 1.3 copy-start.1
  258.7 8.6 %copy-start.2 = (bf16[4,256,2048]{2,1,0:T(8,128)(2,1)}, bf16[4,256,2048]{2,1,0:T(8,128)(2,1)S(1)}, u32[]{:S(2)}) copy-start(bf16[4,256,2048]{2,1,0:T(8,128)(2,1)S(1)} %get-tuple-element.32.cot_ref) | copy-start | bytes 12582916
  258.7 8.6 %copy-start.3 = (f32[8,256,256]{2,1,0:T(8,128)}, f32[8,256,256]{2,1,0:T(8,128)S(1)}, u32[]{:S(2)}) copy-start(f32[8,256,256]{2,1,0:T(8,128)S(1)} %get-tuple-element.35.full_ref) | copy-start | bytes 6291460
  258.7 8.6 %copy-start.4 = (bf16[8,384,256]{2,1,0:T(8,128)(2,1)}, bf16[8,384,256]{2,1,0:T(8,128)(2,1)S(1)}, u32[]{:S(2)}) copy-start(bf16[8,384,256]{2,1,0:T(8,128)(2,1)S(1)} %get-tuple-element.31.x_ref) | copy-start | bytes 4718596
  267.3 1.3 copy-start.5
  420.9 264.7 %reduce-scatter.3.cloned.1.call-start = ((), (), s32[]{:S(2)}) async-start(), calls=%async_computation.4 | async-start | bytes 9437184 | tf_op jit(solution)/shard_map/reduce_scatter | solution.py:850
  422.5 3.0 copy-start.6
  422.5 3.5 copy-start.8
  426.7 6.8 copy-start.17
  561.3 2.7 copy-start.11
  561.3 2.7 copy-start.20
  561.3 2.7 copy-start.22
  563.9 10.4 %copy-start.12 = (bf16[8,256,256]{2,1,0:T(8,128)(2,1)}, bf16[8,256,256]{2,1,0:T(8,128)(2,1)S(1)}, u32[]{:S(2)}) copy-start(bf16[8,256,256]{2,1,0:T(8,128)(2,1)S(1)} %slice.56) | copy-start | bytes 3145732
  575.2 3.7 copy-start.13
  575.2 5.0 copy-start.9
  575.2 5.0 copy-start.16
  579.0 2.3 copy-start.7
  683.3 6.6 copy-start.18
  685.7 5.9 copy-start.15
Sparse Core Ops, SparseCore 0:
  9.9 82.8 all-gather.4
  107.4 142.7 all-gather.2
  421.1 166.6 reduce-scatter.4
  591.1 94.5 reduce-scatter.2
